TPU v7x, 32 devices: a whole 2x2x4 slice. The times are simulated.
32 devices in a mesh: sub: 4 (over z), blk: 8 (over y, x, core).
Axes of the slice: x: 2, y: 2, z: 4, core: 2. Of those that a mesh axis runs over, the one named last changes fastest.
Arguments:
- coords: float32 [3, 1024, 256], P(None, ('sub', 'blk')), may hold values from -3.8 to 3.8
- strain: float32 [1024, 256], P(('sub', 'blk')), may hold values from 0.3 to 8
- history: float32 [1024, 256], P(('sub', 'blk')), may hold values from 1 to 3
- corner_load: float32 [24, 1024, 256], P(None, ('sub', 'blk')), may hold values from -0.4 to 0.4
- tile_count: int32 [1024], P(('sub', 'blk')), may hold values from 128 to 256, as said below
- tile_sub: int32 [1024], P(('sub', 'blk')), may hold values from 0 to 3
- local_pairs: int32 [2, 1024], P(None, ('sub', 'blk')), may hold values from 0 to 31, as said below
- send_tile: int32 [256], P(('sub', 'blk')), may hold values from 0 to 3
- remote_pairs: int32 [2, 256], P(None, ('sub', 'blk')), may hold values from 0 to 7, as said below
- remote_count: int32 [32], P(('sub', 'blk')), may hold values from 2 to 8, as said below
- corner_map: int32 [128, 24], P(('sub', 'blk')), may hold values from 0 to 1023
- external: float32 [4096], P(('sub', 'blk')), may hold values from -6 to 6
Outputs:
- damage: float32 [1024, 256], P(('sub', 'blk'))
- coarse_residual: float32 [4096], P(('sub', 'blk'))
Inputs may be any that keep to these rules, and one draw needn't show every extreme that they name: `tile_count`: used slots of a tile come first; some tiles are full. `local_pairs`: each column names two different tiles of its device. `remote_pairs`: first row: one of the first four tiles of the device, by local index. Second row: in each device's block of 8 entries, every blk index exactly once. `remote_count`: some device has all 8 entries live. `send_tile`: one of the first four tiles of the sending device.
All inputs are finite; a program needn't handle non-finite values.
Results may differ from a plain program's by a relative error of at most 0.0001.
Values sent between devices are 32-bit elements; how exact they have to be, the bound alone decides.
No kernel may reach another device: no remote copies, remote signals or barrier semaphores. Data moves between devices by JAX's collectives and lax.ppermute only.
A program may use at most 64 MiB of HBM per device.

v0:
```python
import jax
import jax.numpy as jnp
from jax import lax
from jax.sharding import PartitionSpec as P

gauss_rate = 4.0
keep_share = 0.05
softening = 0.5
block_most = 16


def padded(cells, sides, width):
    for axis, dim in sides:
        count = lax.axis_size(axis)
        ends = count - 1
        head = lax.slice_in_dim(cells, 0, width, axis=dim)
        tail = lax.slice_in_dim(cells, cells.shape[dim] - width, cells.shape[dim], axis=dim)
        cells = jnp.concatenate(
            [
                lax.ppermute(tail, axis, [(i, (i + 1) % count) for i in range(ends)]),
                cells,
                lax.ppermute(head, axis, [((i + 1) % count, i) for i in range(ends)]),
            ],
            axis=dim,
        )
    return cells


def pair_block(first, second, weights_on):
    sq_dist = (first[0][:, :, None] - second[0][:, None, :]) ** 2
    sq_dist = sq_dist + (first[1][:, :, None] - second[1][:, None, :]) ** 2
    sq_dist = sq_dist + (first[2][:, :, None] - second[2][:, None, :]) ** 2
    kernel = jnp.exp(-gauss_rate * sq_dist) * first[4][:, :, None] * second[4][:, None, :]
    kernel = kernel * weights_on[:, None, None]
    num_first = jnp.einsum("gpq,gq->gp", kernel, second[3], precision=lax.Precision.HIGHEST)
    den_first = jnp.sum(kernel, axis=2)
    num_second = jnp.einsum("gpq,gp->gq", kernel, first[3], precision=lax.Precision.HIGHEST)
    den_second = jnp.sum(kernel, axis=1)
    return (jnp.stack([num_first, den_first]), jnp.stack([num_second, den_second]))


def add_block(total, piece, offset):
    width = piece.shape[1]
    current = lax.dynamic_slice_in_dim(total, offset, width, 1)
    return lax.dynamic_update_slice_in_dim(total, current + piece, offset, 1)


def dense_pass(first_source, second_source, sums_near):
    tiles_here = first_source.shape[1]
    width = min(block_most, tiles_here)
    steps_count = tiles_here // width
    ones_here = jnp.ones((width,), jnp.float32)

    def dense_advance(step_idx, carry):
        offset = step_idx * width
        first = lax.dynamic_slice_in_dim(first_source, offset, width, 1)
        second = lax.dynamic_slice_in_dim(second_source, offset, width, 1)
        near, far = pair_block(first, second, ones_here)
        return (add_block(carry[0], near, offset),)

    return lax.fori_loop(0, steps_count, dense_advance, (sums_near,))[0]


def listed_pass(
    steps_count,
    width,
    first_source,
    second_source,
    first_ids,
    second_ids,
    weights_on,
    sums_near,
    sums_far,
):

    def listed_advance(step_idx, carry):
        offset = step_idx * width
        pick_first = lax.dynamic_slice_in_dim(first_ids, offset, width)
        pick_second = lax.dynamic_slice_in_dim(second_ids, offset, width)
        weight_now = lax.dynamic_slice_in_dim(weights_on, offset, width)
        near, far = pair_block(
            jnp.take(first_source, pick_first, axis=1),
            jnp.take(second_source, pick_second, axis=1),
            weight_now,
        )
        if sums_far is None:
            return (carry[0].at[:, pick_first].add(near).at[:, pick_second].add(far),)
        return (carry[0].at[:, pick_first].add(near), carry[1].at[:, pick_second].add(far))

    if sums_far is None:
        return lax.fori_loop(0, steps_count, listed_advance, (sums_near,))[0]
    return lax.fori_loop(0, steps_count, listed_advance, (sums_near, sums_far))


def per_device(
    coords,
    strain,
    history,
    corner_load,
    tile_count,
    tile_sub,
    local_pairs,
    send_tile,
    remote_pairs,
    remote_count,
    corner_map,
    external,
):
    tiles_here = strain.shape[0]
    points_per = strain.shape[1]
    peers = lax.axis_size("blk")
    positions = jnp.arange(points_per, dtype=jnp.int32)
    valid_mask = (positions[None, :] < tile_count[:, None]).astype(jnp.float32)
    tile_data = jnp.concatenate([coords, strain[None], valid_mask[None]], axis=0)
    all_on = jnp.ones((tiles_here,), jnp.float32)
    tile_width = min(block_most, tiles_here)
    totals = jnp.zeros((2, tiles_here, points_per), jnp.float32)
    totals = dense_pass(tile_data, tile_data, totals)
    totals = listed_pass(
        tiles_here // tile_width,
        tile_width,
        tile_data,
        tile_data,
        local_pairs[0],
        local_pairs[1],
        all_on,
        totals,
        None,
    )
    extended = padded(tile_data, (("sub", 1),), tiles_here)
    below_tiles = extended[:, :tiles_here]
    above_tiles = extended[:, 2 * tiles_here :]
    totals = dense_pass(tile_data, below_tiles, totals)
    totals = dense_pass(tile_data, jnp.roll(below_tiles, -1, axis=1), totals)
    totals = dense_pass(tile_data, above_tiles, totals)
    totals = dense_pass(tile_data, jnp.roll(above_tiles, 1, axis=1), totals)
    outbox = jnp.take(tile_data, send_tile, axis=1)
    inbox = lax.all_to_all(outbox, "blk", split_axis=1, concat_axis=1, tiled=True)
    live_count = remote_count[0]
    slots = jnp.arange(peers, dtype=jnp.int32)
    remote_on = (slots < live_count).astype(jnp.float32)
    inbox_sums = jnp.zeros((2, peers, points_per), jnp.float32)
    remote_width = min(block_most, peers)
    remote_steps = peers // remote_width
    totals, inbox_sums = listed_pass(
        remote_steps,
        remote_width,
        tile_data,
        inbox,
        remote_pairs[0],
        remote_pairs[1],
        remote_on,
        totals,
        inbox_sums,
    )
    returned = lax.all_to_all(inbox_sums, "blk", split_axis=1, concat_axis=1, tiled=True)
    totals = totals.at[:, send_tile].add(returned)
    strain_bar = totals[0] / (totals[1] + 1.0 - valid_mask)
    kappa_new = jnp.maximum(strain_bar, history)
    damage = (
        1.0
        - (keep_share + (1.0 - keep_share) * jnp.exp(-softening * (kappa_new - 1.0))) / kappa_new
    )
    intact = (1.0 - damage) * valid_mask
    tile_part = jnp.einsum("ctp,tp->ct", corner_load, intact, precision=lax.Precision.HIGHEST)
    sub_count = corner_map.shape[0]
    sub_onehot = (tile_sub[None, :] == jnp.arange(sub_count, dtype=jnp.int32)[:, None]).astype(
        jnp.float32
    )
    sub_part = jnp.dot(sub_onehot, tile_part.T, precision=lax.Precision.HIGHEST)
    coarse_span = external.shape[0] * peers
    dense_sums = (
        jnp.zeros((coarse_span,), jnp.float32).at[corner_map.reshape(-1)].add(sub_part.reshape(-1))
    )
    internal = lax.psum_scatter(dense_sums, "blk", scatter_dimension=0, tiled=True)
    return (damage, external - internal)


def solution(mesh):
    placed = (
        P(None, ("sub", "blk"), None),
        P(("sub", "blk"), None),
        P(("sub", "blk"), None),
        P(None, ("sub", "blk"), None),
        P(("sub", "blk")),
        P(("sub", "blk")),
        P(None, ("sub", "blk")),
        P(("sub", "blk")),
        P(None, ("sub", "blk")),
        P(("sub", "blk")),
        P(("sub", "blk"), None),
        P(("sub", "blk")),
    )
    return jax.shard_map(
        per_device,
        mesh=mesh,
        in_specs=placed,
        out_specs=(P(("sub", "blk"), None), P(("sub", "blk"))),
        check_vma=False,
    )
```

profile of v0, /device:TPU:8, one launch (start us, length us, event | category | flops | bytes accessed | tf_op | source)
XLA Modules:
  0.0 208.0 jit_solution(12552419147153011510)
XLA Ops:
  12.7 3.7 %all-to-all-start = ((f32[5,8,256]{2,0,1:T(8,128)}), f32[5,8,256]{2,0,1:T(8,128)S(1)}, u32[]{:S(2)}, u32[]{:S(2)}) async-start(f32[5,8,256]{2,0,1:T(8,128)} %select_bitcast_fusion.2), calls=%async_computation | async-start | bytes 131072 | tf_op jit(solution)/shard_map/all_to_all | solution.py:138
  18.0 21.2 %while.84 = (s32[]{:T(128)}, f32[2,32,256]{2,0,1:T(2,128)S(1)}, f32[5,32,256]{2,1,0:T(8,128)S(1)}, s32[]{:T(128)}, s32[]{:T(128)}, /*index=5*/s32[]{:T(128)}, s32[]{:T(128)}, s32[]{}, s32[]{}, s32[]{}, /*index=10*/s32[]{}) while((s32[]{:T(128)}, f32[2,32,256]{2,0,1:T(2,128)S(1)}, f32[5,32,256]{2,1,0:T(8,128)S(1)}, s32[]{:T(128)}, s32[]{:T(128)}, ...), condition=%wide.region_2.0_spmd, body=%wide.region_0.0_spmd.sunk | while | flops 36712456 | bytes 606447 | solution.py:61
  18.1 3.7 %fusion.124 = f32[16,256]{1,0:T(8,128)S(1)} fusion(f32[16,256]{1,0:T(8,128)S(1)} %get-tuple-element.910, f32[16,256]{1,0:T(8,128)S(1)} %get-tuple-element.911, f32[16,256]{1,0:T(8,128)S(1)} %get-tuple-element.912, f32[16,256]{1,0:T(8,128)S(1)} %get-tuple-element.913), kind=kLoop, calls=%fused_computation.12.clone.1 | loop fusion | flops 12578816 | bytes 81920 | tf_op jit(solution)/shard_map/while/body/eval_jaxpr/reduce_sum | solution.py:36
  21.7 6.8 %fusion.125 = f32[16,1,256]{2,1,0:T(1,128)S(1)} fusion(f32[16,256]{1,0:T(8,128)S(1)} %get-tuple-element.910, f32[16,256]{1,0:T(8,128)S(1)} %get-tuple-element.911, f32[16,256]{1,0:T(8,128)S(1)} %get-tuple-element.912, f32[16,256]{1,0:T(8,128)S(1)} %get-tuple-element.913, f32[16,256,1]{1,0,2:T(8,128)S(1)} %get-tuple-element.914), kind=kOutput, calls=%fused_computation.13.clone.1 | convolution fusion | flops 24117248 | bytes 98304 | tf_op jit(solution)/shard_map/while/body/eval_jaxpr/gpq,gq->gp/dot_general | solution.py:35
  32.4 6.8 %fusion.125 = f32[16,1,256]{2,1,0:T(1,128)S(1)} fusion(f32[16,256]{1,0:T(8,128)S(1)} %get-tuple-element.910, f32[16,256]{1,0:T(8,128)S(1)} %get-tuple-element.911, f32[16,256]{1,0:T(8,128)S(1)} %get-tuple-element.912, f32[16,256]{1,0:T(8,128)S(1)} %get-tuple-element.913, f32[16,256,1]{1,0,2:T(8,128)S(1)} %get-tuple-element.914), kind=kOutput, calls=%fused_computation.13.clone.1 | convolution fusion | flops 24117248 | bytes 98304 | tf_op jit(solution)/shard_map/while/body/eval_jaxpr/gpq,gq->gp/dot_general | solution.py:35
  39.3 43.8 %while.85 = (s32[]{:T(128)}, f32[2,32,256]{2,0,1:T(2,128)S(1)}, s32[32]{0:T(128)S(1)}, f32[5,32,256]{2,0,1:T(8,128)}, s32[32]{0:T(128)S(1)}, /*index=5*/s32[]{:T(128)}, s32[]{:T(128)}, s32[]{:T(128)}, s32[]{:T(128)}) while((s32[]{:T(128)}, f32[2,32,256]{2,0,1:T(2,128)S(1)}, s32[32]{0:T(128)S(1)}, f32[5,32,256]{2,0,1:T(8,128)}, ...), condition=%wide.region_8.0_spmd, body=%wide.region_3.9_spmd.sunk | while | flops 61933764 | bytes 2204503 | solution.py:91
  46.5 6.8 %fusion.129 = f32[16,1,256]{2,1,0:T(1,128)S(1)} fusion(f32[16,256]{1,0:T(8,128)S(1)} %bitcast.328, f32[16,256]{1,0:T(8,128)S(1)} %bitcast.331, f32[16,256]{1,0:T(8,128)S(1)} %bitcast.334, f32[16,256]{1,0:T(8,128)S(1)} %bitcast.337, f32[16,256]{1,0:T(8,128)S(1)} %bitcast.340, f32[16,256]{1,0:T(8,128)S(1)} %bitcast.343, f32[16,256]{1,0:T(8,128)S(1)} %bitcast.346, ...), kind=kOutput, calls=%fused_computation.142.clone.1 | convolution fusion | flops 24117248 | bytes 163840 | tf_op jit(solution)/shard_map/while/body/eval_jaxpr/gpq,gq->gp/dot_general | solution.py:35
  54.5 5.5 %fusion.130 = f32[16,1,256]{2,1,0:T(1,128)S(1)} fusion(f32[16,256]{1,0:T(8,128)S(1)} %bitcast.329, f32[16,256]{1,0:T(8,128)S(1)} %bitcast.332, f32[16,256]{1,0:T(8,128)S(1)} %bitcast.335, f32[16,256]{1,0:T(8,128)S(1)} %bitcast.338, f32[16,256]{1,0:T(8,128)S(1)} %bitcast.341, f32[16,256]{1,0:T(8,128)S(1)} %bitcast.344, f32[16,256]{1,0:T(8,128)S(1)} %bitcast.347, ...), kind=kOutput, calls=%fused_computation.140.clone.1 | convolution fusion | flops 24117248 | bytes 163840 | tf_op jit(solution)/shard_map/while/body/eval_jaxpr/gpq,gp->gq/dot_general | solution.py:37
  68.4 6.8 %fusion.129 = f32[16,1,256]{2,1,0:T(1,128)S(1)} fusion(f32[16,256]{1,0:T(8,128)S(1)} %bitcast.328, f32[16,256]{1,0:T(8,128)S(1)} %bitcast.331, f32[16,256]{1,0:T(8,128)S(1)} %bitcast.334, f32[16,256]{1,0:T(8,128)S(1)} %bitcast.337, f32[16,256]{1,0:T(8,128)S(1)} %bitcast.340, f32[16,256]{1,0:T(8,128)S(1)} %bitcast.343, f32[16,256]{1,0:T(8,128)S(1)} %bitcast.346, ...), kind=kOutput, calls=%fused_computation.142.clone.1 | convolution fusion | flops 24117248 | bytes 163840 | tf_op jit(solution)/shard_map/while/body/eval_jaxpr/gpq,gq->gp/dot_general | solution.py:35
  76.4 5.5 %fusion.130 = f32[16,1,256]{2,1,0:T(1,128)S(1)} fusion(f32[16,256]{1,0:T(8,128)S(1)} %bitcast.329, f32[16,256]{1,0:T(8,128)S(1)} %bitcast.332, f32[16,256]{1,0:T(8,128)S(1)} %bitcast.335, f32[16,256]{1,0:T(8,128)S(1)} %bitcast.338, f32[16,256]{1,0:T(8,128)S(1)} %bitcast.341, f32[16,256]{1,0:T(8,128)S(1)} %bitcast.344, f32[16,256]{1,0:T(8,128)S(1)} %bitcast.347, ...), kind=kOutput, calls=%fused_computation.140.clone.1 | convolution fusion | flops 24117248 | bytes 163840 | tf_op jit(solution)/shard_map/while/body/eval_jaxpr/gpq,gp->gq/dot_general | solution.py:37
  98.5 4.2 %all-to-all-start.1 = ((f32[2,8,256]{2,0,1:T(2,128)}), f32[2,8,256]{2,0,1:T(2,128)S(1)}, u32[]{:S(2)}, u32[]{:S(2)}) async-start(f32[2,8,256]{2,0,1:T(2,128)} %scatter_fusion.3), calls=%async_computation.1 | async-start | bytes 32768 | tf_op jit(solution)/shard_map/all_to_all | solution.py:156
  102.7 21.2 %while.86 = (s32[]{:T(128)}, f32[2,32,256]{2,1,0:T(8,128)S(1)}, f32[5,32,256]{2,1,0:T(8,128)S(1)}, f32[5,32,256]{2,1,0:T(8,128)S(1)}, s32[]{:T(128)}, /*index=5*...) while((s32[]{:T(128)}, f32[2,32,256]{2,1,0:T(8,128)S(1)}, ...), condition=%wide.region_11.0_spmd, body=%wide.region_9.0_spmd.sunk | while | flops 36712456 | bytes 737539 | solution.py:61
  106.5 6.8 %fusion.133 = f32[16,1,256]{2,1,0:T(1,128)S(1)} fusion(f32[16,256]{1,0:T(8,128)S(1)} %get-tuple-element.938, f32[16,256]{1,0:T(8,128)S(1)} %get-tuple-element.939, f32[16,256]{1,0:T(8,128)S(1)} %get-tuple-element.940, f32[16,256]{1,0:T(8,128)S(1)} %get-tuple-element.941, f32[16,256]{1,0:T(8,128)S(1)} %get-tuple-element.942, ...), kind=kOutput, calls=%fused_computation.36.clone.1 | convolution fusion | flops 24117248 | bytes 163840 | tf_op jit(solution)/shard_map/while/body/eval_jaxpr/gpq,gq->gp/dot_general | solution.py:35
  117.0 6.8 %fusion.133 = f32[16,1,256]{2,1,0:T(1,128)S(1)} fusion(f32[16,256]{1,0:T(8,128)S(1)} %get-tuple-element.938, f32[16,256]{1,0:T(8,128)S(1)} %get-tuple-element.939, f32[16,256]{1,0:T(8,128)S(1)} %get-tuple-element.940, f32[16,256]{1,0:T(8,128)S(1)} %get-tuple-element.941, f32[16,256]{1,0:T(8,128)S(1)} %get-tuple-element.942, ...), kind=kOutput, calls=%fused_computation.36.clone.1 | convolution fusion | flops 24117248 | bytes 163840 | tf_op jit(solution)/shard_map/while/body/eval_jaxpr/gpq,gq->gp/dot_general | solution.py:35
  124.0 21.2 %while.87 = (s32[]{:T(128)}, f32[2,32,256]{2,1,0:T(8,128)S(1)}, f32[5,32,256]{2,1,0:T(8,128)S(1)}, f32[5,32,256]{2,1,0:T(8,128)S(1)}, s32[]{:T(128)}, /*index=5*...) while((s32[]{:T(128)}, f32[2,32,256]{2,1,0:T(8,128)S(1)}, ...), condition=%wide.region_14.16_spmd, body=%wide.region_12.0_spmd.sunk | while | flops 36712456 | bytes 737539 | solution.py:61
  127.8 6.8 %fusion.137 = f32[16,1,256]{2,1,0:T(1,128)S(1)} fusion(f32[16,256]{1,0:T(8,128)S(1)} %get-tuple-element.951, f32[16,256]{1,0:T(8,128)S(1)} %get-tuple-element.952, f32[16,256]{1,0:T(8,128)S(1)} %get-tuple-element.953, f32[16,256]{1,0:T(8,128)S(1)} %get-tuple-element.954, f32[16,256]{1,0:T(8,128)S(1)} %get-tuple-element.955, ...), kind=kOutput, calls=%fused_computation.62.clone.1 | convolution fusion | flops 24117248 | bytes 163840 | tf_op jit(solution)/shard_map/while/body/eval_jaxpr/gpq,gq->gp/dot_general | solution.py:35
  138.4 6.8 %fusion.137 = f32[16,1,256]{2,1,0:T(1,128)S(1)} fusion(f32[16,256]{1,0:T(8,128)S(1)} %get-tuple-element.951, f32[16,256]{1,0:T(8,128)S(1)} %get-tuple-element.952, f32[16,256]{1,0:T(8,128)S(1)} %get-tuple-element.953, f32[16,256]{1,0:T(8,128)S(1)} %get-tuple-element.954, f32[16,256]{1,0:T(8,128)S(1)} %get-tuple-element.955, ...), kind=kOutput, calls=%fused_computation.62.clone.1 | convolution fusion | flops 24117248 | bytes 163840 | tf_op jit(solution)/shard_map/while/body/eval_jaxpr/gpq,gq->gp/dot_general | solution.py:35
  145.3 21.2 %while.88 = (s32[]{:T(128)}, f32[2,32,256]{2,1,0:T(8,128)S(1)}, f32[5,32,256]{2,1,0:T(8,128)S(1)}, f32[5,32,256]{2,1,0:T(8,128)S(1)}, s32[]{:T(128)}, /*index=5*...) while((s32[]{:T(128)}, f32[2,32,256]{2,1,0:T(8,128)S(1)}, ...), condition=%wide.region_17.19_spmd, body=%wide.region_15.18_spmd.sunk | while | flops 36712456 | bytes 737539 | solution.py:61
  149.0 6.8 %fusion.141 = f32[16,1,256]{2,1,0:T(1,128)S(1)} fusion(f32[16,256]{1,0:T(8,128)S(1)} %get-tuple-element.964, f32[16,256]{1,0:T(8,128)S(1)} %get-tuple-element.965, f32[16,256]{1,0:T(8,128)S(1)} %get-tuple-element.966, f32[16,256]{1,0:T(8,128)S(1)} %get-tuple-element.967, f32[16,256]{1,0:T(8,128)S(1)} %get-tuple-element.968, ...), kind=kOutput, calls=%fused_computation.88.clone.1 | convolution fusion | flops 24117248 | bytes 163840 | tf_op jit(solution)/shard_map/while/body/eval_jaxpr/gpq,gq->gp/dot_general | solution.py:35
  159.6 6.8 %fusion.141 = f32[16,1,256]{2,1,0:T(1,128)S(1)} fusion(f32[16,256]{1,0:T(8,128)S(1)} %get-tuple-element.964, f32[16,256]{1,0:T(8,128)S(1)} %get-tuple-element.965, f32[16,256]{1,0:T(8,128)S(1)} %get-tuple-element.966, f32[16,256]{1,0:T(8,128)S(1)} %get-tuple-element.967, f32[16,256]{1,0:T(8,128)S(1)} %get-tuple-element.968, ...), kind=kOutput, calls=%fused_computation.88.clone.1 | convolution fusion | flops 24117248 | bytes 163840 | tf_op jit(solution)/shard_map/while/body/eval_jaxpr/gpq,gq->gp/dot_general | solution.py:35
  166.7 21.2 %while.89 = (s32[]{:T(128)}, f32[2,32,256]{2,1,0:T(8,128)S(1)}, f32[5,32,256]{2,1,0:T(8,128)S(1)}, f32[5,32,256]{2,1,0:T(8,128)S(1)}, s32[]{:T(128)}, /*index=5*...) while((s32[]{:T(128)}, f32[2,32,256]{2,1,0:T(8,128)S(1)}, ...), condition=%wide.region_20.22_spmd, body=%wide.region_18.21_spmd.sunk | while | flops 36712456 | bytes 737539 | solution.py:61
  170.4 6.8 %fusion.145 = f32[16,1,256]{2,1,0:T(1,128)S(1)} fusion(f32[16,256]{1,0:T(8,128)S(1)} %get-tuple-element.977, f32[16,256]{1,0:T(8,128)S(1)} %get-tuple-element.978, f32[16,256]{1,0:T(8,128)S(1)} %get-tuple-element.979, f32[16,256]{1,0:T(8,128)S(1)} %get-tuple-element.980, f32[16,256]{1,0:T(8,128)S(1)} %get-tuple-element.981, ...), kind=kOutput, calls=%fused_computation.114.clone.1 | convolution fusion | flops 24117248 | bytes 163840 | tf_op jit(solution)/shard_map/while/body/eval_jaxpr/gpq,gq->gp/dot_general | solution.py:35
  181.0 6.8 %fusion.145 = f32[16,1,256]{2,1,0:T(1,128)S(1)} fusion(f32[16,256]{1,0:T(8,128)S(1)} %get-tuple-element.977, f32[16,256]{1,0:T(8,128)S(1)} %get-tuple-element.978, f32[16,256]{1,0:T(8,128)S(1)} %get-tuple-element.979, f32[16,256]{1,0:T(8,128)S(1)} %get-tuple-element.980, f32[16,256]{1,0:T(8,128)S(1)} %get-tuple-element.981, ...), kind=kOutput, calls=%fused_computation.114.clone.1 | convolution fusion | flops 24117248 | bytes 163840 | tf_op jit(solution)/shard_map/while/body/eval_jaxpr/gpq,gq->gp/dot_general | solution.py:35
  193.0 14.5 %all-reduce = f32[1024]{0:T(1024)S(1)} all-reduce(f32[1024]{0:T(1024)S(1)} %scatter_custom_fusion.5), channel_id=2, replica_groups=mesh['sub'=4,'blk'=8] {'blk'}, use_global_device_ids=true, to_apply=%region_27.30.clone | all-reduce | flops 1024 | bytes 8192
  (197 shorter events, 85.8 us)
Async XLA Ops:
  0.6 189.7 %copy-start = (f32[24,32,256]{2,1,0:T(8,128)S(1)}, f32[24,32,256]{2,1,0:T(8,128)}, u32[]{:S(2)}) copy-start(f32[24,32,256]{2,1,0:T(8,128)} %param.31) | copy-start | bytes 2359300
  0.6 9.2 %copy-start.11 = (s32[8]{0:T(128)S(1)}, s32[8]{0:T(128)}, u32[]{:S(2)}) copy-start(s32[8]{0:T(128)} %param.35) | copy-start | bytes 100
  0.7 16.8 %copy-start.2 = (s32[2,8]{1,0:T(2,128)S(1)}, s32[2,8]{1,0:T(2,128)}, u32[]{:S(2)}) copy-start(s32[2,8]{1,0:T(2,128)} %param.36) | copy-start | bytes 196
  4.0 98.6 %collective-permute-start = (f32[5,32,256]{2,0,1:T(8,128)}, f32[5,32,256]{2,0,1:T(8,128)S(1)}, u32[]{:S(2)}, u32[]{:S(2)}) collective-permute-start(f32[5,32,256]{2,0,1:T(8,128)} %pad_maximum_fusion), channel_id=1, source_target_pairs={{0,8},{8,16},{16,24},{1,9},{9,17},{17,25},{2,10},{10,18},{18,26},{... | collective-permute-start | bytes 491528 | tf_op jit(solution)/shard_map/ppermute | solution.py:20
  7.5 137.7 %collective-permute-start.1 = (f32[5,32,256]{2,0,1:T(8,128)}, f32[5,32,256]{2,0,1:T(8,128)S(1)}, u32[]{:S(2)}, u32[]{:S(2)}) collective-permute-start(f32[5,32,256]{2,0,1:T(8,128)} %pad_maximum_fusion), channel_id=1, source_target_pairs={{8,0},{16,8},{24,16},{9,1},{17,9},{25,17},{10,2},{18,10},{26,18},{... | collective-permute-start | bytes 491528 | tf_op jit(solution)/shard_map/ppermute | solution.py:22
  9.9 0.5 copy-start.4
  12.7 74.2 %all-to-all-start = ((f32[5,8,256]{2,0,1:T(8,128)}), f32[5,8,256]{2,0,1:T(8,128)S(1)}, u32[]{:S(2)}, u32[]{:S(2)}) async-start(f32[5,8,256]{2,0,1:T(8,128)} %select_bitcast_fusion.2), calls=%async_computation | async-start | bytes 131072 | tf_op jit(solution)/shard_map/all_to_all | solution.py:138
  18.0 21.2 %copy-start.8 = (s32[2,32]{1,0:T(2,128)S(1)}, s32[2,32]{1,0:T(2,128)}, u32[]{:S(2)}) copy-start(s32[2,32]{1,0:T(2,128)} %param.34) | copy-start | bytes 772
  39.3 46.2 %copy-start.7 = (s32[4,24]{1,0:T(4,128)S(1)}, s32[4,24]{1,0:T(4,128)}, u32[]{:S(2)}) copy-start(s32[4,24]{1,0:T(4,128)} %param.38) | copy-start | bytes 1156
  39.3 46.3 %copy-start.12 = (u32[32]{0:T(128)S(1)}, u32[32]{0:T(128)}, u32[]{:S(2)}) copy-start(u32[32]{0:T(128)} %constant.326) | copy-start | bytes 388
  98.5 90.3 %all-to-all-start.1 = ((f32[2,8,256]{2,0,1:T(2,128)}), f32[2,8,256]{2,0,1:T(2,128)S(1)}, u32[]{:S(2)}, u32[]{:S(2)}) async-start(f32[2,8,256]{2,0,1:T(2,128)} %scatter_fusion.3), calls=%async_computation.1 | async-start | bytes 32768 | tf_op jit(solution)/shard_map/all_to_all | solution.py:156
  166.6 21.3 %copy-start.6 = (s32[8]{0:T(128)S(1)}, s32[8]{0:T(128)}, u32[]{:S(2)}) copy-start(s32[8]{0:T(128)} %get-tuple-element.715) | copy-start | bytes 100
  166.6 22.1 %copy-start.5 = (s32[8]{0:T(128)S(1)}, s32[8]{0:T(128)}, u32[]{:S(2)}) copy-start(s32[8]{0:T(128)} %copy-done.4) | copy-start | bytes 100
  166.6 23.0 %copy-start.1 = (f32[32,256]{1,0:T(8,128)S(1)}, f32[32,256]{1,0:T(8,128)}, u32[]{:S(2)}) copy-start(f32[32,256]{1,0:T(8,128)} %param.30) | copy-start | bytes 98308
  166.6 23.0 %copy-start.3 = (s32[32]{0:T(128)S(1)}, s32[32]{0:T(128)}, u32[]{:S(2)}) copy-start(s32[32]{0:T(128)} %param.32) | copy-start | bytes 388
  187.8 3.7 %copy-start.9 = (s32[32]{0:T(128)S(1)}, s32[32]{0:T(128)}, u32[]{:S(2)}) copy-start(s32[32]{0:T(128)} %param.33) | copy-start | bytes 388
  187.9 19.6 %copy-start.10 = (f32[128]{0:T(128)S(1)}, f32[128]{0:T(128)}, u32[]{:S(2)}) copy-start(f32[128]{0:T(128)} %param.39) | copy-start | bytes 1540
where the time goes:
time: 209 us; the launch traced here: 208 us
  matrix products  100 us (48%)
  other arithmetic  60.3 us (29%)
  local copies, waits for them, and re-layouts  15.6 us (7%)
  blocking collectives  14.5 us (7%)
  starting transfers between devices  13.8 us (7%)
  between operations  2.52 us (1%)
    dot_general x13, matrix products, pair_block(): jnp.einsum('gpq,gq->gp', kernel, second[3], precision=lax.Precision.HIGHEST)  85.3 us
    reduce_sum x10, other arithmetic, pair_block(): den_first = jnp.sum(kernel, axis=2)  36.5 us
    unnamed x1, blocking collectives  14.5 us
    dot_general x3, matrix products, pair_block(): jnp.einsum('gpq,gp->gq', kernel, first[3], precision=lax.Precision.HIGHEST)  13.9 us
    reduce_sum x3, other arithmetic, pair_block(): den_second = jnp.sum(kernel, axis=1)  9.16 us
    gather x3, local copies, waits for them, and re-layouts, listed_advance(): jnp.take(first_source, pick_first, axis=1)  4.51 us
    scatter-add x4, other arithmetic, listed_advance(): return (carry[0].at[:, pick_first].add(near).at[:, pick_second].add(far),)  4.51 us
    all_to_all x1, starting transfers between devices, per_device(): lax.all_to_all(inbox_sums, 'blk', split_axis=1, concat_axis=1, tiled=True)  4.19 us
  transfers between devices with their start and end apart: 4, of which 0 were waited for; matrix products, arithmetic and copies ran while one was open for 81% of the time, Pallas kernels for 0%

commit v1 on v0

v1 whole, which is shorter than its diff:
```python
import functools
import math

import jax
import jax.numpy as jnp
from jax import lax
from jax.experimental import pallas as pl
from jax.experimental.pallas import tpu as pltpu
from jax.sharding import PartitionSpec as P

gauss_rate = 4.0
keep_share = 0.05
softening = 0.5
coord_scale = math.sqrt(gauss_rate * math.log2(math.e))
far_off = 2048.0
depth = 32
grant = 48 * 1024 * 1024

f32 = jnp.float32
bf16 = jnp.bfloat16
in_vmem = pl.BlockSpec(memory_space=pltpu.VMEM)
in_smem = pl.BlockSpec(memory_space=pltpu.SMEM)


def pieces(value):
    high = value.astype(bf16).astype(f32)
    rest = value - high
    middle = rest.astype(bf16).astype(f32)
    low = (rest - middle).astype(bf16).astype(f32)
    return high, middle, low


def put_rows(rows_ref, tiles, rows):
    for r, row in enumerate(rows):
        for half in range(row.shape[1] // 128):
            rows_ref[half, pl.ds(r, tiles, stride=depth), :] = row[:, half * 128 : (half + 1) * 128]


def point_rows(planes):
    scaled = [p * coord_scale for p in planes[:3]]
    split = [pieces(s) for s in scaled]
    norm = scaled[0] * scaled[0] + scaled[1] * scaled[1] + scaled[2] * scaled[2]
    return split, norm


def build_source(planes, rows_ref, a_ref, s_ref, base):
    tiles = planes[3].shape[0]
    split, norm = point_rows(planes)
    ones = jnp.ones_like(norm)
    zeros = jnp.zeros_like(norm)
    norm = norm + jnp.where(planes[3] > 0.0, 0.0, far_off)
    rows = []
    for high, middle, low in split:
        rows += [high, high, middle, high, low, middle]
    rows += list(pieces(-norm)) + [ones, ones, ones] + [planes[3]]
    rows += [zeros] * (depth - len(rows))
    put_rows(rows_ref, tiles, rows)
    halves = norm.shape[1] // 128

    def one_tile(t, carry):
        for half in range(halves):
            block = rows_ref[half, pl.ds(pl.multiple_of(t * depth, depth), depth), :]
            turned = block.T
            a_ref[base + t, half * 128 : (half + 1) * 128, :] = turned.astype(bf16)
            s_ref[base + t, half * 128 : (half + 1) * 128, :] = jnp.broadcast_to(turned[:, 24:25], (128, 128))
        return carry

    lax.fori_loop(0, tiles, one_tile, 0)


def build_target(planes, rows_ref, b_ref):
    tiles = planes[3].shape[0]
    split, norm = point_rows(planes)
    ones = jnp.ones_like(norm)
    zeros = jnp.zeros_like(norm)
    rows = []
    for high, middle, low in split:
        rows += [2.0 * v for v in (high, middle, high, low, high, middle)]
    rows += [ones, ones, ones] + list(pieces(-norm))
    rows += [zeros] * (depth - len(rows))
    put_rows(rows_ref, tiles, rows)
    halves = norm.shape[1] // 128

    def one_tile(t, carry):
        for half in range(halves):
            block = rows_ref[half, pl.ds(pl.multiple_of(t * depth, depth), depth), :]
            b_ref[t, :, half * 128 : (half + 1) * 128] = block.astype(bf16)
        return carry

    lax.fori_loop(0, tiles, one_tile, 0)


def pair_sums(a, s, b):
    points = a.shape[0]
    width = b.shape[1]
    step = min(points, 128)
    num = jnp.zeros((8, width), f32)
    den = jnp.zeros((8, width), f32)
    for lo in range(0, points, step):
        power = jnp.dot(a[lo : lo + step], b, preferred_element_type=f32)
        weight = jnp.exp2(power)
        load = jnp.concatenate([s[lo : lo + step]] * (width // 128), axis=1)
        den = den + jnp.sum(weight.reshape(step // 8, 8, width), axis=0)
        num = num + jnp.sum((weight * load).reshape(step // 8, 8, width), axis=0)
    return num, den


def pack_kernel(peers, coords, strain, tile_count, send_tile, remote_pairs, remote_count, payload, outbox):
    tiles, points = strain.shape
    payload[0:3] = coords[...]
    lane = lax.broadcasted_iota(jnp.int32, (1, points), 1)
    for t in range(tiles):
        payload[3, t : t + 1, :] = jnp.where(lane < tile_count[t], strain[t : t + 1, :], 0.0)

    def sent(h, carry):
        t = send_tile[h]
        for k in range(4):
            outbox[h, k : k + 1, :] = payload[k, pl.ds(t, 1), :]
        return carry

    def listed(i, carry):
        t = remote_pairs[0, i]
        h = remote_pairs[1, i]
        live = (i < remote_count[0]).astype(f32)
        for k in range(3):
            outbox[h, 4 + k : 5 + k, :] = payload[k, pl.ds(t, 1), :]
        outbox[h, 7:8, :] = payload[3, pl.ds(t, 1), :] * live
        return carry

    lax.fori_loop(0, peers, sent, 0)
    lax.fori_loop(0, peers, listed, 0)


def own_kernel(payload, local_pairs, b_ref, num_ref, den_ref, rows_ref, a_ref, s_ref):
    tiles = payload.shape[1]
    planes = [payload[k] for k in range(4)]
    build_source(planes, rows_ref, a_ref, s_ref, 0)
    build_target(planes, rows_ref, b_ref)

    def own(t, carry):
        num, den = pair_sums(a_ref[t], s_ref[t], b_ref[t])
        num_ref[t] = num
        den_ref[t] = den
        return carry

    lax.fori_loop(0, tiles, own, 0)

    def listed(i, carry):
        one = local_pairs[0, i]
        two = local_pairs[1, i]
        for src, dst in ((one, two), (two, one)):
            num, den = pair_sums(a_ref[src], s_ref[src], b_ref[dst])
            num_ref[dst] = num_ref[dst] + num
            den_ref[dst] = den_ref[dst] + den
        return carry

    lax.fori_loop(0, local_pairs.shape[1], listed, 0)


def rest_kernel(
    peers,
    below,
    above,
    inbox,
    b_ref,
    num_in,
    den_in,
    payload,
    history,
    corner_load,
    tile_sub,
    corner_map,
    send_tile,
    remote_pairs,
    remote_count,
    damage_ref,
    parts_ref,
    rows_ref,
    a_ref,
    s_ref,
    far_rows,
    far_a,
    far_s,
    num_ref,
    den_ref,
    sub_rows,
    map_rows,
):
    tiles, points = history.shape
    num_ref[...] = num_in[...]
    den_ref[...] = den_in[...]

    def border(offset):
        def one(t, carry):
            num = num_ref[t]
            den = den_ref[t]
            other = lax.rem(t + offset, tiles)
            for src in (t, other):
                more_num, more_den = pair_sums(a_ref[src], s_ref[src], b_ref[t])
                num = num + more_num
                den = den + more_den
            num_ref[t] = num
            den_ref[t] = den
            return carry

        lax.fori_loop(0, tiles, one, 0)

    build_source([below[k] for k in range(4)], rows_ref, a_ref, s_ref, 0)
    border(1)
    build_source([above[k] for k in range(4)], rows_ref, a_ref, s_ref, 0)
    border(tiles - 1)

    for which in range(2):
        planes = [
            jnp.concatenate(
                [inbox[half, pl.ds(4 * which + k, peers, stride=8), :] for half in range(points // 128)], axis=1
            )
            for k in range(4)
        ]
        build_source(planes, far_rows, far_a, far_s, which * peers)

    def add_far(src, dst):
        num, den = pair_sums(far_a[src], far_s[src], b_ref[dst])
        num_ref[dst] = num_ref[dst] + num
        den_ref[dst] = den_ref[dst] + den

    def listed(i, carry):
        add_far(remote_pairs[1, i], remote_pairs[0, i])
        return carry

    def named(h, carry):
        add_far(peers + h, send_tile[h])
        return carry

    lax.fori_loop(0, remote_count[0], listed, 0)
    lax.fori_loop(0, peers, named, 0)

    valid = (payload[3] > 0.0).astype(f32)
    num = jnp.sum(num_ref[...], axis=1) * valid
    den = jnp.sum(den_ref[...], axis=1) * valid
    strain_bar = num / (den + 1.0 - valid)
    kappa = jnp.maximum(strain_bar, history[...])
    damage = 1.0 - (keep_share + (1.0 - keep_share) * jnp.exp(-softening * (kappa - 1.0))) / kappa
    damage_ref[...] = damage
    intact = (1.0 - damage) * valid

    for t in range(tiles):
        sub_rows[t : t + 1, :] = jnp.full((1, 128), tile_sub[t], jnp.int32)
    subs, corners = corner_map.shape
    for m in range(subs):
        for c in range(corners):
            r = m * corners + c
            map_rows[r : r + 1, :] = jnp.full((1, 128), corner_map[m, c], jnp.int32)

    folded = corner_load[:, :, 0:128] * intact[None, :, 0:128]
    for half in range(1, points // 128):
        cut = slice(half * 128, (half + 1) * 128)
        folded = folded + corner_load[:, :, cut] * intact[None, :, cut]
    owner = sub_rows[...]
    sums = []
    for m in range(subs):
        chosen = jnp.where((owner == m)[None], folded, 0.0)
        sums.append(jnp.sum(jnp.sum(chosen, axis=1), axis=1, keepdims=True))
    sub_part = jnp.broadcast_to(jnp.concatenate(sums, axis=0), (subs * corners, 128))
    target = map_rows[...] - lax.broadcasted_iota(jnp.int32, (subs * corners, 128), 1)

    def scatter(j, carry):
        parts_ref[pl.ds(j, 1), :] = jnp.sum(jnp.where(target == j * 128, sub_part, 0.0), axis=0, keepdims=True)
        return carry

    lax.fori_loop(0, peers, scatter, 0, unroll=peers <= 8)


def per_device(
    coords,
    strain,
    history,
    corner_load,
    tile_count,
    tile_sub,
    local_pairs,
    send_tile,
    remote_pairs,
    remote_count,
    corner_map,
    external,
):
    tiles, points = strain.shape
    halves = points // 128
    peers = lax.axis_size("blk")
    layers = lax.axis_size("sub")
    subs, corners = corner_map.shape
    params = pltpu.CompilerParams(vmem_limit_bytes=grant)
    block = 2 * points * points

    payload, outbox = pl.pallas_call(
        functools.partial(pack_kernel, peers),
        out_shape=(
            jax.ShapeDtypeStruct((4, tiles, points), f32),
            jax.ShapeDtypeStruct((peers, 8, points), f32),
        ),
        in_specs=[in_vmem] * 2 + [in_smem] * 4,
        out_specs=(in_vmem, in_vmem),
        compiler_params=params,
        name="pack",
    )(coords, strain, tile_count, send_tile, remote_pairs, remote_count)

    up = [(i, i + 1) for i in range(layers - 1)]
    down = [(i + 1, i) for i in range(layers - 1)]
    below = lax.ppermute(payload, "sub", up)
    above = lax.ppermute(payload, "sub", down)
    inbox = lax.all_to_all(outbox, "blk", split_axis=0, concat_axis=0, tiled=True)

    b_own, num, den = pl.pallas_call(
        own_kernel,
        out_shape=(
            jax.ShapeDtypeStruct((tiles, depth, points), bf16),
            jax.ShapeDtypeStruct((tiles, 8, points), f32),
            jax.ShapeDtypeStruct((tiles, 8, points), f32),
        ),
        in_specs=[in_vmem, in_smem],
        out_specs=(in_vmem,) * 3,
        scratch_shapes=[
            pltpu.VMEM((halves, tiles * depth, 128), f32),
            pltpu.VMEM((tiles, points, depth), bf16),
            pltpu.VMEM((tiles, points, 128), f32),
        ],
        compiler_params=params,
        cost_estimate=pl.CostEstimate(
            flops=3 * tiles * block * depth, bytes_accessed=1 << 20, transcendentals=3 * tiles * points * points
        ),
        name="own",
    )(payload, local_pairs)

    inbox = inbox.reshape(peers * 8, halves, 128).transpose(1, 0, 2)
    damage, parts = pl.pallas_call(
        functools.partial(rest_kernel, peers),
        out_shape=(
            jax.ShapeDtypeStruct((tiles, points), f32),
            jax.ShapeDtypeStruct((peers, 128), f32),
        ),
        in_specs=[in_vmem] * 9 + [in_smem] * 5,
        out_specs=(in_vmem,) * 2,
        scratch_shapes=[
            pltpu.VMEM((halves, tiles * depth, 128), f32),
            pltpu.VMEM((tiles, points, depth), bf16),
            pltpu.VMEM((tiles, points, 128), f32),
            pltpu.VMEM((halves, peers * depth, 128), f32),
            pltpu.VMEM((2 * peers, points, depth), bf16),
            pltpu.VMEM((2 * peers, points, 128), f32),
            pltpu.VMEM((tiles, 8, points), f32),
            pltpu.VMEM((tiles, 8, points), f32),
            pltpu.VMEM((tiles, 128), jnp.int32),
            pltpu.VMEM((subs * corners, 128), jnp.int32),
        ],
        compiler_params=params,
        cost_estimate=pl.CostEstimate(
            flops=4 * tiles * block * depth, bytes_accessed=1 << 21, transcendentals=4 * tiles * points * points
        ),
        name="rest",
    )(
        below,
        above,
        inbox,
        b_own,
        num,
        den,
        payload,
        history,
        corner_load,
        tile_sub,
        corner_map,
        send_tile,
        remote_pairs,
        remote_count,
    )
    gathered = lax.all_to_all(parts, "blk", split_axis=0, concat_axis=0, tiled=True)
    return damage, external - jnp.sum(gathered, axis=0)


def solution(mesh):
    placed = (
        P(None, ("sub", "blk"), None),
        P(("sub", "blk"), None),
        P(("sub", "blk"), None),
        P(None, ("sub", "blk"), None),
        P(("sub", "blk")),
        P(("sub", "blk")),
        P(None, ("sub", "blk")),
        P(("sub", "blk")),
        P(None, ("sub", "blk")),
        P(("sub", "blk")),
        P(("sub", "blk"), None),
        P(("sub", "blk")),
    )
    return jax.shard_map(
        per_device,
        mesh=mesh,
        in_specs=placed,
        out_specs=(P(("sub", "blk"), None), P(("sub", "blk"))),
        check_vma=False,
    )
```

time: 209 us -> 81.2 us (0.39)
  the two profiles are of different devices: /device:TPU:8 before, /device:TPU:0 now
where the time goes in v1:
time: 81.2 us; the launch traced here: 80.7 us
  Pallas kernels  55.7 us (69%)
  starting transfers between devices  11 us (14%)
  blocking collectives  8.28 us (10%)
  local copies, waits for them, and re-layouts  3.68 us (5%)
  between operations  1.46 us (2%)
    pallas_call x1, Pallas kernels, per_device(): pl.pallas_call(functools.partial(rest_kernel, peers), out_shape=(jax.Shap...  33.6 us
    pallas_call x1, Pallas kernels, per_device(): pl.pallas_call(own_kernel, out_shape=(jax.ShapeDtypeStruct((tiles, depth,...  20.7 us
    all_to_all x1, blocking collectives, per_device(): lax.all_to_all(parts, 'blk', split_axis=0, concat_axis=0, tiled=True)  8.28 us
    ppermute x1, starting transfers between devices, per_device(): below = lax.ppermute(payload, 'sub', up)  5.56 us
    all_to_all x1, starting transfers between devices, per_device(): lax.all_to_all(outbox, 'blk', split_axis=0, concat_axis=0, tiled=True)  4.17 us
    unnamed x24, local copies, waits for them, and re-layouts  3.64 us
  transfers between devices with their start and end apart: 3, of which 0 were waited for; matrix products, arithmetic and copies ran while one was open for 0% of the time, Pallas kernels for 26%

profile of v1, /device:TPU:0, one launch (start us, length us, event | category | flops | bytes accessed | tf_op | source)
XLA Modules:
  0.0 80.7 jit_solution(7867517389001107099)
XLA Ops:
  0.6 0.0 copy-start.2
  1.3 0.9 %copy-done = f32[3,32,256]{2,1,0:T(8,128)S(1)} copy-done((f32[3,32,256]{2,1,0:T(8,128)S(1)}, f32[3,32,256]{2,1,0:T(8,128)}, u32[]{:S(2)}) %copy-start) | copy-done | bytes 98328
  2.2 0.8 copy-done.1
  3.0 0.7 copy-done.4
  3.6 1.4 %pack.1 = (f32[4,32,256]{2,1,0:T(8,128)S(1)}, f32[8,8,256]{2,1,0:T(8,128)}) custom-call(f32[3,32,256]{2,1,0:T(8,128)S(1)} %copy-done, f32[32,256]{1,0:T(8,128)S(1)} %copy-done.1, s32[32]{0:T(128)S(1)} %copy-done.3, s32[8]{0:T(128)S(1)} %copy-done.4, s32[2,8]{1,0:T(2,128)S(1)} %copy-done.2, s32[1]{0:T(128)S(6)} %copy.19.remote_count), custom_call_target="tpu_custom_call" | custom-call | tf_op jit(solution)/shard_map/pack/pallas_call | solution.py:296
  5.0 1.3 %collective-permute-start.1 = (f32[4,32,256]{2,1,0:T(8,128)S(1)}, f32[4,32,256]{2,1,0:T(8,128)S(1)}, u32[]{:S(2)}, u32[]{:S(2)}) collective-permute-start(f32[4,32,256]{2,1,0:T(8,128)S(1)} %get-tuple-element.9.payload), channel_id=1, source_target_pairs={{8,0},{16,8},{24,16},{9,1},{17,9},{25,17},{10,2},{18,10},{26,18},{... | collective-permute-start | bytes 393224 | tf_op jit(solution)/shard_map/ppermute | solution.py:311
  6.3 5.6 %collective-permute-start = (f32[4,32,256]{2,1,0:T(8,128)S(1)}, f32[4,32,256]{2,1,0:T(8,128)S(1)}, u32[]{:S(2)}, u32[]{:S(2)}) collective-permute-start(f32[4,32,256]{2,1,0:T(8,128)S(1)} %get-tuple-element.9.payload), channel_id=1, source_target_pairs={{0,8},{8,16},{16,24},{1,9},{9,17},{17,25},{2,10},{10,18},{18,26},{... | collective-permute-start | bytes 393224 | tf_op jit(solution)/shard_map/ppermute | solution.py:310
  11.9 0.0 copy-start.9
  11.9 4.2 %all-to-all-start = ((f32[8,8,256]{2,1,0:T(8,128)}), f32[8,8,256]{2,1,0:T(8,128)S(1)}, u32[]{:S(2)}, u32[]{:S(2)}) async-start(f32[8,8,256]{2,1,0:T(8,128)} %get-tuple-element.10), calls=%async_computation | async-start | bytes 131072 | tf_op jit(solution)/shard_map/all_to_all | solution.py:312
  16.1 0.0 copy-start.6
  16.1 20.7 %own.1 = (bf16[32,32,256]{2,1,0:T(8,128)(2,1)S(1)}, f32[32,8,256]{2,1,0:T(8,128)S(1)}, f32[32,8,256]{2,1,0:T(8,128)S(1)}) custom-call(f32[4,32,256]{2,1,0:T(8,128)S(1)} %get-tuple-element.9.payload, s32[2,32]{1,0:T(2,128)S(1)} %copy-done.9), custom_call_target="tpu_custom_call" | custom-call | flops 402653184 | bytes 1048576 | tf_op jit(solution)/shard_map/own/pallas_call | solution.py:314
  36.8 0.0 all-to-all-done
  36.8 0.0 copy-start.7
  36.9 0.0 collective-permute-done.1.above
  36.9 0.0 collective-permute-done.below
  36.9 0.0 copy-start.8
  36.9 0.0 copy-start.5
  36.9 0.0 copy-start.10
  36.9 0.7 copy-done.7
  37.6 0.0 copy-done.8
  37.6 33.6 %rest.1 = (f32[32,256]{1,0:T(8,128)}, f32[8,128]{1,0:T(8,128)S(1)}) custom-call(f32[4,32,256]{2,1,0:T(8,128)S(1)} %collective-permute-done.below, f32[4,32,256]{2,1,0:T(8,128)S(1)} %collective-permute-done.1.above, f32[2,64,128]{2,1,0:T(8,128)S(1)} %bitcast.6, bf16[32,32,256]{2,1,0:T(8,128)(2,1)S(1)} %get-tuple-element.11.b_ref, ...), custom_call_target="tpu_custom_call" | custom-call | flops 536870912 | bytes 2097152 | tf_op jit(solution)/shard_map/rest/pallas_call | solution.py:336
  71.2 8.3 %all_to_all.14 = f32[8,1,128]{2,1,0:T(1,128)S(1)} all-to-all(f32[8,1,128]{2,1,0:T(1,128)S(1)} %bitcast.7), channel_id=1, replica_groups=mesh['sub'=4,'blk'=8] {'blk'}, dimensions={0} | all-to-all | bytes 8192 | tf_op jit(solution)/shard_map/all_to_all | solution.py:377
  79.5 0.6 copy-done.11
  80.2 0.5 sub.3
  (14 shorter events, 0.1 us)
Async XLA Ops:
  0.6 0.7 copy-start.2
  0.6 0.7 copy-start.3
  1.3 0.9 %copy-start = (f32[3,32,256]{2,1,0:T(8,128)S(1)}, f32[3,32,256]{2,1,0:T(8,128)}, u32[]{:S(2)}) copy-start(f32[3,32,256]{2,1,0:T(8,128)} %coords.1) | copy-start | bytes 294916
  2.2 0.8 copy-start.1
  3.0 0.7 copy-start.4
  5.0 31.8 %collective-permute-start.1 = (f32[4,32,256]{2,1,0:T(8,128)S(1)}, f32[4,32,256]{2,1,0:T(8,128)S(1)}, u32[]{:S(2)}, u32[]{:S(2)}) collective-permute-start(f32[4,32,256]{2,1,0:T(8,128)S(1)} %get-tuple-element.9.payload), channel_id=1, source_target_pairs={{8,0},{16,8},{24,16},{9,1},{17,9},{25,17},{10,2},{18,10},{26,18},{... | collective-permute-start | bytes 393224 | tf_op jit(solution)/shard_map/ppermute | solution.py:311
  6.3 30.6 %collective-permute-start = (f32[4,32,256]{2,1,0:T(8,128)S(1)}, f32[4,32,256]{2,1,0:T(8,128)S(1)}, u32[]{:S(2)}, u32[]{:S(2)}) collective-permute-start(f32[4,32,256]{2,1,0:T(8,128)S(1)} %get-tuple-element.9.payload), channel_id=1, source_target_pairs={{0,8},{8,16},{16,24},{1,9},{9,17},{17,25},{2,10},{10,18},{18,26},{... | collective-permute-start | bytes 393224 | tf_op jit(solution)/shard_map/ppermute | solution.py:310
  11.9 4.2 %copy-start.9 = (s32[2,32]{1,0:T(2,128)S(1)}, s32[2,32]{1,0:T(2,128)}, u32[]{:S(2)}) copy-start(s32[2,32]{1,0:T(2,128)} %local_pairs.1) | copy-start | bytes 772
  11.9 24.9 %all-to-all-start = ((f32[8,8,256]{2,1,0:T(8,128)}), f32[8,8,256]{2,1,0:T(8,128)S(1)}, u32[]{:S(2)}, u32[]{:S(2)}) async-start(f32[8,8,256]{2,1,0:T(8,128)} %get-tuple-element.10), calls=%async_computation | async-start | bytes 131072 | tf_op jit(solution)/shard_map/all_to_all | solution.py:312
  16.1 20.8 %copy-start.6 = (f32[24,32,256]{2,1,0:T(8,128)S(1)}, f32[24,32,256]{2,1,0:T(8,128)}, u32[]{:S(2)}) copy-start(f32[24,32,256]{2,1,0:T(8,128)} %corner_load.1) | copy-start | bytes 2359300
  36.8 0.8 copy-start.7
  36.9 0.7 copy-start.8
  36.9 0.7 copy-start.5
  36.9 0.7 copy-start.10
  79.5 0.7 copy-start.11

commit v2 on v1

--- a/solution.py
+++ b/solution.py
@@ -19,7 +19,7 @@
 f32 = jnp.float32
 bf16 = jnp.bfloat16
 in_vmem = pl.BlockSpec(memory_space=pltpu.VMEM)
-in_smem = pl.BlockSpec(memory_space=pltpu.SMEM)
+anywhere = pl.BlockSpec(memory_space=pl.ANY)
 
 
 def pieces(value):
@@ -105,12 +105,41 @@
     return num, den
 
 
-def pack_kernel(peers, coords, strain, tile_count, send_tile, remote_pairs, remote_count, payload, outbox):
+def fetch(sources, targets, sems):
+    copies = [pltpu.make_async_copy(src, dst, sems.at[i]) for i, (src, dst) in enumerate(zip(sources, targets))]
+    for copy in copies:
+        copy.start()
+    return copies
+
+
+def pack_kernel(
+    peers,
+    coords,
+    strain,
+    tile_count_in,
+    send_tile_in,
+    remote_pairs_in,
+    remote_count_in,
+    payload,
+    outbox,
+    strain_here,
+    tile_count,
+    send_tile,
+    remote_pairs,
+    remote_count,
+    sems,
+):
     tiles, points = strain.shape
-    payload[0:3] = coords[...]
+    copies = fetch(
+        (coords, strain, tile_count_in, send_tile_in, remote_pairs_in, remote_count_in),
+        (payload.at[0:3], strain_here, tile_count, send_tile, remote_pairs, remote_count),
+        sems,
+    )
+    for copy in copies:
+        copy.wait()
     lane = lax.broadcasted_iota(jnp.int32, (1, points), 1)
     for t in range(tiles):
-        payload[3, t : t + 1, :] = jnp.where(lane < tile_count[t], strain[t : t + 1, :], 0.0)
+        payload[3, t : t + 1, :] = jnp.where(lane < tile_count[t], strain_here[t : t + 1, :], 0.0)
 
     def sent(h, carry):
         t = send_tile[h]
@@ -127,34 +156,42 @@
         outbox[h, 7:8, :] = payload[3, pl.ds(t, 1), :] * live
         return carry
 
-    lax.fori_loop(0, peers, sent, 0)
-    lax.fori_loop(0, peers, listed, 0)
-
-
-def own_kernel(payload, local_pairs, b_ref, num_ref, den_ref, rows_ref, a_ref, s_ref):
+    lax.fori_loop(0, peers, sent, 0, unroll=peers <= 8)
+    lax.fori_loop(0, peers, listed, 0, unroll=peers <= 8)
+
+
+def own_kernel(payload, local_pairs_in, b_ref, num_ref, den_ref, rows_ref, a_ref, s_ref, local_pairs, sems):
     tiles = payload.shape[1]
+    copies = fetch((local_pairs_in,), (local_pairs,), sems)
     planes = [payload[k] for k in range(4)]
     build_source(planes, rows_ref, a_ref, s_ref, 0)
     build_target(planes, rows_ref, b_ref)
-
-    def own(t, carry):
-        num, den = pair_sums(a_ref[t], s_ref[t], b_ref[t])
-        num_ref[t] = num
-        den_ref[t] = den
-        return carry
-
-    lax.fori_loop(0, tiles, own, 0)
-
-    def listed(i, carry):
-        one = local_pairs[0, i]
-        two = local_pairs[1, i]
-        for src, dst in ((one, two), (two, one)):
-            num, den = pair_sums(a_ref[src], s_ref[src], b_ref[dst])
+    for copy in copies:
+        copy.wait()
+
+    def own(step, carry):
+        group = [step * 4 + i for i in range(4)]
+        sums = [pair_sums(a_ref[t], s_ref[t], b_ref[t]) for t in group]
+        for t, (num, den) in zip(group, sums):
+            num_ref[t] = num
+            den_ref[t] = den
+        return carry
+
+    lax.fori_loop(0, tiles // 4, own, 0)
+
+    def listed(step, carry):
+        group = []
+        for i in range(2):
+            one = local_pairs[0, step * 2 + i]
+            two = local_pairs[1, step * 2 + i]
+            group += [(one, two), (two, one)]
+        sums = [pair_sums(a_ref[src], s_ref[src], b_ref[dst]) for src, dst in group]
+        for (src, dst), (num, den) in zip(group, sums):
             num_ref[dst] = num_ref[dst] + num
             den_ref[dst] = den_ref[dst] + den
         return carry
 
-    lax.fori_loop(0, local_pairs.shape[1], listed, 0)
+    lax.fori_loop(0, local_pairs.shape[1] // 2, listed, 0)
 
 
 def rest_kernel(
@@ -166,13 +203,14 @@
     num_in,
     den_in,
     payload,
-    history,
-    corner_load,
-    tile_sub,
-    corner_map,
-    send_tile,
-    remote_pairs,
-    remote_count,
+    history_in,
+    corner_load_in,
+    external_in,
+    tile_sub_in,
+    corner_map_in,
+    send_tile_in,
+    remote_pairs_in,
+    remote_count_in,
     damage_ref,
     parts_ref,
     rows_ref,
@@ -185,25 +223,49 @@
     den_ref,
     sub_rows,
     map_rows,
+    history,
+    corner_load,
+    external,
+    tile_sub,
+    corner_map,
+    send_tile,
+    remote_pairs,
+    remote_count,
+    sems,
 ):
+    copies = fetch(
+        (
+            history_in,
+            corner_load_in,
+            external_in,
+            tile_sub_in,
+            corner_map_in,
+            send_tile_in,
+            remote_pairs_in,
+            remote_count_in,
+        ),
+        (history, corner_load, external, tile_sub, corner_map, send_tile, remote_pairs, remote_count),
+        sems,
+    )
     tiles, points = history.shape
     num_ref[...] = num_in[...]
     den_ref[...] = den_in[...]
 
     def border(offset):
-        def one(t, carry):
-            num = num_ref[t]
-            den = den_ref[t]
-            other = lax.rem(t + offset, tiles)
-            for src in (t, other):
-                more_num, more_den = pair_sums(a_ref[src], s_ref[src], b_ref[t])
-                num = num + more_num
-                den = den + more_den
-            num_ref[t] = num
-            den_ref[t] = den
+        def some(step, carry):
+            for t in (2 * step, 2 * step + 1):
+                num = num_ref[t]
+                den = den_ref[t]
+                other = lax.rem(t + offset, tiles)
+                for src in (t, other):
+                    more_num, more_den = pair_sums(a_ref[src], s_ref[src], b_ref[t])
+                    num = num + more_num
+                    den = den + more_den
+                num_ref[t] = num
+                den_ref[t] = den
             return carry
 
-        lax.fori_loop(0, tiles, one, 0)
+        lax.fori_loop(0, tiles // 2, some, 0)
 
     build_source([below[k] for k in range(4)], rows_ref, a_ref, s_ref, 0)
     border(1)
@@ -219,21 +281,23 @@
         ]
         build_source(planes, far_rows, far_a, far_s, which * peers)
 
-    def add_far(src, dst):
-        num, den = pair_sums(far_a[src], far_s[src], b_ref[dst])
-        num_ref[dst] = num_ref[dst] + num
-        den_ref[dst] = den_ref[dst] + den
-
-    def listed(i, carry):
-        add_far(remote_pairs[1, i], remote_pairs[0, i])
-        return carry
-
-    def named(h, carry):
-        add_far(peers + h, send_tile[h])
-        return carry
-
-    lax.fori_loop(0, remote_count[0], listed, 0)
-    lax.fori_loop(0, peers, named, 0)
+    for copy in copies:
+        copy.wait()
+
+    def far(step, carry):
+        group = []
+        for i in (2 * step, 2 * step + 1):
+            live = (i < remote_count[0]).astype(f32)
+            group += [(remote_pairs[1, i], remote_pairs[0, i], live), (peers + i, send_tile[i], None)]
+        sums = [pair_sums(far_a[src], far_s[src], b_ref[dst]) for src, dst, live in group]
+        for (src, dst, live), (num, den) in zip(group, sums):
+            if live is not None:
+                num, den = num * live, den * live
+            num_ref[dst] = num_ref[dst] + num
+            den_ref[dst] = den_ref[dst] + den
+        return carry
+
+    lax.fori_loop(0, peers // 2, far, 0)
 
     valid = (payload[3] > 0.0).astype(f32)
     num = jnp.sum(num_ref[...], axis=1) * valid
@@ -265,7 +329,9 @@
     target = map_rows[...] - lax.broadcasted_iota(jnp.int32, (subs * corners, 128), 1)
 
     def scatter(j, carry):
-        parts_ref[pl.ds(j, 1), :] = jnp.sum(jnp.where(target == j * 128, sub_part, 0.0), axis=0, keepdims=True)
+        held = jnp.where(j == lax.axis_index("blk"), external[...], 0.0).reshape(1, 128)
+        force = jnp.sum(jnp.where(target == j * 128, sub_part, 0.0), axis=0, keepdims=True)
+        parts_ref[pl.ds(j, 1), :] = held - force
         return carry
 
     lax.fori_loop(0, peers, scatter, 0, unroll=peers <= 8)
@@ -299,8 +365,11 @@
             jax.ShapeDtypeStruct((4, tiles, points), f32),
             jax.ShapeDtypeStruct((peers, 8, points), f32),
         ),
-        in_specs=[in_vmem] * 2 + [in_smem] * 4,
+        in_specs=[anywhere] * 6,
         out_specs=(in_vmem, in_vmem),
+        scratch_shapes=[pltpu.VMEM((tiles, points), f32)]
+        + [pltpu.SMEM(v.shape, jnp.int32) for v in (tile_count, send_tile, remote_pairs, remote_count)]
+        + [pltpu.SemaphoreType.DMA((6,))],
         compiler_params=params,
         name="pack",
     )(coords, strain, tile_count, send_tile, remote_pairs, remote_count)
@@ -318,12 +387,14 @@
             jax.ShapeDtypeStruct((tiles, 8, points), f32),
             jax.ShapeDtypeStruct((tiles, 8, points), f32),
         ),
-        in_specs=[in_vmem, in_smem],
+        in_specs=[in_vmem, anywhere],
         out_specs=(in_vmem,) * 3,
         scratch_shapes=[
             pltpu.VMEM((halves, tiles * depth, 128), f32),
             pltpu.VMEM((tiles, points, depth), bf16),
             pltpu.VMEM((tiles, points, 128), f32),
+            pltpu.SMEM(local_pairs.shape, jnp.int32),
+            pltpu.SemaphoreType.DMA((1,)),
         ],
         compiler_params=params,
         cost_estimate=pl.CostEstimate(
@@ -339,7 +410,7 @@
             jax.ShapeDtypeStruct((tiles, points), f32),
             jax.ShapeDtypeStruct((peers, 128), f32),
         ),
-        in_specs=[in_vmem] * 9 + [in_smem] * 5,
+        in_specs=[in_vmem] * 7 + [anywhere] * 8,
         out_specs=(in_vmem,) * 2,
         scratch_shapes=[
             pltpu.VMEM((halves, tiles * depth, 128), f32),
@@ -352,7 +423,12 @@
             pltpu.VMEM((tiles, 8, points), f32),
             pltpu.VMEM((tiles, 128), jnp.int32),
             pltpu.VMEM((subs * corners, 128), jnp.int32),
-        ],
+            pltpu.VMEM(history.shape, f32),
+            pltpu.VMEM(corner_load.shape, f32),
+            pltpu.VMEM(external.shape, f32),
+        ]
+        + [pltpu.SMEM(v.shape, jnp.int32) for v in (tile_sub, corner_map, send_tile, remote_pairs, remote_count)]
+        + [pltpu.SemaphoreType.DMA((8,))],
         compiler_params=params,
         cost_estimate=pl.CostEstimate(
             flops=4 * tiles * block * depth, bytes_accessed=1 << 21, transcendentals=4 * tiles * points * points
@@ -368,6 +444,7 @@
         payload,
         history,
         corner_load,
+        external,
         tile_sub,
         corner_map,
         send_tile,
@@ -375,7 +452,7 @@
         remote_count,
     )
     gathered = lax.all_to_all(parts, "blk", split_axis=0, concat_axis=0, tiled=True)
-    return damage, external - jnp.sum(gathered, axis=0)
+    return damage, jnp.sum(gathered, axis=0)
 
 
 def solution(mesh):

time: 81.2 us -> 69 us (0.85)
  Pallas kernels: 55.7 us -> 43.8 us
    pallas_call x1, Pallas kernels: 20.7 us -> 14.4 us  [per_device(): pl.pallas_call(own_kernel, out_shape=(jax.ShapeDtypeStruct((tiles, depth,...]
    pallas_call x1, Pallas kernels: 33.6 us -> 27.9 us  [per_device(): pl.pallas_call(functools.partial(rest_kernel, peers), out_shape=(jax.Shap...]
  transfers between devices with their start and end apart: 3 -> 3, of which waited for: 0 -> 0; matrix products, arithmetic and copies ran while one was open for 0% -> 0% of each run, Pallas kernels for 26% -> 21%
where the time goes in v2:
time: 69 us; the launch traced here: 68.6 us
  Pallas kernels  43.8 us (63%)
  starting transfers between devices  11 us (16%)
  blocking collectives  8.64 us (13%)
  local copies, waits for them, and re-layouts  3.05 us (4%)
  between operations  1.49 us (2%)
    pallas_call x1, Pallas kernels, per_device(): pl.pallas_call(functools.partial(rest_kernel, peers), out_shape=(jax.Shap...  27.9 us
    pallas_call x1, Pallas kernels, per_device(): pl.pallas_call(own_kernel, out_shape=(jax.ShapeDtypeStruct((tiles, depth,...  14.4 us
    all_to_all x1, blocking collectives, per_device(): lax.all_to_all(parts, 'blk', split_axis=0, concat_axis=0, tiled=True)  8.64 us
    ppermute x1, starting transfers between devices, per_device(): below = lax.ppermute(payload, 'sub', up)  5.56 us
    all_to_all x1, starting transfers between devices, per_device(): lax.all_to_all(outbox, 'blk', split_axis=0, concat_axis=0, tiled=True)  4.17 us
    unnamed x24, local copies, waits for them, and re-layouts  3 us
    pallas_call x1, Pallas kernels, per_device(): pl.pallas_call(functools.partial(pack_kernel, peers), out_shape=(jax.Shap...  1.48 us
  transfers between devices with their start and end apart: 3, of which 0 were waited for; matrix products, arithmetic and copies ran while one was open for 0% of the time, Pallas kernels for 21%

profile of v2, /device:TPU:0, one launch (start us, length us, event | category | flops | bytes accessed | tf_op | source)
XLA Modules:
  0.0 68.6 jit_solution(10638471521534350182)
XLA Ops:
  1.3 0.9 %copy-done = f32[3,32,256]{2,1,0:T(8,128)S(1)} copy-done((f32[3,32,256]{2,1,0:T(8,128)S(1)}, f32[3,32,256]{2,1,0:T(8,128)}, u32[]{:S(2)}) %copy-start) | copy-done | bytes 98328
  2.2 0.8 %copy-done.1 = f32[32,256]{1,0:T(8,128)S(1)} copy-done((f32[32,256]{1,0:T(8,128)S(1)}, f32[32,256]{1,0:T(8,128)}, u32[]{:S(2)}) %copy-start.1) | copy-done | bytes 32792
  3.0 0.7 copy-done.4
  3.6 1.5 %pack.1 = (f32[4,32,256]{2,1,0:T(8,128)S(1)}, f32[8,8,256]{2,1,0:T(8,128)}) custom-call(f32[3,32,256]{2,1,0:T(8,128)S(1)} %copy-done, f32[32,256]{1,0:T(8,128)S(1)} %copy-done.1, s32[32]{0:T(128)S(1)} %copy-done.3, s32[8]{0:T(128)S(1)} %copy-done.4, s32[2,8]{1,0:T(2,128)S(1)} %copy-done.2, s32[1]{0:T(128)S(6)} %copy.19.remote_count_in), custom_call_target="tpu_custom_call" | custom-call | tf_op jit(solution)/shard_map/pack/pallas_call | solution.py:362
  5.1 1.3 %collective-permute-start.1 = (f32[4,32,256]{2,1,0:T(8,128)S(1)}, f32[4,32,256]{2,1,0:T(8,128)S(1)}, u32[]{:S(2)}, u32[]{:S(2)}) collective-permute-start(f32[4,32,256]{2,1,0:T(8,128)S(1)} %get-tuple-element.9.payload), channel_id=1, source_target_pairs={{8,0},{16,8},{24,16},{9,1},{17,9},{25,17},{10,2},{18,10},{26,18},{... | collective-permute-start | bytes 393224 | tf_op jit(solution)/shard_map/ppermute | solution.py:380
  6.4 5.6 %collective-permute-start = (f32[4,32,256]{2,1,0:T(8,128)S(1)}, f32[4,32,256]{2,1,0:T(8,128)S(1)}, u32[]{:S(2)}, u32[]{:S(2)}) collective-permute-start(f32[4,32,256]{2,1,0:T(8,128)S(1)} %get-tuple-element.9.payload), channel_id=1, source_target_pairs={{0,8},{8,16},{16,24},{1,9},{9,17},{17,25},{2,10},{10,18},{18,26},{... | collective-permute-start | bytes 393224 | tf_op jit(solution)/shard_map/ppermute | solution.py:379
  12.0 0.0 copy-start.9
  12.0 4.2 %all-to-all-start = ((f32[8,8,256]{2,1,0:T(8,128)}), f32[8,8,256]{2,1,0:T(8,128)S(1)}, u32[]{:S(2)}, u32[]{:S(2)}) async-start(f32[8,8,256]{2,1,0:T(8,128)} %get-tuple-element.10), calls=%async_computation | async-start | bytes 131072 | tf_op jit(solution)/shard_map/all_to_all | solution.py:381
  16.2 0.0 copy-done.9
  16.2 0.0 copy-start.6
  16.2 14.4 %own.1 = (bf16[32,32,256]{2,1,0:T(8,128)(2,1)S(1)}, f32[32,8,256]{2,1,0:T(8,128)S(1)}, f32[32,8,256]{2,1,0:T(8,128)S(1)}) custom-call(f32[4,32,256]{2,1,0:T(8,128)S(1)} %get-tuple-element.9.payload, s32[2,32]{1,0:T(2,128)S(1)} %copy-done.9), custom_call_target="tpu_custom_call" | custom-call | flops 402653184 | bytes 1048576 | tf_op jit(solution)/shard_map/own/pallas_call | solution.py:383
  30.7 0.0 all-to-all-done
  30.7 0.0 copy-start.7
  30.7 0.0 collective-permute-done.1.above
  30.7 0.0 collective-permute-done.below
  30.8 0.0 copy-start.8
  30.8 0.0 copy-start.5
  30.8 0.0 copy-start.10
  30.8 0.0 copy-start.11
  30.8 0.7 copy-done.7
  31.5 0.0 copy-done.11
  31.5 27.9 %rest.1 = (f32[32,256]{1,0:T(8,128)}, f32[8,128]{1,0:T(8,128)S(1)}) custom-call(f32[4,32,256]{2,1,0:T(8,128)S(1)} %collective-permute-done.below, f32[4,32,256]{2,1,0:T(8,128)S(1)} %collective-permute-done.1.above, f32[2,64,128]{2,1,0:T(8,128)S(1)} %bitcast.6, bf16[32,32,256]{2,1,0:T(8,128)(2,1)S(1)} %get-tuple-element.11.b_ref, ...), custom_call_target="tpu_custom_call" | custom-call | flops 536870912 | bytes 2097152 | tf_op jit(solution)/shard_map/rest/pallas_call | solution.py:407
  59.4 8.6 %all_to_all.14 = f32[8,1,128]{2,1,0:T(1,128)S(1)} all-to-all(f32[8,1,128]{2,1,0:T(1,128)S(1)} %bitcast.7), channel_id=1, replica_groups=mesh['sub'=4,'blk'=8] {'blk'}, dimensions={0} | all-to-all | bytes 8192 | tf_op jit(solution)/shard_map/all_to_all | solution.py:454
  68.0 0.5 reduce_sum.9
  (13 shorter events, 0.1 us)
Async XLA Ops:
  0.6 0.7 %copy-start.2 = (s32[2,8]{1,0:T(2,128)S(1)}, s32[2,8]{1,0:T(2,128)}, u32[]{:S(2)}) copy-start(s32[2,8]{1,0:T(2,128)} %remote_pairs_in.3) | copy-start | bytes 196
  0.6 0.7 %copy-start.3 = (s32[32]{0:T(128)S(1)}, s32[32]{0:T(128)}, u32[]{:S(2)}) copy-start(s32[32]{0:T(128)} %tile_count_in.1) | copy-start | bytes 388
  1.3 0.9 %copy-start = (f32[3,32,256]{2,1,0:T(8,128)S(1)}, f32[3,32,256]{2,1,0:T(8,128)}, u32[]{:S(2)}) copy-start(f32[3,32,256]{2,1,0:T(8,128)} %coords.1) | copy-start | bytes 294916
  2.2 0.8 %copy-start.1 = (f32[32,256]{1,0:T(8,128)S(1)}, f32[32,256]{1,0:T(8,128)}, u32[]{:S(2)}) copy-start(f32[32,256]{1,0:T(8,128)} %strain.1) | copy-start | bytes 98308
  3.0 0.7 copy-start.4
  5.1 25.6 %collective-permute-start.1 = (f32[4,32,256]{2,1,0:T(8,128)S(1)}, f32[4,32,256]{2,1,0:T(8,128)S(1)}, u32[]{:S(2)}, u32[]{:S(2)}) collective-permute-start(f32[4,32,256]{2,1,0:T(8,128)S(1)} %get-tuple-element.9.payload), channel_id=1, source_target_pairs={{8,0},{16,8},{24,16},{9,1},{17,9},{25,17},{10,2},{18,10},{26,18},{... | collective-permute-start | bytes 393224 | tf_op jit(solution)/shard_map/ppermute | solution.py:380
  6.4 24.3 %collective-permute-start = (f32[4,32,256]{2,1,0:T(8,128)S(1)}, f32[4,32,256]{2,1,0:T(8,128)S(1)}, u32[]{:S(2)}, u32[]{:S(2)}) collective-permute-start(f32[4,32,256]{2,1,0:T(8,128)S(1)} %get-tuple-element.9.payload), channel_id=1, source_target_pairs={{0,8},{8,16},{16,24},{1,9},{9,17},{17,25},{2,10},{10,18},{18,26},{... | collective-permute-start | bytes 393224 | tf_op jit(solution)/shard_map/ppermute | solution.py:379
  12.0 4.2 %copy-start.9 = (s32[2,32]{1,0:T(2,128)S(1)}, s32[2,32]{1,0:T(2,128)}, u32[]{:S(2)}) copy-start(s32[2,32]{1,0:T(2,128)} %local_pairs_in.1) | copy-start | bytes 772
  12.0 18.6 %all-to-all-start = ((f32[8,8,256]{2,1,0:T(8,128)}), f32[8,8,256]{2,1,0:T(8,128)S(1)}, u32[]{:S(2)}, u32[]{:S(2)}) async-start(f32[8,8,256]{2,1,0:T(8,128)} %get-tuple-element.10), calls=%async_computation | async-start | bytes 131072 | tf_op jit(solution)/shard_map/all_to_all | solution.py:381
  16.2 14.6 %copy-start.6 = (f32[24,32,256]{2,1,0:T(8,128)S(1)}, f32[24,32,256]{2,1,0:T(8,128)}, u32[]{:S(2)}) copy-start(f32[24,32,256]{2,1,0:T(8,128)} %corner_load_in.1) | copy-start | bytes 2359300
  30.7 0.8 %copy-start.7 = (f32[32,256]{1,0:T(8,128)S(1)}, f32[32,256]{1,0:T(8,128)}, u32[]{:S(2)}) copy-start(f32[32,256]{1,0:T(8,128)} %history_in.1) | copy-start | bytes 98308
  30.8 0.7 %copy-start.8 = (s32[4,24]{1,0:T(4,128)S(1)}, s32[4,24]{1,0:T(4,128)}, u32[]{:S(2)}) copy-start(s32[4,24]{1,0:T(4,128)} %corner_map_in.1) | copy-start | bytes 1156
  30.8 0.7 %copy-start.5 = (s32[8]{0:T(128)S(1)}, s32[8]{0:T(128)}, u32[]{:S(2)}) copy-start(s32[8]{0:T(128)} %send_tile_in.3) | copy-start | bytes 100
  30.8 0.7 %copy-start.10 = (f32[128]{0:T(128)S(1)}, f32[128]{0:T(128)}, u32[]{:S(2)}) copy-start(f32[128]{0:T(128)} %external_in.1) | copy-start | bytes 1540
  30.8 0.7 %copy-start.11 = (s32[32]{0:T(128)S(1)}, s32[32]{0:T(128)}, u32[]{:S(2)}) copy-start(s32[32]{0:T(128)} %tile_sub_in.1) | copy-start | bytes 388

commit v3 on v2

--- a/solution.py
+++ b/solution.py
@@ -14,12 +14,12 @@
 coord_scale = math.sqrt(gauss_rate * math.log2(math.e))
 far_off = 2048.0
 depth = 32
-grant = 48 * 1024 * 1024
+grant = 60 * 1024 * 1024
 
 f32 = jnp.float32
 bf16 = jnp.bfloat16
 in_vmem = pl.BlockSpec(memory_space=pltpu.VMEM)
-anywhere = pl.BlockSpec(memory_space=pl.ANY)
+in_hbm = pl.BlockSpec(memory_space=pltpu.HBM)
 
 
 def pieces(value):
@@ -57,15 +57,16 @@
     put_rows(rows_ref, tiles, rows)
     halves = norm.shape[1] // 128
 
-    def one_tile(t, carry):
-        for half in range(halves):
-            block = rows_ref[half, pl.ds(pl.multiple_of(t * depth, depth), depth), :]
-            turned = block.T
-            a_ref[base + t, half * 128 : (half + 1) * 128, :] = turned.astype(bf16)
-            s_ref[base + t, half * 128 : (half + 1) * 128, :] = jnp.broadcast_to(turned[:, 24:25], (128, 128))
-        return carry
-
-    lax.fori_loop(0, tiles, one_tile, 0)
+    def some_tiles(step, carry):
+        for t in [step * 4 + i for i in range(4)]:
+            for half in range(halves):
+                block = rows_ref[half, pl.ds(pl.multiple_of(t * depth, depth), depth), :]
+                turned = block.T
+                a_ref[base + t, half * 128 : (half + 1) * 128, :] = turned.astype(bf16)
+                s_ref[base + t, half * 128 : (half + 1) * 128, :] = jnp.broadcast_to(turned[:, 24:25], (128, 128))
+        return carry
+
+    lax.fori_loop(0, tiles // 4, some_tiles, 0)
 
 
 def build_target(planes, rows_ref, b_ref):
@@ -81,13 +82,14 @@
     put_rows(rows_ref, tiles, rows)
     halves = norm.shape[1] // 128
 
-    def one_tile(t, carry):
-        for half in range(halves):
-            block = rows_ref[half, pl.ds(pl.multiple_of(t * depth, depth), depth), :]
-            b_ref[t, :, half * 128 : (half + 1) * 128] = block.astype(bf16)
-        return carry
-
-    lax.fori_loop(0, tiles, one_tile, 0)
+    def some_tiles(step, carry):
+        for t in [step * 4 + i for i in range(4)]:
+            for half in range(halves):
+                block = rows_ref[half, pl.ds(pl.multiple_of(t * depth, depth), depth), :]
+                b_ref[t, :, half * 128 : (half + 1) * 128] = block.astype(bf16)
+        return carry
+
+    lax.fori_loop(0, tiles // 4, some_tiles, 0)
 
 
 def pair_sums(a, s, b):
@@ -144,7 +146,7 @@
     def sent(h, carry):
         t = send_tile[h]
         for k in range(4):
-            outbox[h, k : k + 1, :] = payload[k, pl.ds(t, 1), :]
+            outbox[pl.ds(8 * h + k, 1), :] = payload[k, pl.ds(t, 1), :]
         return carry
 
     def listed(i, carry):
@@ -152,8 +154,8 @@
         h = remote_pairs[1, i]
         live = (i < remote_count[0]).astype(f32)
         for k in range(3):
-            outbox[h, 4 + k : 5 + k, :] = payload[k, pl.ds(t, 1), :]
-        outbox[h, 7:8, :] = payload[3, pl.ds(t, 1), :] * live
+            outbox[pl.ds(8 * h + 4 + k, 1), :] = payload[k, pl.ds(t, 1), :]
+        outbox[pl.ds(8 * h + 7, 1), :] = payload[3, pl.ds(t, 1), :] * live
         return carry
 
     lax.fori_loop(0, peers, sent, 0, unroll=peers <= 8)
@@ -196,13 +198,12 @@
 
 def rest_kernel(
     peers,
-    below,
-    above,
-    inbox,
-    b_ref,
+    layers_in,
+    inbox_in,
+    b_in,
     num_in,
     den_in,
-    payload,
+    payload_in,
     history_in,
     corner_load_in,
     external_in,
@@ -219,10 +220,15 @@
     far_rows,
     far_a,
     far_s,
+    sub_rows,
+    map_rows,
+    below,
+    above,
+    inbox,
+    b_ref,
     num_ref,
     den_ref,
-    sub_rows,
-    map_rows,
+    own_strain,
     history,
     corner_load,
     external,
@@ -231,10 +237,24 @@
     send_tile,
     remote_pairs,
     remote_count,
+    layer_sems,
+    sum_sems,
     sems,
 ):
+    tiles, points = history.shape
+    count = layers_in.shape[0]
+    layer = lax.axis_index("sub")
+    from_below, from_above = fetch(
+        (layers_in.at[jnp.maximum(layer - 1, 0)], layers_in.at[jnp.minimum(layer + 1, count - 1)]),
+        (below, above),
+        layer_sems,
+    )
+    sum_copies = fetch((b_in, num_in, den_in), (b_ref, num_ref, den_ref), sum_sems)
+    halves = points // 128
     copies = fetch(
-        (
+        [inbox_in.at[:, half * 128 : (half + 1) * 128] for half in range(halves)]
+        + [
+            payload_in.at[3],
             history_in,
             corner_load_in,
             external_in,
@@ -243,13 +263,11 @@
             send_tile_in,
             remote_pairs_in,
             remote_count_in,
-        ),
-        (history, corner_load, external, tile_sub, corner_map, send_tile, remote_pairs, remote_count),
+        ],
+        [inbox.at[half] for half in range(halves)]
+        + [own_strain, history, corner_load, external, tile_sub, corner_map, send_tile, remote_pairs, remote_count],
         sems,
     )
-    tiles, points = history.shape
-    num_ref[...] = num_in[...]
-    den_ref[...] = den_in[...]
 
     def border(offset):
         def some(step, carry):
@@ -267,11 +285,24 @@
 
         lax.fori_loop(0, tiles // 2, some, 0)
 
+    from_below.wait()
     build_source([below[k] for k in range(4)], rows_ref, a_ref, s_ref, 0)
-    border(1)
-    build_source([above[k] for k in range(4)], rows_ref, a_ref, s_ref, 0)
-    border(tiles - 1)
-
+    for copy in sum_copies:
+        copy.wait()
+
+    @pl.when(layer > 0)
+    def lower():
+        border(1)
+
+    from_above.wait()
+
+    @pl.when(layer < count - 1)
+    def upper():
+        build_source([above[k] for k in range(4)], rows_ref, a_ref, s_ref, 0)
+        border(tiles - 1)
+
+    for copy in copies:
+        copy.wait()
     for which in range(2):
         planes = [
             jnp.concatenate(
@@ -280,9 +311,6 @@
             for k in range(4)
         ]
         build_source(planes, far_rows, far_a, far_s, which * peers)
-
-    for copy in copies:
-        copy.wait()
 
     def far(step, carry):
         group = []
@@ -299,7 +327,7 @@
 
     lax.fori_loop(0, peers // 2, far, 0)
 
-    valid = (payload[3] > 0.0).astype(f32)
+    valid = (own_strain[...] > 0.0).astype(f32)
     num = jnp.sum(num_ref[...], axis=1) * valid
     den = jnp.sum(den_ref[...], axis=1) * valid
     strain_bar = num / (den + 1.0 - valid)
@@ -354,7 +382,6 @@
     tiles, points = strain.shape
     halves = points // 128
     peers = lax.axis_size("blk")
-    layers = lax.axis_size("sub")
     subs, corners = corner_map.shape
     params = pltpu.CompilerParams(vmem_limit_bytes=grant)
     block = 2 * points * points
@@ -363,9 +390,9 @@
         functools.partial(pack_kernel, peers),
         out_shape=(
             jax.ShapeDtypeStruct((4, tiles, points), f32),
-            jax.ShapeDtypeStruct((peers, 8, points), f32),
+            jax.ShapeDtypeStruct((peers * 8, points), f32),
         ),
-        in_specs=[anywhere] * 6,
+        in_specs=[in_hbm] * 6,
         out_specs=(in_vmem, in_vmem),
         scratch_shapes=[pltpu.VMEM((tiles, points), f32)]
         + [pltpu.SMEM(v.shape, jnp.int32) for v in (tile_count, send_tile, remote_pairs, remote_count)]
@@ -374,10 +401,7 @@
         name="pack",
     )(coords, strain, tile_count, send_tile, remote_pairs, remote_count)
 
-    up = [(i, i + 1) for i in range(layers - 1)]
-    down = [(i + 1, i) for i in range(layers - 1)]
-    below = lax.ppermute(payload, "sub", up)
-    above = lax.ppermute(payload, "sub", down)
+    layers = lax.all_gather(payload, "sub")
     inbox = lax.all_to_all(outbox, "blk", split_axis=0, concat_axis=0, tiled=True)
 
     b_own, num, den = pl.pallas_call(
@@ -387,7 +411,7 @@
             jax.ShapeDtypeStruct((tiles, 8, points), f32),
             jax.ShapeDtypeStruct((tiles, 8, points), f32),
         ),
-        in_specs=[in_vmem, anywhere],
+        in_specs=[in_vmem, in_hbm],
         out_specs=(in_vmem,) * 3,
         scratch_shapes=[
             pltpu.VMEM((halves, tiles * depth, 128), f32),
@@ -403,14 +427,13 @@
         name="own",
     )(payload, local_pairs)
 
-    inbox = inbox.reshape(peers * 8, halves, 128).transpose(1, 0, 2)
     damage, parts = pl.pallas_call(
         functools.partial(rest_kernel, peers),
         out_shape=(
             jax.ShapeDtypeStruct((tiles, points), f32),
             jax.ShapeDtypeStruct((peers, 128), f32),
         ),
-        in_specs=[in_vmem] * 7 + [anywhere] * 8,
+        in_specs=[in_hbm] * 14,
         out_specs=(in_vmem,) * 2,
         scratch_shapes=[
             pltpu.VMEM((halves, tiles * depth, 128), f32),
@@ -419,24 +442,28 @@
             pltpu.VMEM((halves, peers * depth, 128), f32),
             pltpu.VMEM((2 * peers, points, depth), bf16),
             pltpu.VMEM((2 * peers, points, 128), f32),
-            pltpu.VMEM((tiles, 8, points), f32),
-            pltpu.VMEM((tiles, 8, points), f32),
             pltpu.VMEM((tiles, 128), jnp.int32),
             pltpu.VMEM((subs * corners, 128), jnp.int32),
+            pltpu.VMEM(payload.shape, f32),
+            pltpu.VMEM(payload.shape, f32),
+            pltpu.VMEM((halves, peers * 8, 128), f32),
+            pltpu.VMEM(b_own.shape, bf16),
+            pltpu.VMEM(num.shape, f32),
+            pltpu.VMEM(den.shape, f32),
+            pltpu.VMEM(strain.shape, f32),
             pltpu.VMEM(history.shape, f32),
             pltpu.VMEM(corner_load.shape, f32),
             pltpu.VMEM(external.shape, f32),
         ]
         + [pltpu.SMEM(v.shape, jnp.int32) for v in (tile_sub, corner_map, send_tile, remote_pairs, remote_count)]
-        + [pltpu.SemaphoreType.DMA((8,))],
+        + [pltpu.SemaphoreType.DMA((n,)) for n in (2, 3, 9 + halves)],
         compiler_params=params,
         cost_estimate=pl.CostEstimate(
             flops=4 * tiles * block * depth, bytes_accessed=1 << 21, transcendentals=4 * tiles * points * points
         ),
         name="rest",
     )(
-        below,
-        above,
+        layers,
         inbox,
         b_own,
         num,

time: 69 us -> 70.8 us (1.026)
  the two profiles are of different devices: /device:TPU:0 before, /device:TPU:8 now
where the time goes in v3:
time: 70.8 us; the launch traced here: 70.5 us
  Pallas kernels  38.1 us (54%)
  blocking collectives  26 us (37%)
  starting transfers between devices  3.87 us (5%)
  between operations  1.33 us (2%)
    pallas_call x1, Pallas kernels, per_device(): pl.pallas_call(functools.partial(rest_kernel, peers), out_shape=(jax.Shap...  22.9 us
    all_gather x1, blocking collectives, per_device(): layers = lax.all_gather(payload, 'sub')  17.2 us
    pallas_call x1, Pallas kernels, per_device(): pl.pallas_call(own_kernel, out_shape=(jax.ShapeDtypeStruct((tiles, depth,...  13.4 us
    all_to_all x1, blocking collectives, per_device(): lax.all_to_all(parts, 'blk', split_axis=0, concat_axis=0, tiled=True)  8.82 us
    all_to_all x1, starting transfers between devices, per_device(): lax.all_to_all(outbox, 'blk', split_axis=0, concat_axis=0, tiled=True)  3.87 us
    pallas_call x1, Pallas kernels, per_device(): pl.pallas_call(functools.partial(pack_kernel, peers), out_shape=(jax.Shap...  1.8 us
  transfers between devices with their start and end apart: 1, of which 0 were waited for; matrix products, arithmetic and copies ran while one was open for 0% of the time, Pallas kernels for 19%

profile of v3, /device:TPU:8, one launch (start us, length us, event | category | flops | bytes accessed | tf_op | source)
XLA Modules:
  0.0 70.5 jit_solution(1094448459441750376)
XLA Ops:
  1.3 1.8 %pack.1 = (f32[4,32,256]{2,1,0:T(8,128)}, f32[64,256]{1,0:T(8,128)}) custom-call(f32[3,32,256]{2,1,0:T(8,128)} %coords.1, f32[32,256]{1,0:T(8,128)} %strain.1, s32[32]{0:T(128)} %tile_count_in.1, s32[8]{0:T(128)} %send_tile_in.3, s32[2,8]{1,0:T(2,128)} %remote_pairs_in.3, s32[1]{0:T(128)S(6)} %copy.15.remote_count_in), custom_call_target="tpu_custom_call" | custom-call | tf_op jit(solution)/shard_map/pack/pallas_call | solution.py:389
  3.1 0.0 copy-start
  3.1 3.9 %all-to-all-start = ((f32[8,8,256]{2,1,0:T(8,128)}), f32[8,8,256]{2,1,0:T(8,128)S(1)}, u32[]{:S(2)}, u32[]{:S(2)}) async-start(f32[8,8,256]{2,1,0:T(8,128)} %bitcast.8), calls=%async_computation | async-start | bytes 131072 | tf_op jit(solution)/shard_map/all_to_all | solution.py:405
  7.0 0.0 copy-done
  7.0 17.2 %all-gather = f32[16,32,256]{2,1,0:T(8,128)} all-gather(f32[4,32,256]{2,1,0:T(8,128)S(1)} %copy-done), channel_id=2, replica_groups=mesh['sub'=4,'blk'=8] {'sub'}, dimensions={0}, use_global_device_ids=true | all-gather | bytes 655360 | tf_op jit(solution)/shard_map/all_gather | solution.py:404
  24.2 13.4 %own.1 = (bf16[32,32,256]{2,1,0:T(8,128)(2,1)}, f32[32,8,256]{2,1,0:T(8,128)}, f32[32,8,256]{2,1,0:T(8,128)}) custom-call(f32[4,32,256]{2,1,0:T(8,128)} %get-tuple-element.9.payload.payload_in, s32[2,32]{1,0:T(2,128)} %local_pairs_in.1), custom_call_target="tpu_custom_call" | custom-call | flops 402653184 | bytes 1048576 | tf_op jit(solution)/shard_map/own/pallas_call | solution.py:407
  37.6 0.0 all-to-all-done
  37.6 0.0 copy-start.1
  37.6 0.6 copy-done.1
  38.2 22.9 %rest.1 = (f32[32,256]{1,0:T(8,128)}, f32[8,128]{1,0:T(8,128)}) custom-call(f32[4,4,32,256]{3,2,1,0:T(8,128)} %bitcast.6, f32[64,256]{1,0:T(8,128)} %bitcast.7, bf16[32,32,256]{2,1,0:T(8,128)(2,1)} %get-tuple-element.11.b_in, f32[32,8,256]{2,1,0:T(8,128)} %get-tuple-element.12.num_in, f32[32,8,256]{2,1,0:T(8,128)} %get-tuple-element.13.den_in, ...), custom_call_target="tpu_custom_call" | custom-call | flops 536870912 | bytes 2097152 | tf_op jit(solution)/shard_map/rest/pallas_call | solution.py:430
  61.1 8.8 %all_to_all.20 = f32[8,1,128]{2,1,0:T(1,128)S(1)} all-to-all(f32[8,1,128]{2,1,0:T(1,128)} %bitcast.9), channel_id=1, replica_groups=mesh['sub'=4,'blk'=8] {'blk'}, dimensions={0} | all-to-all | bytes 8192 | tf_op jit(solution)/shard_map/all_to_all | solution.py:481
  70.0 0.5 reduce_sum.9
Async XLA Ops:
  3.1 3.9 %copy-start = (f32[4,32,256]{2,1,0:T(8,128)S(1)}, f32[4,32,256]{2,1,0:T(8,128)}, u32[]{:S(2)}) copy-start(f32[4,32,256]{2,1,0:T(8,128)} %get-tuple-element.9.payload.payload_in) | copy-start | bytes 393220
  3.1 34.5 %all-to-all-start = ((f32[8,8,256]{2,1,0:T(8,128)}), f32[8,8,256]{2,1,0:T(8,128)S(1)}, u32[]{:S(2)}, u32[]{:S(2)}) async-start(f32[8,8,256]{2,1,0:T(8,128)} %bitcast.8), calls=%async_computation | async-start | bytes 131072 | tf_op jit(solution)/shard_map/all_to_all | solution.py:405
  37.6 0.6 copy-start.1

commit v4 on v3

--- a/solution.py
+++ b/solution.py
@@ -30,10 +30,11 @@
     return high, middle, low
 
 
-def put_rows(rows_ref, tiles, rows):
+def put_rows(rows_ref, base, rows):
     for r, row in enumerate(rows):
+        tiles = row.shape[0]
         for half in range(row.shape[1] // 128):
-            rows_ref[half, pl.ds(r, tiles, stride=depth), :] = row[:, half * 128 : (half + 1) * 128]
+            rows_ref[half, pl.ds(base * depth + r, tiles, stride=depth), :] = row[:, half * 128 : (half + 1) * 128]
 
 
 def point_rows(planes):
@@ -43,67 +44,49 @@
     return split, norm
 
 
-def build_source(planes, rows_ref, a_ref, s_ref, base):
-    tiles = planes[3].shape[0]
+def put_source(planes, rows_ref, base):
     split, norm = point_rows(planes)
     ones = jnp.ones_like(norm)
-    zeros = jnp.zeros_like(norm)
     norm = norm + jnp.where(planes[3] > 0.0, 0.0, far_off)
     rows = []
     for high, middle, low in split:
         rows += [high, high, middle, high, low, middle]
     rows += list(pieces(-norm)) + [ones, ones, ones] + [planes[3]]
-    rows += [zeros] * (depth - len(rows))
-    put_rows(rows_ref, tiles, rows)
-    halves = norm.shape[1] // 128
-
-    def some_tiles(step, carry):
-        for t in [step * 4 + i for i in range(4)]:
-            for half in range(halves):
-                block = rows_ref[half, pl.ds(pl.multiple_of(t * depth, depth), depth), :]
-                turned = block.T
-                a_ref[base + t, half * 128 : (half + 1) * 128, :] = turned.astype(bf16)
-                s_ref[base + t, half * 128 : (half + 1) * 128, :] = jnp.broadcast_to(turned[:, 24:25], (128, 128))
-        return carry
-
-    lax.fori_loop(0, tiles // 4, some_tiles, 0)
-
-
-def build_target(planes, rows_ref, b_ref):
-    tiles = planes[3].shape[0]
+    rows += [jnp.zeros_like(norm)] * (depth - len(rows))
+    put_rows(rows_ref, base, rows)
+
+
+def put_target(planes, rows_ref):
     split, norm = point_rows(planes)
     ones = jnp.ones_like(norm)
-    zeros = jnp.zeros_like(norm)
     rows = []
     for high, middle, low in split:
         rows += [2.0 * v for v in (high, middle, high, low, high, middle)]
     rows += [ones, ones, ones] + list(pieces(-norm))
-    rows += [zeros] * (depth - len(rows))
-    put_rows(rows_ref, tiles, rows)
-    halves = norm.shape[1] // 128
-
-    def some_tiles(step, carry):
-        for t in [step * 4 + i for i in range(4)]:
-            for half in range(halves):
-                block = rows_ref[half, pl.ds(pl.multiple_of(t * depth, depth), depth), :]
-                b_ref[t, :, half * 128 : (half + 1) * 128] = block.astype(bf16)
-        return carry
-
-    lax.fori_loop(0, tiles // 4, some_tiles, 0)
+    rows += [jnp.zeros_like(norm)] * (depth - len(rows))
+    put_rows(rows_ref, 0, rows)
+
+
+def turn_group(rows_ref, group):
+    rows = pl.ds(pl.multiple_of(group * 128, 128), 128)
+    turned = jnp.concatenate([rows_ref[half, rows, :].T for half in range(rows_ref.shape[0])], axis=0)
+    left = turned.astype(bf16)
+    column = lax.broadcasted_iota(jnp.int32, (1, 128), 1) // depth
+    operands = []
+    for j in range(4):
+        mask = (column == j).astype(f32).astype(bf16)
+        lane = depth * j + 24
+        operands.append((left * mask, jnp.broadcast_to(turned[:, lane : lane + 1], turned.shape)))
+    return operands
 
 
 def pair_sums(a, s, b):
     points = a.shape[0]
     width = b.shape[1]
-    step = min(points, 128)
-    num = jnp.zeros((8, width), f32)
-    den = jnp.zeros((8, width), f32)
-    for lo in range(0, points, step):
-        power = jnp.dot(a[lo : lo + step], b, preferred_element_type=f32)
-        weight = jnp.exp2(power)
-        load = jnp.concatenate([s[lo : lo + step]] * (width // 128), axis=1)
-        den = den + jnp.sum(weight.reshape(step // 8, 8, width), axis=0)
-        num = num + jnp.sum((weight * load).reshape(step // 8, 8, width), axis=0)
+    weight = jnp.exp2(jnp.dot(a, b, preferred_element_type=f32))
+    load = jnp.concatenate([s] * (width // 128), axis=1)
+    den = jnp.sum(weight.reshape(points // 8, 8, width), axis=0)
+    num = jnp.sum((weight * load).reshape(points // 8, 8, width), axis=0)
     return num, den
 
 
@@ -162,19 +145,35 @@
     lax.fori_loop(0, peers, listed, 0, unroll=peers <= 8)
 
 
-def own_kernel(payload, local_pairs_in, b_ref, num_ref, den_ref, rows_ref, a_ref, s_ref, local_pairs, sems):
+def own_kernel(
+    payload, local_pairs_in, b_out, num_ref, den_ref, rows_ref, a_ref, s_ref, b_ref, local_pairs, sems, b_sems
+):
     tiles = payload.shape[1]
     copies = fetch((local_pairs_in,), (local_pairs,), sems)
     planes = [payload[k] for k in range(4)]
-    build_source(planes, rows_ref, a_ref, s_ref, 0)
-    build_target(planes, rows_ref, b_ref)
+    put_target(planes, rows_ref)
+
+    def set_target(group, carry):
+        for t in [group * 4 + i for i in range(4)]:
+            rows = pl.ds(pl.multiple_of(t * depth, depth), depth)
+            for half in range(rows_ref.shape[0]):
+                block = rows_ref[half, rows, :].astype(bf16)
+                for j in range(4):
+                    b_ref[t, depth * j : depth * (j + 1), half * 128 : (half + 1) * 128] = block
+        return carry
+
+    lax.fori_loop(0, tiles // 4, set_target, 0)
+    b_copies = fetch((b_ref.at[:, 0:depth, :],), (b_out,), b_sems)
+    put_source(planes, rows_ref, 0)
     for copy in copies:
         copy.wait()
 
-    def own(step, carry):
-        group = [step * 4 + i for i in range(4)]
-        sums = [pair_sums(a_ref[t], s_ref[t], b_ref[t]) for t in group]
-        for t, (num, den) in zip(group, sums):
+    def own(group, carry):
+        for i, (a, s) in enumerate(turn_group(rows_ref, group)):
+            t = group * 4 + i
+            a_ref[t] = a
+            s_ref[t] = s
+            num, den = pair_sums(a, s, b_ref[t])
             num_ref[t] = num
             den_ref[t] = den
         return carry
@@ -183,9 +182,9 @@
 
     def listed(step, carry):
         group = []
-        for i in range(2):
-            one = local_pairs[0, step * 2 + i]
-            two = local_pairs[1, step * 2 + i]
+        for i in range(4):
+            one = local_pairs[0, step * 4 + i]
+            two = local_pairs[1, step * 4 + i]
             group += [(one, two), (two, one)]
         sums = [pair_sums(a_ref[src], s_ref[src], b_ref[dst]) for src, dst in group]
         for (src, dst), (num, den) in zip(group, sums):
@@ -193,12 +192,15 @@
             den_ref[dst] = den_ref[dst] + den
         return carry
 
-    lax.fori_loop(0, local_pairs.shape[1] // 2, listed, 0)
+    lax.fori_loop(0, local_pairs.shape[1] // 4, listed, 0)
+    for copy in b_copies:
+        copy.wait()
 
 
 def rest_kernel(
     peers,
-    layers_in,
+    below_in,
+    above_in,
     inbox_in,
     b_in,
     num_in,
@@ -215,11 +217,7 @@
     damage_ref,
     parts_ref,
     rows_ref,
-    a_ref,
-    s_ref,
     far_rows,
-    far_a,
-    far_s,
     sub_rows,
     map_rows,
     below,
@@ -237,19 +235,21 @@
     send_tile,
     remote_pairs,
     remote_count,
+    far_tile,
+    far_live,
     layer_sems,
     sum_sems,
     sems,
 ):
     tiles, points = history.shape
-    count = layers_in.shape[0]
+    count = lax.axis_size("sub")
     layer = lax.axis_index("sub")
-    from_below, from_above = fetch(
-        (layers_in.at[jnp.maximum(layer - 1, 0)], layers_in.at[jnp.minimum(layer + 1, count - 1)]),
-        (below, above),
-        layer_sems,
+    from_below, from_above = fetch((below_in, above_in), (below, above), layer_sems)
+    sum_copies = fetch(
+        [b_in] * 4 + [num_in, den_in],
+        [b_ref.at[:, depth * j : depth * (j + 1), :] for j in range(4)] + [num_ref, den_ref],
+        sum_sems,
     )
-    sum_copies = fetch((b_in, num_in, den_in), (b_ref, num_ref, den_ref), sum_sems)
     halves = points // 128
     copies = fetch(
         [inbox_in.at[:, half * 128 : (half + 1) * 128] for half in range(halves)]
@@ -269,37 +269,38 @@
         sems,
     )
 
-    def border(offset):
-        def some(step, carry):
-            for t in (2 * step, 2 * step + 1):
-                num = num_ref[t]
-                den = den_ref[t]
-                other = lax.rem(t + offset, tiles)
-                for src in (t, other):
-                    more_num, more_den = pair_sums(a_ref[src], s_ref[src], b_ref[t])
-                    num = num + more_num
-                    den = den + more_den
-                num_ref[t] = num
-                den_ref[t] = den
+    def border(shift):
+        def some(group, carry):
+            sums = {}
+            for i, (a, s) in enumerate(turn_group(rows_ref, group)):
+                for place in (i, i + shift):
+                    t = lax.rem(group * 4 + place + tiles, tiles)
+                    num, den = pair_sums(a, s, b_ref[t])
+                    if place in sums:
+                        num, den = sums[place][1] + num, sums[place][2] + den
+                    sums[place] = (t, num, den)
+            for t, num, den in sums.values():
+                num_ref[t] = num_ref[t] + num
+                den_ref[t] = den_ref[t] + den
             return carry
 
-        lax.fori_loop(0, tiles // 2, some, 0)
+        lax.fori_loop(0, tiles // 4, some, 0)
 
     from_below.wait()
-    build_source([below[k] for k in range(4)], rows_ref, a_ref, s_ref, 0)
+    put_source([below[k] for k in range(4)], rows_ref, 0)
     for copy in sum_copies:
         copy.wait()
 
     @pl.when(layer > 0)
     def lower():
-        border(1)
+        border(-1)
 
     from_above.wait()
 
     @pl.when(layer < count - 1)
     def upper():
-        build_source([above[k] for k in range(4)], rows_ref, a_ref, s_ref, 0)
-        border(tiles - 1)
+        put_source([above[k] for k in range(4)], rows_ref, 0)
+        border(1)
 
     for copy in copies:
         copy.wait()
@@ -310,22 +311,28 @@
             )
             for k in range(4)
         ]
-        build_source(planes, far_rows, far_a, far_s, which * peers)
-
-    def far(step, carry):
-        group = []
-        for i in (2 * step, 2 * step + 1):
-            live = (i < remote_count[0]).astype(f32)
-            group += [(remote_pairs[1, i], remote_pairs[0, i], live), (peers + i, send_tile[i], None)]
-        sums = [pair_sums(far_a[src], far_s[src], b_ref[dst]) for src, dst, live in group]
-        for (src, dst, live), (num, den) in zip(group, sums):
-            if live is not None:
-                num, den = num * live, den * live
-            num_ref[dst] = num_ref[dst] + num
-            den_ref[dst] = den_ref[dst] + den
-        return carry
-
-    lax.fori_loop(0, peers // 2, far, 0)
+        put_source(planes, far_rows, which * peers)
+
+    def place(i, carry):
+        h = remote_pairs[1, i]
+        far_tile[h] = remote_pairs[0, i]
+        far_live[h] = (i < remote_count[0]).astype(jnp.int32)
+        far_tile[peers + i] = send_tile[i]
+        far_live[peers + i] = 1
+        return carry
+
+    lax.fori_loop(0, peers, place, 0, unroll=peers <= 8)
+
+    def far(group, carry):
+        for i, (a, s) in enumerate(turn_group(far_rows, group)):
+            t = far_tile[group * 4 + i]
+            live = far_live[group * 4 + i].astype(f32)
+            num, den = pair_sums(a, s, b_ref[t])
+            num_ref[t] = num_ref[t] + num * live
+            den_ref[t] = den_ref[t] + den * live
+        return carry
+
+    lax.fori_loop(0, 2 * peers // 4, far, 0)
 
     valid = (own_strain[...] > 0.0).astype(f32)
     num = jnp.sum(num_ref[...], axis=1) * valid
@@ -401,7 +408,9 @@
         name="pack",
     )(coords, strain, tile_count, send_tile, remote_pairs, remote_count)
 
-    layers = lax.all_gather(payload, "sub")
+    layers = lax.axis_size("sub")
+    below = lax.ppermute(payload, "sub", [(i, i + 1) for i in range(layers - 1)])
+    above = lax.ppermute(payload, "sub", [(i + 1, i) for i in range(layers - 1)])
     inbox = lax.all_to_all(outbox, "blk", split_axis=0, concat_axis=0, tiled=True)
 
     b_own, num, den = pl.pallas_call(
@@ -412,12 +421,14 @@
             jax.ShapeDtypeStruct((tiles, 8, points), f32),
         ),
         in_specs=[in_vmem, in_hbm],
-        out_specs=(in_vmem,) * 3,
+        out_specs=(in_hbm, in_vmem, in_vmem),
         scratch_shapes=[
             pltpu.VMEM((halves, tiles * depth, 128), f32),
-            pltpu.VMEM((tiles, points, depth), bf16),
+            pltpu.VMEM((tiles, points, 4 * depth), bf16),
             pltpu.VMEM((tiles, points, 128), f32),
+            pltpu.VMEM((tiles, 4 * depth, points), bf16),
             pltpu.SMEM(local_pairs.shape, jnp.int32),
+            pltpu.SemaphoreType.DMA((1,)),
             pltpu.SemaphoreType.DMA((1,)),
         ],
         compiler_params=params,
@@ -433,21 +444,17 @@
             jax.ShapeDtypeStruct((tiles, points), f32),
             jax.ShapeDtypeStruct((peers, 128), f32),
         ),
-        in_specs=[in_hbm] * 14,
+        in_specs=[in_hbm] * 15,
         out_specs=(in_vmem,) * 2,
         scratch_shapes=[
             pltpu.VMEM((halves, tiles * depth, 128), f32),
-            pltpu.VMEM((tiles, points, depth), bf16),
-            pltpu.VMEM((tiles, points, 128), f32),
-            pltpu.VMEM((halves, peers * depth, 128), f32),
-            pltpu.VMEM((2 * peers, points, depth), bf16),
-            pltpu.VMEM((2 * peers, points, 128), f32),
+            pltpu.VMEM((halves, 2 * peers * depth, 128), f32),
             pltpu.VMEM((tiles, 128), jnp.int32),
             pltpu.VMEM((subs * corners, 128), jnp.int32),
             pltpu.VMEM(payload.shape, f32),
             pltpu.VMEM(payload.shape, f32),
             pltpu.VMEM((halves, peers * 8, 128), f32),
-            pltpu.VMEM(b_own.shape, bf16),
+            pltpu.VMEM((tiles, 4 * depth, points), bf16),
             pltpu.VMEM(num.shape, f32),
             pltpu.VMEM(den.shape, f32),
             pltpu.VMEM(strain.shape, f32),
@@ -456,14 +463,16 @@
             pltpu.VMEM(external.shape, f32),
         ]
         + [pltpu.SMEM(v.shape, jnp.int32) for v in (tile_sub, corner_map, send_tile, remote_pairs, remote_count)]
-        + [pltpu.SemaphoreType.DMA((n,)) for n in (2, 3, 9 + halves)],
+        + [pltpu.SMEM((2 * peers,), jnp.int32)] * 2
+        + [pltpu.SemaphoreType.DMA((n,)) for n in (2, 6, 9 + halves)],
         compiler_params=params,
         cost_estimate=pl.CostEstimate(
             flops=4 * tiles * block * depth, bytes_accessed=1 << 21, transcendentals=4 * tiles * points * points
         ),
         name="rest",
     )(
-        layers,
+        below,
+        above,
         inbox,
         b_own,
         num,

time: 70.8 us -> 49.1 us (0.69)
  blocking collectives: 26 us -> 8.86 us
  Pallas kernels: 38.1 us -> 27.7 us
  starting transfers between devices: 3.87 us -> 9.58 us
    all_gather x1 -> x0, blocking collectives: 17.2 us -> none  [per_device(): layers = lax.all_gather(payload, 'sub')]
    pallas_call x1, Pallas kernels: 22.9 us -> 15.4 us  [per_device(): pl.pallas_call(functools.partial(rest_kernel, peers), out_shape=(jax.Shap...]
    ppermute x0 -> x2, starting transfers between devices: none -> 5.84 us  [the longest x1 3.92 us: per_device(): lax.ppermute(payload, 'sub', [(i, i + 1) for i in range(layers - 1)])]
    pallas_call x1, Pallas kernels: 13.4 us -> 10.5 us  [per_device(): pl.pallas_call(own_kernel, out_shape=(jax.ShapeDtypeStruct((tiles, depth,...]
  transfers between devices with their start and end apart: 1 -> 3, of which waited for: 0 -> 0; matrix products, arithmetic and copies ran while one was open for 0% -> 0% of each run, Pallas kernels for 19% -> 22%
where the time goes in v4:
time: 49.1 us; the launch traced here: 48.7 us
  Pallas kernels  27.7 us (56%)
  starting transfers between devices  9.58 us (20%)
  blocking collectives  8.86 us (18%)
  between operations  1.37 us (3%)
  local copies, waits for them, and re-layouts  0.69 us (1%)
  other arithmetic  0.54 us (1%)
    pallas_call x1, Pallas kernels, per_device(): pl.pallas_call(functools.partial(rest_kernel, peers), out_shape=(jax.Shap...  15.4 us
    pallas_call x1, Pallas kernels, per_device(): pl.pallas_call(own_kernel, out_shape=(jax.ShapeDtypeStruct((tiles, depth,...  10.5 us
    all_to_all x1, blocking collectives, per_device(): lax.all_to_all(parts, 'blk', split_axis=0, concat_axis=0, tiled=True)  8.86 us
    ppermute x1, starting transfers between devices, per_device(): lax.ppermute(payload, 'sub', [(i, i + 1) for i in range(layers - 1)])  3.92 us
    all_to_all x1, starting transfers between devices, per_device(): lax.all_to_all(outbox, 'blk', split_axis=0, concat_axis=0, tiled=True)  3.74 us
    ppermute x1, starting transfers between devices, per_device(): lax.ppermute(payload, 'sub', [(i + 1, i) for i in range(layers - 1)])  1.92 us
    pallas_call x1, Pallas kernels, per_device(): pl.pallas_call(functools.partial(pack_kernel, peers), out_shape=(jax.Shap...  1.79 us
  transfers between devices with their start and end apart: 3, of which 0 were waited for; matrix products, arithmetic and copies ran while one was open for 0% of the time, Pallas kernels for 22%

profile of v4, /device:TPU:8, one launch (start us, length us, event | category | flops | bytes accessed | tf_op | source)
XLA Modules:
  0.0 48.7 jit_solution(16084756232406055963)
XLA Ops:
  1.3 1.8 %pack.1 = (f32[4,32,256]{2,1,0:T(8,128)}, f32[64,256]{1,0:T(8,128)}) custom-call(f32[3,32,256]{2,1,0:T(8,128)} %coords.1, f32[32,256]{1,0:T(8,128)} %strain.1, s32[32]{0:T(128)} %tile_count_in.1, s32[8]{0:T(128)} %send_tile_in.3, s32[2,8]{1,0:T(2,128)} %remote_pairs_in.3, s32[1]{0:T(128)S(6)} %copy.15.remote_count_in), custom_call_target="tpu_custom_call" | custom-call | tf_op jit(solution)/shard_map/pack/pallas_call | solution.py:396
  3.1 1.9 %collective-permute-start.1 = (f32[4,32,256]{2,1,0:T(8,128)}, f32[4,32,256]{2,1,0:T(8,128)S(1)}, u32[]{:S(2)}, u32[]{:S(2)}) collective-permute-start(f32[4,32,256]{2,1,0:T(8,128)} %get-tuple-element.9.payload.payload_in), channel_id=1, source_target_pairs={{8,0},{16,8},{24,16},{9,1},{17,9},{25,17},{10,2},{18,10},{26,18},{... | collective-permute-start | bytes 393224 | tf_op jit(solution)/shard_map/ppermute | solution.py:413
  5.0 3.9 %collective-permute-start = (f32[4,32,256]{2,1,0:T(8,128)}, f32[4,32,256]{2,1,0:T(8,128)S(1)}, u32[]{:S(2)}, u32[]{:S(2)}) collective-permute-start(f32[4,32,256]{2,1,0:T(8,128)} %get-tuple-element.9.payload.payload_in), channel_id=1, source_target_pairs={{0,8},{8,16},{16,24},{1,9},{9,17},{17,25},{2,10},{10,18},{18,26},{... | collective-permute-start | bytes 393224 | tf_op jit(solution)/shard_map/ppermute | solution.py:412
  8.9 3.7 %all-to-all-start = ((f32[8,8,256]{2,1,0:T(8,128)}), f32[8,8,256]{2,1,0:T(8,128)S(1)}, u32[]{:S(2)}, u32[]{:S(2)}) async-start(f32[8,8,256]{2,1,0:T(8,128)} %bitcast.6), calls=%async_computation | async-start | bytes 131072 | tf_op jit(solution)/shard_map/all_to_all | solution.py:414
  12.7 10.5 %own.1 = (bf16[32,32,256]{2,1,0:T(8,128)(2,1)}, f32[32,8,256]{2,1,0:T(8,128)}, f32[32,8,256]{2,1,0:T(8,128)}) custom-call(f32[4,32,256]{2,1,0:T(8,128)} %get-tuple-element.9.payload.payload_in, s32[2,32]{1,0:T(2,128)} %local_pairs_in.1), custom_call_target="tpu_custom_call" | custom-call | flops 402653184 | bytes 1048576 | tf_op jit(solution)/shard_map/own/pallas_call | solution.py:416
  23.2 0.0 all-to-all-done
  23.2 0.0 copy-start
  23.2 0.0 collective-permute-done.1.above_in
  23.2 0.0 copy-start.1
  23.2 0.0 collective-permute-done.below_in
  23.2 0.0 copy-start.2
  23.2 0.6 %copy-done = f32[8,8,256]{2,1,0:T(8,128)} copy-done((f32[8,8,256]{2,1,0:T(8,128)}, f32[8,8,256]{2,1,0:T(8,128)S(1)}, u32[]{:S(2)}) %copy-start) | copy-done | bytes 65560
  23.8 0.1 copy-done.1
  23.9 0.1 copy-done.2
  23.9 15.4 %rest.1 = (f32[32,256]{1,0:T(8,128)}, f32[8,128]{1,0:T(8,128)}) custom-call(f32[4,32,256]{2,1,0:T(8,128)} %copy-done.2, f32[4,32,256]{2,1,0:T(8,128)} %copy-done.1, f32[64,256]{1,0:T(8,128)} %bitcast.5, bf16[32,32,256]{2,1,0:T(8,128)(2,1)} %get-tuple-element.11.b_in, f32[32,8,256]{2,1,0:T(8,128)} %get-tuple-element.12.num_in, ...), custom_call_target="tpu_custom_call" | custom-call | flops 536870912 | bytes 2097152 | tf_op jit(solution)/shard_map/rest/pallas_call | solution.py:441
  39.3 8.9 %all_to_all.20 = f32[8,1,128]{2,1,0:T(1,128)S(1)} all-to-all(f32[8,1,128]{2,1,0:T(1,128)} %bitcast.7), channel_id=1, replica_groups=mesh['sub'=4,'blk'=8] {'blk'}, dimensions={0} | all-to-all | bytes 8192 | tf_op jit(solution)/shard_map/all_to_all | solution.py:490
  48.2 0.5 %reduce_sum.9 = f32[128]{0:T(128)} reduce(f32[8,1,128]{2,1,0:T(1,128)S(1)} %all_to_all.20, f32[]{:T(128)} %constant.0.clone.1), dimensions={0,1}, to_apply=%region_0.0 | reduce | flops 896 | bytes 4612 | tf_op jit(solution)/shard_map/reduce_sum | solution.py:491
Async XLA Ops:
  3.1 20.1 %collective-permute-start.1 = (f32[4,32,256]{2,1,0:T(8,128)}, f32[4,32,256]{2,1,0:T(8,128)S(1)}, u32[]{:S(2)}, u32[]{:S(2)}) collective-permute-start(f32[4,32,256]{2,1,0:T(8,128)} %get-tuple-element.9.payload.payload_in), channel_id=1, source_target_pairs={{8,0},{16,8},{24,16},{9,1},{17,9},{25,17},{10,2},{18,10},{26,18},{... | collective-permute-start | bytes 393224 | tf_op jit(solution)/shard_map/ppermute | solution.py:413
  5.0 18.2 %collective-permute-start = (f32[4,32,256]{2,1,0:T(8,128)}, f32[4,32,256]{2,1,0:T(8,128)S(1)}, u32[]{:S(2)}, u32[]{:S(2)}) collective-permute-start(f32[4,32,256]{2,1,0:T(8,128)} %get-tuple-element.9.payload.payload_in), channel_id=1, source_target_pairs={{0,8},{8,16},{16,24},{1,9},{9,17},{17,25},{2,10},{10,18},{18,26},{... | collective-permute-start | bytes 393224 | tf_op jit(solution)/shard_map/ppermute | solution.py:412
  8.9 14.2 %all-to-all-start = ((f32[8,8,256]{2,1,0:T(8,128)}), f32[8,8,256]{2,1,0:T(8,128)S(1)}, u32[]{:S(2)}, u32[]{:S(2)}) async-start(f32[8,8,256]{2,1,0:T(8,128)} %bitcast.6), calls=%async_computation | async-start | bytes 131072 | tf_op jit(solution)/shard_map/all_to_all | solution.py:414
  23.2 0.6 %copy-start = (f32[8,8,256]{2,1,0:T(8,128)}, f32[8,8,256]{2,1,0:T(8,128)S(1)}, u32[]{:S(2)}) copy-start(f32[8,8,256]{2,1,0:T(8,128)S(1)} %all-to-all-done) | copy-start | bytes 196612
  23.2 0.7 %copy-start.1 = (f32[4,32,256]{2,1,0:T(8,128)}, f32[4,32,256]{2,1,0:T(8,128)S(1)}, u32[]{:S(2)}) copy-start(f32[4,32,256]{2,1,0:T(8,128)S(1)} %collective-permute-done.1.above_in) | copy-start | bytes 393220
  23.2 0.7 %copy-start.2 = (f32[4,32,256]{2,1,0:T(8,128)}, f32[4,32,256]{2,1,0:T(8,128)S(1)}, u32[]{:S(2)}) copy-start(f32[4,32,256]{2,1,0:T(8,128)S(1)} %collective-permute-done.below_in) | copy-start | bytes 393220

commit v5 on v4

--- a/solution.py
+++ b/solution.py
@@ -14,12 +14,14 @@
 coord_scale = math.sqrt(gauss_rate * math.log2(math.e))
 far_off = 2048.0
 depth = 32
-grant = 60 * 1024 * 1024
+pitch = depth + 1
+grant = 24 * 1024 * 1024
+whole_grant = 60 * 1024 * 1024
 
 f32 = jnp.float32
 bf16 = jnp.bfloat16
 in_vmem = pl.BlockSpec(memory_space=pltpu.VMEM)
-in_hbm = pl.BlockSpec(memory_space=pltpu.HBM)
+anywhere = pl.BlockSpec(memory_space=pl.ANY)
 
 
 def pieces(value):
@@ -34,7 +36,7 @@
     for r, row in enumerate(rows):
         tiles = row.shape[0]
         for half in range(row.shape[1] // 128):
-            rows_ref[half, pl.ds(base * depth + r, tiles, stride=depth), :] = row[:, half * 128 : (half + 1) * 128]
+            rows_ref[half, pl.ds(base * pitch + r, tiles, stride=pitch), :] = row[:, half * 128 : (half + 1) * 128]
 
 
 def point_rows(planes):
@@ -68,8 +70,13 @@
 
 
 def turn_group(rows_ref, group):
-    rows = pl.ds(pl.multiple_of(group * 128, 128), 128)
-    turned = jnp.concatenate([rows_ref[half, rows, :].T for half in range(rows_ref.shape[0])], axis=0)
+    turned = jnp.concatenate(
+        [
+            jnp.concatenate([rows_ref[half, pl.ds((group * 4 + j) * pitch, depth), :] for j in range(4)], axis=0).T
+            for half in range(rows_ref.shape[0])
+        ],
+        axis=0,
+    )
     left = turned.astype(bf16)
     column = lax.broadcasted_iota(jnp.int32, (1, 128), 1) // depth
     operands = []
@@ -126,28 +133,35 @@
     for t in range(tiles):
         payload[3, t : t + 1, :] = jnp.where(lane < tile_count[t], strain_here[t : t + 1, :], 0.0)
 
+    halves = points // 128
+
+    def put(h, first, t, live):
+        for k in range(4):
+            row = payload[k, pl.ds(t, 1), :]
+            if k == 3 and live is not None:
+                row = row * live
+            for half in range(halves):
+                outbox[pl.ds((h * halves + half) * 8 + first + k, 1), :] = row[:, half * 128 : (half + 1) * 128]
+
     def sent(h, carry):
-        t = send_tile[h]
-        for k in range(4):
-            outbox[pl.ds(8 * h + k, 1), :] = payload[k, pl.ds(t, 1), :]
+        put(h, 0, send_tile[h], None)
         return carry
 
     def listed(i, carry):
-        t = remote_pairs[0, i]
-        h = remote_pairs[1, i]
-        live = (i < remote_count[0]).astype(f32)
-        for k in range(3):
-            outbox[pl.ds(8 * h + 4 + k, 1), :] = payload[k, pl.ds(t, 1), :]
-        outbox[pl.ds(8 * h + 7, 1), :] = payload[3, pl.ds(t, 1), :] * live
+        put(remote_pairs[1, i], 4, remote_pairs[0, i], (i < remote_count[0]).astype(f32))
         return carry
 
     lax.fori_loop(0, peers, sent, 0, unroll=peers <= 8)
     lax.fori_loop(0, peers, listed, 0, unroll=peers <= 8)
 
 
-def own_kernel(
-    payload, local_pairs_in, b_out, num_ref, den_ref, rows_ref, a_ref, s_ref, b_ref, local_pairs, sems, b_sems
-):
+def spread_rows(values):
+    n = values.shape[1]
+    wide = jnp.concatenate([values.astype(f32), jnp.zeros((1, 128 - n), f32)], axis=1)
+    return jnp.broadcast_to(wide, (128, 128)).T[0:n]
+
+
+def own_kernel(payload, local_pairs_in, b_ref, num_ref, den_ref, rows_ref, a_ref, s_ref, local_pairs, sems):
     tiles = payload.shape[1]
     copies = fetch((local_pairs_in,), (local_pairs,), sems)
     planes = [payload[k] for k in range(4)]
@@ -155,7 +169,7 @@
 
     def set_target(group, carry):
         for t in [group * 4 + i for i in range(4)]:
-            rows = pl.ds(pl.multiple_of(t * depth, depth), depth)
+            rows = pl.ds(t * pitch, depth)
             for half in range(rows_ref.shape[0]):
                 block = rows_ref[half, rows, :].astype(bf16)
                 for j in range(4):
@@ -163,7 +177,6 @@
         return carry
 
     lax.fori_loop(0, tiles // 4, set_target, 0)
-    b_copies = fetch((b_ref.at[:, 0:depth, :],), (b_out,), b_sems)
     put_source(planes, rows_ref, 0)
     for copy in copies:
         copy.wait()
@@ -193,121 +206,103 @@
         return carry
 
     lax.fori_loop(0, local_pairs.shape[1] // 4, listed, 0)
-    for copy in b_copies:
-        copy.wait()
 
 
 def rest_kernel(
     peers,
-    below_in,
-    above_in,
-    inbox_in,
-    b_in,
+    below,
+    above,
+    inbox,
+    b_ref,
     num_in,
     den_in,
-    payload_in,
-    history_in,
-    corner_load_in,
-    external_in,
-    tile_sub_in,
-    corner_map_in,
+    payload,
+    history,
+    corner_load,
+    external,
+    tile_sub,
+    corner_map,
     send_tile_in,
     remote_pairs_in,
     remote_count_in,
     damage_ref,
     parts_ref,
+    num_ref,
+    den_ref,
     rows_ref,
     far_rows,
-    sub_rows,
-    map_rows,
-    below,
-    above,
-    inbox,
-    b_ref,
-    num_ref,
-    den_ref,
-    own_strain,
-    history,
-    corner_load,
-    external,
-    tile_sub,
-    corner_map,
+    last_a,
+    last_s,
     send_tile,
     remote_pairs,
     remote_count,
     far_tile,
     far_live,
-    layer_sems,
-    sum_sems,
     sems,
 ):
     tiles, points = history.shape
+    halves = points // 128
+    groups = tiles // 4
     count = lax.axis_size("sub")
     layer = lax.axis_index("sub")
-    from_below, from_above = fetch((below_in, above_in), (below, above), layer_sems)
-    sum_copies = fetch(
-        [b_in] * 4 + [num_in, den_in],
-        [b_ref.at[:, depth * j : depth * (j + 1), :] for j in range(4)] + [num_ref, den_ref],
-        sum_sems,
-    )
-    halves = points // 128
     copies = fetch(
-        [inbox_in.at[:, half * 128 : (half + 1) * 128] for half in range(halves)]
-        + [
-            payload_in.at[3],
-            history_in,
-            corner_load_in,
-            external_in,
-            tile_sub_in,
-            corner_map_in,
-            send_tile_in,
-            remote_pairs_in,
-            remote_count_in,
-        ],
-        [inbox.at[half] for half in range(halves)]
-        + [own_strain, history, corner_load, external, tile_sub, corner_map, send_tile, remote_pairs, remote_count],
+        (send_tile_in, remote_pairs_in, remote_count_in),
+        (send_tile, remote_pairs, remote_count),
         sems,
     )
 
     def border(shift):
-        def some(group, carry):
-            sums = {}
-            for i, (a, s) in enumerate(turn_group(rows_ref, group)):
-                for place in (i, i + shift):
-                    t = lax.rem(group * 4 + place + tiles, tiles)
-                    num, den = pair_sums(a, s, b_ref[t])
-                    if place in sums:
-                        num, den = sums[place][1] + num, sums[place][2] + den
-                    sums[place] = (t, num, den)
-            for t, num, den in sums.values():
+        def turned(step):
+            group = step if shift < 0 else groups - 1 - step
+            return group, turn_group(rows_ref, group)
+
+        edge = 3 if shift < 0 else 0
+
+        def keep(operands):
+            last_a[...] = operands[edge][0]
+            last_s[...] = operands[edge][1]
+
+        keep(turned(groups - 1)[1])
+
+        def some(step, carry):
+            group, operands = turned(step)
+            outer = (last_a[...], last_s[...])
+            sums = []
+            for i in range(4):
+                a, s = operands[i]
+                more_a, more_s = operands[i + shift] if 0 <= i + shift < 4 else outer
+                sums.append(
+                    pair_sums(
+                        jnp.concatenate([a, more_a], axis=0),
+                        jnp.concatenate([s, more_s], axis=0),
+                        b_ref[group * 4 + i],
+                    )
+                )
+            for i, (num, den) in enumerate(sums):
+                t = group * 4 + i
                 num_ref[t] = num_ref[t] + num
                 den_ref[t] = den_ref[t] + den
+            keep(operands)
             return carry
 
-        lax.fori_loop(0, tiles // 4, some, 0)
-
-    from_below.wait()
-    put_source([below[k] for k in range(4)], rows_ref, 0)
-    for copy in sum_copies:
-        copy.wait()
+        lax.fori_loop(0, groups, some, 0)
 
     @pl.when(layer > 0)
     def lower():
-        border(-1)
-
-    from_above.wait()
+        put_source([below[k] for k in range(4)], rows_ref, 0)
+        border(1)
 
     @pl.when(layer < count - 1)
     def upper():
         put_source([above[k] for k in range(4)], rows_ref, 0)
-        border(1)
+        border(-1)
 
     for copy in copies:
         copy.wait()
     for which in range(2):
         planes = [
             jnp.concatenate(
-                [inbox[half, pl.ds(4 * which + k, peers, stride=8), :] for half in range(points // 128)], axis=1
+                [inbox[pl.ds(half * 8 + 4 * which + k, peers, stride=8 * halves), :] for half in range(halves)], axis=1
             )
             for k in range(4)
         ]
@@ -334,7 +329,7 @@
 
     lax.fori_loop(0, 2 * peers // 4, far, 0)
 
-    valid = (own_strain[...] > 0.0).astype(f32)
+    valid = (payload[3] > 0.0).astype(f32)
     num = jnp.sum(num_ref[...], axis=1) * valid
     den = jnp.sum(den_ref[...], axis=1) * valid
     strain_bar = num / (den + 1.0 - valid)
@@ -343,25 +338,19 @@
     damage_ref[...] = damage
     intact = (1.0 - damage) * valid
 
-    for t in range(tiles):
-        sub_rows[t : t + 1, :] = jnp.full((1, 128), tile_sub[t], jnp.int32)
-    subs, corners = corner_map.shape
-    for m in range(subs):
-        for c in range(corners):
-            r = m * corners + c
-            map_rows[r : r + 1, :] = jnp.full((1, 128), corner_map[m, c], jnp.int32)
-
     folded = corner_load[:, :, 0:128] * intact[None, :, 0:128]
     for half in range(1, points // 128):
         cut = slice(half * 128, (half + 1) * 128)
         folded = folded + corner_load[:, :, cut] * intact[None, :, cut]
-    owner = sub_rows[...]
+    owner = spread_rows(tile_sub[...].reshape(1, tiles))
+    subs, corners = corner_map.shape
+    map_rows = spread_rows(jnp.concatenate([corner_map[m : m + 1, :] for m in range(subs)], axis=1))
     sums = []
     for m in range(subs):
-        chosen = jnp.where((owner == m)[None], folded, 0.0)
+        chosen = jnp.where((owner == float(m))[None], folded, 0.0)
         sums.append(jnp.sum(jnp.sum(chosen, axis=1), axis=1, keepdims=True))
     sub_part = jnp.broadcast_to(jnp.concatenate(sums, axis=0), (subs * corners, 128))
-    target = map_rows[...] - lax.broadcasted_iota(jnp.int32, (subs * corners, 128), 1)
+    target = map_rows.astype(jnp.int32) - lax.broadcasted_iota(jnp.int32, (subs * corners, 128), 1)
 
     def scatter(j, carry):
         held = jnp.where(j == lax.axis_index("blk"), external[...], 0.0).reshape(1, 128)
@@ -389,22 +378,22 @@
     tiles, points = strain.shape
     halves = points // 128
     peers = lax.axis_size("blk")
-    subs, corners = corner_map.shape
     params = pltpu.CompilerParams(vmem_limit_bytes=grant)
+    whole_params = pltpu.CompilerParams(vmem_limit_bytes=whole_grant)
     block = 2 * points * points
 
     payload, outbox = pl.pallas_call(
         functools.partial(pack_kernel, peers),
         out_shape=(
             jax.ShapeDtypeStruct((4, tiles, points), f32),
-            jax.ShapeDtypeStruct((peers * 8, points), f32),
+            jax.ShapeDtypeStruct((peers * halves * 8, 128), f32),
         ),
-        in_specs=[in_hbm] * 6,
+        in_specs=[anywhere] * 6,
         out_specs=(in_vmem, in_vmem),
         scratch_shapes=[pltpu.VMEM((tiles, points), f32)]
         + [pltpu.SMEM(v.shape, jnp.int32) for v in (tile_count, send_tile, remote_pairs, remote_count)]
         + [pltpu.SemaphoreType.DMA((6,))],
-        compiler_params=params,
+        compiler_params=whole_params,
         name="pack",
     )(coords, strain, tile_count, send_tile, remote_pairs, remote_count)
 
@@ -416,19 +405,17 @@
     b_own, num, den = pl.pallas_call(
         own_kernel,
         out_shape=(
-            jax.ShapeDtypeStruct((tiles, depth, points), bf16),
+            jax.ShapeDtypeStruct((tiles, 4 * depth, points), bf16),
             jax.ShapeDtypeStruct((tiles, 8, points), f32),
             jax.ShapeDtypeStruct((tiles, 8, points), f32),
         ),
-        in_specs=[in_vmem, in_hbm],
-        out_specs=(in_hbm, in_vmem, in_vmem),
+        in_specs=[in_vmem, anywhere],
+        out_specs=(in_vmem,) * 3,
         scratch_shapes=[
-            pltpu.VMEM((halves, tiles * depth, 128), f32),
+            pltpu.VMEM((halves, tiles * pitch, 128), f32),
             pltpu.VMEM((tiles, points, 4 * depth), bf16),
             pltpu.VMEM((tiles, points, 128), f32),
-            pltpu.VMEM((tiles, 4 * depth, points), bf16),
             pltpu.SMEM(local_pairs.shape, jnp.int32),
-            pltpu.SemaphoreType.DMA((1,)),
             pltpu.SemaphoreType.DMA((1,)),
         ],
         compiler_params=params,
@@ -438,33 +425,26 @@
         name="own",
     )(payload, local_pairs)
 
-    damage, parts = pl.pallas_call(
+    damage, parts, num, den = pl.pallas_call(
         functools.partial(rest_kernel, peers),
         out_shape=(
             jax.ShapeDtypeStruct((tiles, points), f32),
             jax.ShapeDtypeStruct((peers, 128), f32),
+            jax.ShapeDtypeStruct(num.shape, f32),
+            jax.ShapeDtypeStruct(den.shape, f32),
         ),
-        in_specs=[in_hbm] * 15,
-        out_specs=(in_vmem,) * 2,
+        in_specs=[in_vmem] * 12 + [anywhere] * 3,
+        out_specs=(in_vmem,) * 4,
+        input_output_aliases={4: 2, 5: 3},
         scratch_shapes=[
-            pltpu.VMEM((halves, tiles * depth, 128), f32),
-            pltpu.VMEM((halves, 2 * peers * depth, 128), f32),
-            pltpu.VMEM((tiles, 128), jnp.int32),
-            pltpu.VMEM((subs * corners, 128), jnp.int32),
-            pltpu.VMEM(payload.shape, f32),
-            pltpu.VMEM(payload.shape, f32),
-            pltpu.VMEM((halves, peers * 8, 128), f32),
-            pltpu.VMEM((tiles, 4 * depth, points), bf16),
-            pltpu.VMEM(num.shape, f32),
-            pltpu.VMEM(den.shape, f32),
-            pltpu.VMEM(strain.shape, f32),
-            pltpu.VMEM(history.shape, f32),
-            pltpu.VMEM(corner_load.shape, f32),
-            pltpu.VMEM(external.shape, f32),
+            pltpu.VMEM((halves, tiles * pitch, 128), f32),
+            pltpu.VMEM((halves, 2 * peers * pitch, 128), f32),
+            pltpu.VMEM((points, 4 * depth), bf16),
+            pltpu.VMEM((points, 128), f32),
         ]
-        + [pltpu.SMEM(v.shape, jnp.int32) for v in (tile_sub, corner_map, send_tile, remote_pairs, remote_count)]
+        + [pltpu.SMEM(v.shape, jnp.int32) for v in (send_tile, remote_pairs, remote_count)]
         + [pltpu.SMEM((2 * peers,), jnp.int32)] * 2
-        + [pltpu.SemaphoreType.DMA((n,)) for n in (2, 6, 9 + halves)],
+        + [pltpu.SemaphoreType.DMA((3,))],
         compiler_params=params,
         cost_estimate=pl.CostEstimate(
             flops=4 * tiles * block * depth, bytes_accessed=1 << 21, transcendentals=4 * tiles * points * points

time: 49.1 us -> 45.8 us (0.933)
  Pallas kernels: 27.7 us -> 20.2 us
  local copies, waits for them, and re-layouts: 0.69 us -> 4.9 us
    unnamed x6 -> x28, local copies, waits for them, and re-layouts: 0.69 us -> 4.9 us
    pallas_call x1, Pallas kernels: 15.4 us -> 11.3 us  [per_device(): pl.pallas_call(functools.partial(rest_kernel, peers), out_shape=(jax.Shap...]
    pallas_call x1, Pallas kernels: 10.5 us -> 7.13 us  [per_device(): pl.pallas_call(own_kernel, out_shape=(jax.ShapeDtypeStruct((tiles, 4 * de...]
  transfers between devices with their start and end apart: 3 -> 3, of which waited for: 0 -> 0; matrix products, arithmetic and copies ran while one was open for 0% -> 0% of each run, Pallas kernels for 22% -> 16%
where the time goes in v5:
time: 45.8 us; the launch traced here: 45.3 us
  Pallas kernels  20.2 us (44%)
  starting transfers between devices  9.58 us (21%)
  blocking collectives  8.65 us (19%)
  local copies, waits for them, and re-layouts  4.9 us (11%)
  between operations  1.45 us (3%)
  other arithmetic  0.54 us (1%)
    pallas_call x1, Pallas kernels, per_device(): pl.pallas_call(functools.partial(rest_kernel, peers), out_shape=(jax.Shap...  11.3 us
    all_to_all x1, blocking collectives, per_device(): lax.all_to_all(parts, 'blk', split_axis=0, concat_axis=0, tiled=True)  8.65 us
    pallas_call x1, Pallas kernels, per_device(): pl.pallas_call(own_kernel, out_shape=(jax.ShapeDtypeStruct((tiles, 4 * de...  7.13 us
    unnamed x28, local copies, waits for them, and re-layouts  4.9 us
    ppermute x1, starting transfers between devices, per_device(): lax.ppermute(payload, 'sub', [(i, i + 1) for i in range(layers - 1)])  3.92 us
    all_to_all x1, starting transfers between devices, per_device(): lax.all_to_all(outbox, 'blk', split_axis=0, concat_axis=0, tiled=True)  3.74 us
    ppermute x1, starting transfers between devices, per_device(): lax.ppermute(payload, 'sub', [(i + 1, i) for i in range(layers - 1)])  1.92 us
    pallas_call x1, Pallas kernels, per_device(): pl.pallas_call(functools.partial(pack_kernel, peers), out_shape=(jax.Shap...  1.79 us
  transfers between devices with their start and end apart: 3, of which 0 were waited for; matrix products, arithmetic and copies ran while one was open for 0% of the time, Pallas kernels for 16%

profile of v5, /device:TPU:8, one launch (start us, length us, event | category | flops | bytes accessed | tf_op | source)
XLA Modules:
  0.0 45.3 jit_solution(577527458260839164)
XLA Ops:
  1.3 1.8 %pack.1 = (f32[4,32,256]{2,1,0:T(8,128)}, f32[128,128]{1,0:T(8,128)}) custom-call(f32[3,32,256]{2,1,0:T(8,128)} %coords.1, f32[32,256]{1,0:T(8,128)} %strain.1, s32[32]{0:T(128)} %tile_count_in.1, s32[8]{0:T(128)} %send_tile_in.3, s32[2,8]{1,0:T(2,128)} %remote_pairs_in.3, s32[1]{0:T(128)S(6)} %copy.19.remote_count_in), custom_call_target="tpu_custom_call" | custom-call | tf_op jit(solution)/shard_map/pack/pallas_call | solution.py:385
  3.1 1.9 %collective-permute-start.1 = (f32[4,32,256]{2,1,0:T(8,128)}, f32[4,32,256]{2,1,0:T(8,128)S(1)}, u32[]{:S(2)}, u32[]{:S(2)}) collective-permute-start(f32[4,32,256]{2,1,0:T(8,128)} %get-tuple-element.9.payload), channel_id=1, source_target_pairs={{8,0},{16,8},{24,16},{9,1},{17,9},{25,17},{10,2},{18,10},{26,18},{... | collective-permute-start | bytes 393224 | tf_op jit(solution)/shard_map/ppermute | solution.py:402
  5.0 3.9 %collective-permute-start = (f32[4,32,256]{2,1,0:T(8,128)}, f32[4,32,256]{2,1,0:T(8,128)S(1)}, u32[]{:S(2)}, u32[]{:S(2)}) collective-permute-start(f32[4,32,256]{2,1,0:T(8,128)} %get-tuple-element.9.payload), channel_id=1, source_target_pairs={{0,8},{8,16},{16,24},{1,9},{9,17},{17,25},{2,10},{10,18},{18,26},{... | collective-permute-start | bytes 393224 | tf_op jit(solution)/shard_map/ppermute | solution.py:401
  8.9 3.7 %all-to-all-start = ((f32[8,16,128]{2,1,0:T(8,128)}), f32[8,16,128]{2,1,0:T(8,128)S(1)}, u32[]{:S(2)}, u32[]{:S(2)}) async-start(f32[8,16,128]{2,1,0:T(8,128)} %bitcast.7), calls=%async_computation | async-start | bytes 131072 | tf_op jit(solution)/shard_map/all_to_all | solution.py:403
  12.7 0.9 %copy-done.3 = f32[4,32,256]{2,1,0:T(8,128)S(1)} copy-done((f32[4,32,256]{2,1,0:T(8,128)S(1)}, f32[4,32,256]{2,1,0:T(8,128)}, u32[]{:S(2)}) %copy-start.3) | copy-done | bytes 131096
  13.6 0.7 %copy-done.7 = s32[2,32]{1,0:T(2,128)S(1)} copy-done((s32[2,32]{1,0:T(2,128)S(1)}, s32[2,32]{1,0:T(2,128)}, u32[]{:S(2)}) %copy-start.7) | copy-done | bytes 280
  14.3 0.0 copy-start.5
  14.3 0.0 copy-start.6
  14.3 0.0 copy-start.8
  14.3 0.0 copy-start.9
  14.3 7.1 %own.1 = (bf16[32,128,256]{2,1,0:T(8,128)(2,1)S(1)}, f32[32,8,256]{2,1,0:T(8,128)S(1)}, f32[32,8,256]{2,1,0:T(8,128)S(1)}) custom-call(f32[4,32,256]{2,1,0:T(8,128)S(1)} %copy-done.3, s32[2,32]{1,0:T(2,128)S(1)} %copy-done.7), custom_call_target="tpu_custom_call" | custom-call | flops 402653184 | bytes 1048576 | tf_op jit(solution)/shard_map/own/pallas_call | solution.py:405
  21.5 0.0 copy-start.10
  21.5 0.7 %copy-done.10 = f32[32,8,256]{2,1,0:T(8,128)} copy-done((f32[32,8,256]{2,1,0:T(8,128)}, f32[32,8,256]{2,1,0:T(8,128)S(1)}, u32[]{:S(2)}) %copy-start.10) | copy-done | bytes 262168
  22.2 0.7 %copy-done.12 = f32[32,8,256]{2,1,0:T(8,128)} copy-done((f32[32,8,256]{2,1,0:T(8,128)}, f32[32,8,256]{2,1,0:T(8,128)S(1)}, u32[]{:S(2)}) %copy-start.12) | copy-done | bytes 262168
  22.9 0.0 all-to-all-done
  22.9 0.0 collective-permute-done.1.above
  22.9 0.0 collective-permute-done.below
  22.9 0.0 copy-done
  22.9 0.0 copy-done.1
  23.0 0.9 %copy-done.11 = f32[32,8,256]{2,1,0:T(8,128)S(1)} copy-done((f32[32,8,256]{2,1,0:T(8,128)S(1)}, f32[32,8,256]{2,1,0:T(8,128)}, u32[]{:S(2)}) %copy-start.11) | copy-done | bytes 262168
  23.9 0.9 %copy-done.13 = f32[32,8,256]{2,1,0:T(8,128)S(1)} copy-done((f32[32,8,256]{2,1,0:T(8,128)S(1)}, f32[32,8,256]{2,1,0:T(8,128)}, u32[]{:S(2)}) %copy-start.13) | copy-done | bytes 262168
  24.8 11.3 %rest.1 = (f32[32,256]{1,0:T(8,128)}, f32[8,128]{1,0:T(8,128)S(1)}, f32[32,8,256]{2,1,0:T(8,128)S(1)}, f32[32,8,256]{2,1,0:T(8,128)S(1)}) custom-call(f32[4,32,256]{2,1,0:T(8,128)S(1)} %collective-permute-done.below, f32[4,32,256]{2,1,0:T(8,128)S(1)} %collective-permute-done.1.above, ...), custom_call_target="tpu_custom_call", output_to_operand_aliasing={{2}: (4, {}), {3}: (5, {})} | custom-call | flops 536870912 | bytes 2097152 | tf_op jit(solution)/shard_map/rest/pallas_call | solution.py:428
  36.1 8.6 %all_to_all.20 = f32[8,1,128]{2,1,0:T(1,128)S(1)} all-to-all(f32[8,1,128]{2,1,0:T(1,128)S(1)} %bitcast.6), channel_id=1, replica_groups=mesh['sub'=4,'blk'=8] {'blk'}, dimensions={0} | all-to-all | bytes 8192 | tf_op jit(solution)/shard_map/all_to_all | solution.py:470
  44.8 0.5 %reduce_sum.9 = f32[128]{0:T(128)} reduce(f32[8,1,128]{2,1,0:T(1,128)S(1)} %all_to_all.20, f32[]{:T(128)} %constant.0.clone.1), dimensions={0,1}, to_apply=%region_0.0 | reduce | flops 896 | bytes 4612 | tf_op jit(solution)/shard_map/reduce_sum | solution.py:471
  (15 shorter events, 0.0 us)
Async XLA Ops:
  3.1 19.8 %collective-permute-start.1 = (f32[4,32,256]{2,1,0:T(8,128)}, f32[4,32,256]{2,1,0:T(8,128)S(1)}, u32[]{:S(2)}, u32[]{:S(2)}) collective-permute-start(f32[4,32,256]{2,1,0:T(8,128)} %get-tuple-element.9.payload), channel_id=1, source_target_pairs={{8,0},{16,8},{24,16},{9,1},{17,9},{25,17},{10,2},{18,10},{26,18},{... | collective-permute-start | bytes 393224 | tf_op jit(solution)/shard_map/ppermute | solution.py:402
  5.0 17.9 %collective-permute-start = (f32[4,32,256]{2,1,0:T(8,128)}, f32[4,32,256]{2,1,0:T(8,128)S(1)}, u32[]{:S(2)}, u32[]{:S(2)}) collective-permute-start(f32[4,32,256]{2,1,0:T(8,128)} %get-tuple-element.9.payload), channel_id=1, source_target_pairs={{0,8},{8,16},{16,24},{1,9},{9,17},{17,25},{2,10},{10,18},{18,26},{... | collective-permute-start | bytes 393224 | tf_op jit(solution)/shard_map/ppermute | solution.py:401
  8.9 13.9 %all-to-all-start = ((f32[8,16,128]{2,1,0:T(8,128)}), f32[8,16,128]{2,1,0:T(8,128)S(1)}, u32[]{:S(2)}, u32[]{:S(2)}) async-start(f32[8,16,128]{2,1,0:T(8,128)} %bitcast.7), calls=%async_computation | async-start | bytes 131072 | tf_op jit(solution)/shard_map/all_to_all | solution.py:403
  12.7 0.9 %copy-start.3 = (f32[4,32,256]{2,1,0:T(8,128)S(1)}, f32[4,32,256]{2,1,0:T(8,128)}, u32[]{:S(2)}) copy-start(f32[4,32,256]{2,1,0:T(8,128)} %get-tuple-element.9.payload) | copy-start | bytes 393220
  13.6 0.7 %copy-start.7 = (s32[2,32]{1,0:T(2,128)S(1)}, s32[2,32]{1,0:T(2,128)}, u32[]{:S(2)}) copy-start(s32[2,32]{1,0:T(2,128)} %local_pairs_in.1) | copy-start | bytes 772
  14.3 8.6 %copy-start = (s32[2,8]{1,0:T(2,128)S(1)}, s32[2,8]{1,0:T(2,128)}, u32[]{:S(2)}) copy-start(s32[2,8]{1,0:T(2,128)} %remote_pairs_in.3) | copy-start | bytes 196
  14.3 8.6 %copy-start.1 = (s32[8]{0:T(128)S(1)}, s32[8]{0:T(128)}, u32[]{:S(2)}) copy-start(s32[8]{0:T(128)} %send_tile_in.3) | copy-start | bytes 100
  14.3 8.6 %copy-start.2 = (f32[24,32,256]{2,1,0:T(8,128)S(1)}, f32[24,32,256]{2,1,0:T(8,128)}, u32[]{:S(2)}) copy-start(f32[24,32,256]{2,1,0:T(8,128)} %corner_load.1) | copy-start | bytes 2359300
  14.3 8.6 %copy-start.4 = (f32[4,32,256]{2,1,0:T(8,128)S(1)}, f32[4,32,256]{2,1,0:T(8,128)}, u32[]{:S(2)}) copy-start(f32[4,32,256]{2,1,0:T(8,128)} %get-tuple-element.9.payload) | copy-start | bytes 393220
  14.3 8.6 %copy-start.5 = (f32[32,256]{1,0:T(8,128)S(1)}, f32[32,256]{1,0:T(8,128)}, u32[]{:S(2)}) copy-start(f32[32,256]{1,0:T(8,128)} %history.1) | copy-start | bytes 98308
  14.3 8.6 %copy-start.6 = (s32[4,24]{1,0:T(4,128)S(1)}, s32[4,24]{1,0:T(4,128)}, u32[]{:S(2)}) copy-start(s32[4,24]{1,0:T(4,128)} %corner_map.1) | copy-start | bytes 1156
  14.3 8.6 %copy-start.8 = (f32[128]{0:T(128)S(1)}, f32[128]{0:T(128)}, u32[]{:S(2)}) copy-start(f32[128]{0:T(128)} %external.1) | copy-start | bytes 1540
  14.3 8.6 %copy-start.9 = (s32[32]{0:T(128)S(1)}, s32[32]{0:T(128)}, u32[]{:S(2)}) copy-start(s32[32]{0:T(128)} %tile_sub.1) | copy-start | bytes 388
  21.5 0.7 %copy-start.10 = (f32[32,8,256]{2,1,0:T(8,128)}, f32[32,8,256]{2,1,0:T(8,128)S(1)}, u32[]{:S(2)}) copy-start(f32[32,8,256]{2,1,0:T(8,128)S(1)} %get-tuple-element.12.num_in) | copy-start | bytes 786436
  22.2 0.7 %copy-start.12 = (f32[32,8,256]{2,1,0:T(8,128)}, f32[32,8,256]{2,1,0:T(8,128)S(1)}, u32[]{:S(2)}) copy-start(f32[32,8,256]{2,1,0:T(8,128)S(1)} %get-tuple-element.13.den_in) | copy-start | bytes 786436
  22.9 1.0 %copy-start.11 = (f32[32,8,256]{2,1,0:T(8,128)S(1)}, f32[32,8,256]{2,1,0:T(8,128)}, u32[]{:S(2)}) copy-start(f32[32,8,256]{2,1,0:T(8,128)} %copy-done.10) | copy-start | bytes 786436
  23.9 0.9 %copy-start.13 = (f32[32,8,256]{2,1,0:T(8,128)S(1)}, f32[32,8,256]{2,1,0:T(8,128)}, u32[]{:S(2)}) copy-start(f32[32,8,256]{2,1,0:T(8,128)} %copy-done.12) | copy-start | bytes 786436

commit v6 on v5

--- a/solution.py
+++ b/solution.py
@@ -43,13 +43,12 @@
     scaled = [p * coord_scale for p in planes[:3]]
     split = [pieces(s) for s in scaled]
     norm = scaled[0] * scaled[0] + scaled[1] * scaled[1] + scaled[2] * scaled[2]
-    return split, norm
+    return split, norm + jnp.where(planes[3] > 0.0, 0.0, far_off)
 
 
 def put_source(planes, rows_ref, base):
     split, norm = point_rows(planes)
     ones = jnp.ones_like(norm)
-    norm = norm + jnp.where(planes[3] > 0.0, 0.0, far_off)
     rows = []
     for high, middle, low in split:
         rows += [high, high, middle, high, low, middle]
@@ -87,14 +86,26 @@
     return operands
 
 
+def fold(x):
+    return jnp.sum(x.reshape(x.shape[0] // 8, 8, x.shape[1]), axis=0)
+
+
+def column_sums(weight, s):
+    load = jnp.concatenate([s] * (weight.shape[1] // 128), axis=1)
+    return fold(weight * load), fold(weight)
+
+
 def pair_sums(a, s, b):
-    points = a.shape[0]
-    width = b.shape[1]
+    return column_sums(jnp.exp2(jnp.dot(a, b, preferred_element_type=f32)), s)
+
+
+def both_sums(a, s, b, s_row):
     weight = jnp.exp2(jnp.dot(a, b, preferred_element_type=f32))
-    load = jnp.concatenate([s] * (width // 128), axis=1)
-    den = jnp.sum(weight.reshape(points // 8, 8, width), axis=0)
-    num = jnp.sum((weight * load).reshape(points // 8, 8, width), axis=0)
-    return num, den
+    cuts = [slice(lo, lo + 128) for lo in range(0, weight.shape[1], 128)]
+    den_row = sum(weight[:, cut] for cut in cuts)
+    num_row = sum(weight[:, cut] * s_row[:, cut] for cut in cuts)
+    turned = [jnp.concatenate([fold(x[cut].T) for cut in cuts], axis=1) for x in (num_row, den_row)]
+    return column_sums(weight, s), turned
 
 
 def fetch(sources, targets, sems):
@@ -112,6 +123,7 @@
     send_tile_in,
     remote_pairs_in,
     remote_count_in,
+    local_pairs_in,
     payload,
     outbox,
     strain_here,
@@ -119,16 +131,19 @@
     send_tile,
     remote_pairs,
     remote_count,
+    local_pairs,
     sems,
 ):
     tiles, points = strain.shape
     copies = fetch(
-        (coords, strain, tile_count_in, send_tile_in, remote_pairs_in, remote_count_in),
-        (payload.at[0:3], strain_here, tile_count, send_tile, remote_pairs, remote_count),
+        (coords, strain, tile_count_in, send_tile_in, remote_pairs_in, remote_count_in, local_pairs_in),
+        (payload.at[0:3], strain_here, tile_count, send_tile, remote_pairs, remote_count, local_pairs),
         sems,
     )
+    payload[4] = jnp.zeros((tiles, points), f32)
     for copy in copies:
         copy.wait()
+    payload[4, 0:2, 0 : local_pairs.shape[1]] = local_pairs[...].astype(f32)
     lane = lax.broadcasted_iota(jnp.int32, (1, points), 1)
     for t in range(tiles):
         payload[3, t : t + 1, :] = jnp.where(lane < tile_count[t], strain_here[t : t + 1, :], 0.0)
@@ -161,9 +176,9 @@
     return jnp.broadcast_to(wide, (128, 128)).T[0:n]
 
 
-def own_kernel(payload, local_pairs_in, b_ref, num_ref, den_ref, rows_ref, a_ref, s_ref, local_pairs, sems):
+def own_kernel(pairs, payload, b_ref, num_ref, den_ref, rows_ref, a_ref, s_ref, local_pairs, sems):
     tiles = payload.shape[1]
-    copies = fetch((local_pairs_in,), (local_pairs,), sems)
+    copies = fetch((payload.at[4, 0:8, 0:128],), (local_pairs,), sems)
     planes = [payload[k] for k in range(4)]
     put_target(planes, rows_ref)
 
@@ -196,16 +211,17 @@
     def listed(step, carry):
         group = []
         for i in range(4):
-            one = local_pairs[0, step * 4 + i]
-            two = local_pairs[1, step * 4 + i]
-            group += [(one, two), (two, one)]
-        sums = [pair_sums(a_ref[src], s_ref[src], b_ref[dst]) for src, dst in group]
-        for (src, dst), (num, den) in zip(group, sums):
-            num_ref[dst] = num_ref[dst] + num
-            den_ref[dst] = den_ref[dst] + den
-        return carry
-
-    lax.fori_loop(0, local_pairs.shape[1] // 4, listed, 0)
+            one = local_pairs[0, step * 4 + i].astype(jnp.int32)
+            two = local_pairs[1, step * 4 + i].astype(jnp.int32)
+            group.append((one, two))
+        sums = [both_sums(a_ref[one], s_ref[one], b_ref[two], payload[3, pl.ds(two, 1), :]) for one, two in group]
+        for (one, two), (for_two, for_one) in zip(group, sums):
+            for t, (num, den) in ((two, for_two), (one, for_one)):
+                num_ref[t] = num_ref[t] + num
+                den_ref[t] = den_ref[t] + den
+        return carry
+
+    lax.fori_loop(0, pairs // 4, listed, 0)
 
 
 def rest_kernel(
@@ -227,12 +243,10 @@
     remote_count_in,
     damage_ref,
     parts_ref,
+    rows_ref,
+    far_rows,
     num_ref,
     den_ref,
-    rows_ref,
-    far_rows,
-    last_a,
-    last_s,
     send_tile,
     remote_pairs,
     remote_count,
@@ -251,38 +265,23 @@
         sems,
     )
 
+    num_ref[...] = num_in[...]
+    den_ref[...] = den_in[...]
+
     def border(shift):
-        def turned(step):
-            group = step if shift < 0 else groups - 1 - step
-            return group, turn_group(rows_ref, group)
-
-        edge = 3 if shift < 0 else 0
-
-        def keep(operands):
-            last_a[...] = operands[edge][0]
-            last_s[...] = operands[edge][1]
-
-        keep(turned(groups - 1)[1])
-
-        def some(step, carry):
-            group, operands = turned(step)
-            outer = (last_a[...], last_s[...])
-            sums = []
-            for i in range(4):
-                a, s = operands[i]
-                more_a, more_s = operands[i + shift] if 0 <= i + shift < 4 else outer
-                sums.append(
-                    pair_sums(
-                        jnp.concatenate([a, more_a], axis=0),
-                        jnp.concatenate([s, more_s], axis=0),
-                        b_ref[group * 4 + i],
-                    )
-                )
-            for i, (num, den) in enumerate(sums):
-                t = group * 4 + i
+        def some(group, carry):
+            sums = {}
+            for i, (a, s) in enumerate(turn_group(rows_ref, group)):
+                places = (i, i + shift)
+                targets = [lax.rem(group * 4 + place + tiles, tiles) for place in places]
+                num, den = pair_sums(a, s, jnp.concatenate([b_ref[t] for t in targets], axis=1))
+                for j, (place, t) in enumerate(zip(places, targets)):
+                    cut = slice(j * points, (j + 1) * points)
+                    held = sums.get(place, (t, 0.0, 0.0))
+                    sums[place] = (t, held[1] + num[:, cut], held[2] + den[:, cut])
+            for t, num, den in sums.values():
                 num_ref[t] = num_ref[t] + num
                 den_ref[t] = den_ref[t] + den
-            keep(operands)
             return carry
 
         lax.fori_loop(0, groups, some, 0)
@@ -290,12 +289,12 @@
     @pl.when(layer > 0)
     def lower():
         put_source([below[k] for k in range(4)], rows_ref, 0)
-        border(1)
+        border(-1)
 
     @pl.when(layer < count - 1)
     def upper():
         put_source([above[k] for k in range(4)], rows_ref, 0)
-        border(-1)
+        border(1)
 
     for copy in copies:
         copy.wait()
@@ -385,17 +384,17 @@
     payload, outbox = pl.pallas_call(
         functools.partial(pack_kernel, peers),
         out_shape=(
-            jax.ShapeDtypeStruct((4, tiles, points), f32),
+            jax.ShapeDtypeStruct((5, tiles, points), f32),
             jax.ShapeDtypeStruct((peers * halves * 8, 128), f32),
         ),
-        in_specs=[anywhere] * 6,
+        in_specs=[anywhere] * 7,
         out_specs=(in_vmem, in_vmem),
         scratch_shapes=[pltpu.VMEM((tiles, points), f32)]
         + [pltpu.SMEM(v.shape, jnp.int32) for v in (tile_count, send_tile, remote_pairs, remote_count)]
-        + [pltpu.SemaphoreType.DMA((6,))],
+        + [pltpu.VMEM(local_pairs.shape, jnp.int32), pltpu.SemaphoreType.DMA((7,))],
         compiler_params=whole_params,
         name="pack",
-    )(coords, strain, tile_count, send_tile, remote_pairs, remote_count)
+    )(coords, strain, tile_count, send_tile, remote_pairs, remote_count, local_pairs)
 
     layers = lax.axis_size("sub")
     below = lax.ppermute(payload, "sub", [(i, i + 1) for i in range(layers - 1)])
@@ -403,19 +402,19 @@
     inbox = lax.all_to_all(outbox, "blk", split_axis=0, concat_axis=0, tiled=True)
 
     b_own, num, den = pl.pallas_call(
-        own_kernel,
+        functools.partial(own_kernel, local_pairs.shape[1]),
         out_shape=(
             jax.ShapeDtypeStruct((tiles, 4 * depth, points), bf16),
             jax.ShapeDtypeStruct((tiles, 8, points), f32),
             jax.ShapeDtypeStruct((tiles, 8, points), f32),
         ),
-        in_specs=[in_vmem, anywhere],
+        in_specs=[in_vmem],
         out_specs=(in_vmem,) * 3,
         scratch_shapes=[
             pltpu.VMEM((halves, tiles * pitch, 128), f32),
             pltpu.VMEM((tiles, points, 4 * depth), bf16),
             pltpu.VMEM((tiles, points, 128), f32),
-            pltpu.SMEM(local_pairs.shape, jnp.int32),
+            pltpu.SMEM((8, 128), f32),
             pltpu.SemaphoreType.DMA((1,)),
         ],
         compiler_params=params,
@@ -423,24 +422,21 @@
             flops=3 * tiles * block * depth, bytes_accessed=1 << 20, transcendentals=3 * tiles * points * points
         ),
         name="own",
-    )(payload, local_pairs)
-
-    damage, parts, num, den = pl.pallas_call(
+    )(payload)
+
+    damage, parts = pl.pallas_call(
         functools.partial(rest_kernel, peers),
         out_shape=(
             jax.ShapeDtypeStruct((tiles, points), f32),
             jax.ShapeDtypeStruct((peers, 128), f32),
-            jax.ShapeDtypeStruct(num.shape, f32),
-            jax.ShapeDtypeStruct(den.shape, f32),
         ),
         in_specs=[in_vmem] * 12 + [anywhere] * 3,
-        out_specs=(in_vmem,) * 4,
-        input_output_aliases={4: 2, 5: 3},
+        out_specs=(in_vmem,) * 2,
         scratch_shapes=[
             pltpu.VMEM((halves, tiles * pitch, 128), f32),
             pltpu.VMEM((halves, 2 * peers * pitch, 128), f32),
-            pltpu.VMEM((points, 4 * depth), bf16),
-            pltpu.VMEM((points, 128), f32),
+            pltpu.VMEM(num.shape, f32),
+            pltpu.VMEM(den.shape, f32),
         ]
         + [pltpu.SMEM(v.shape, jnp.int32) for v in (send_tile, remote_pairs, remote_count)]
         + [pltpu.SMEM((2 * peers,), jnp.int32)] * 2

time: 45.8 us -> 45.7 us (level)
  Pallas kernels: 20.2 us -> 20.9 us
  local copies, waits for them, and re-layouts: 4.9 us -> 4.21 us
    pallas_call x1, Pallas kernels: 7.13 us -> 8.03 us  [per_device(): pl.pallas_call(functools.partial(own_kernel, local_pairs.shape[1]), out_s...]
    unnamed x28 -> x26, local copies, waits for them, and re-layouts: 4.9 us -> 4.21 us
  transfers between devices with their start and end apart: 3 -> 3, of which waited for: 0 -> 0; matrix products, arithmetic and copies ran while one was open for 0% -> 0% of each run, Pallas kernels for 16% -> 18%
where the time goes in v6:
time: 45.7 us; the launch traced here: 45.3 us
  Pallas kernels  20.9 us (46%)
  starting transfers between devices  9.58 us (21%)
  blocking collectives  8.65 us (19%)
  local copies, waits for them, and re-layouts  4.21 us (9%)
  between operations  1.44 us (3%)
  other arithmetic  0.54 us (1%)
    pallas_call x1, Pallas kernels, per_device(): pl.pallas_call(functools.partial(rest_kernel, peers), out_shape=(jax.Shap...  11 us
    all_to_all x1, blocking collectives, per_device(): lax.all_to_all(parts, 'blk', split_axis=0, concat_axis=0, tiled=True)  8.65 us
    pallas_call x1, Pallas kernels, per_device(): pl.pallas_call(functools.partial(own_kernel, local_pairs.shape[1]), out_s...  8.03 us
    unnamed x26, local copies, waits for them, and re-layouts  4.21 us
    ppermute x1, starting transfers between devices, per_device(): lax.ppermute(payload, 'sub', [(i, i + 1) for i in range(layers - 1)])  3.92 us
    all_to_all x1, starting transfers between devices, per_device(): lax.all_to_all(outbox, 'blk', split_axis=0, concat_axis=0, tiled=True)  3.74 us
    ppermute x1, starting transfers between devices, per_device(): lax.ppermute(payload, 'sub', [(i + 1, i) for i in range(layers - 1)])  1.92 us
    pallas_call x1, Pallas kernels, per_device(): pl.pallas_call(functools.partial(pack_kernel, peers), out_shape=(jax.Shap...  1.8 us
  transfers between devices with their start and end apart: 3, of which 0 were waited for; matrix products, arithmetic and copies ran while one was open for 0% of the time, Pallas kernels for 18%

profile of v6, /device:TPU:8, one launch (start us, length us, event | category | flops | bytes accessed | tf_op | source)
XLA Modules:
  0.0 45.3 jit_solution(14493018159357416215)
XLA Ops:
  1.3 1.8 %pack.1 = (f32[5,32,256]{2,1,0:T(8,128)}, f32[128,128]{1,0:T(8,128)}) custom-call(f32[3,32,256]{2,1,0:T(8,128)} %coords.1, f32[32,256]{1,0:T(8,128)} %strain.1, s32[32]{0:T(128)} %tile_count_in.1, s32[8]{0:T(128)} %send_tile_in.3, s32[2,8]{1,0:T(2,128)} %remote_pairs_in.3, s32[1]{0:T(128)S(6)} %copy.15.remote_count_in, s32[2,32]{1,0:T(2,128)} %local_pairs_in.1), custom_call_target="tpu_custom_call" | custom-call | tf_op jit(solution)/shard_map/pack/pallas_call | solution.py:384
  3.1 1.9 %collective-permute-start.1 = (f32[5,32,256]{2,1,0:T(8,128)}, f32[5,32,256]{2,1,0:T(8,128)S(1)}, u32[]{:S(2)}, u32[]{:S(2)}) collective-permute-start(f32[5,32,256]{2,1,0:T(8,128)} %get-tuple-element.9.payload), channel_id=1, source_target_pairs={{8,0},{16,8},{24,16},{9,1},{17,9},{25,17},{10,2},{18,10},{26,18},{... | collective-permute-start | bytes 491528 | tf_op jit(solution)/shard_map/ppermute | solution.py:401
  5.0 3.9 %collective-permute-start = (f32[5,32,256]{2,1,0:T(8,128)}, f32[5,32,256]{2,1,0:T(8,128)S(1)}, u32[]{:S(2)}, u32[]{:S(2)}) collective-permute-start(f32[5,32,256]{2,1,0:T(8,128)} %get-tuple-element.9.payload), channel_id=1, source_target_pairs={{0,8},{8,16},{16,24},{1,9},{9,17},{17,25},{2,10},{10,18},{18,26},{... | collective-permute-start | bytes 491528 | tf_op jit(solution)/shard_map/ppermute | solution.py:400
  8.9 3.7 %all-to-all-start = ((f32[8,16,128]{2,1,0:T(8,128)}), f32[8,16,128]{2,1,0:T(8,128)S(1)}, u32[]{:S(2)}, u32[]{:S(2)}) async-start(f32[8,16,128]{2,1,0:T(8,128)} %bitcast.7), calls=%async_computation | async-start | bytes 131072 | tf_op jit(solution)/shard_map/all_to_all | solution.py:402
  12.7 0.9 %copy-done.3 = f32[5,32,256]{2,1,0:T(8,128)S(1)} copy-done((f32[5,32,256]{2,1,0:T(8,128)S(1)}, f32[5,32,256]{2,1,0:T(8,128)}, u32[]{:S(2)}) %copy-start.3) | copy-done | bytes 163864
  13.6 0.0 copy-start.5
  13.6 0.0 copy-start.6
  13.6 0.0 copy-start.7
  13.6 0.0 copy-start.8
  13.7 8.0 %own.1 = (bf16[32,128,256]{2,1,0:T(8,128)(2,1)S(1)}, f32[32,8,256]{2,1,0:T(8,128)S(1)}, f32[32,8,256]{2,1,0:T(8,128)S(1)}) custom-call(f32[5,32,256]{2,1,0:T(8,128)S(1)} %copy-done.3), custom_call_target="tpu_custom_call" | custom-call | flops 402653184 | bytes 1048576 | tf_op jit(solution)/shard_map/own/pallas_call | solution.py:404
  21.7 0.0 copy-start.9
  21.7 0.7 %copy-done.9 = f32[32,8,256]{2,1,0:T(8,128)} copy-done((f32[32,8,256]{2,1,0:T(8,128)}, f32[32,8,256]{2,1,0:T(8,128)S(1)}, u32[]{:S(2)}) %copy-start.9) | copy-done | bytes 262168
  22.4 0.7 %copy-done.11 = f32[32,8,256]{2,1,0:T(8,128)} copy-done((f32[32,8,256]{2,1,0:T(8,128)}, f32[32,8,256]{2,1,0:T(8,128)S(1)}, u32[]{:S(2)}) %copy-start.11) | copy-done | bytes 262168
  23.1 0.0 all-to-all-done
  23.1 0.0 collective-permute-done.1.above
  23.1 0.0 collective-permute-done.below
  23.1 0.0 copy-done
  23.1 0.0 copy-done.1
  23.1 0.0 copy-done.2
  23.2 0.9 %copy-done.10 = f32[32,8,256]{2,1,0:T(8,128)S(1)} copy-done((f32[32,8,256]{2,1,0:T(8,128)S(1)}, f32[32,8,256]{2,1,0:T(8,128)}, u32[]{:S(2)}) %copy-start.10) | copy-done | bytes 262168
  24.1 0.9 %copy-done.12 = f32[32,8,256]{2,1,0:T(8,128)S(1)} copy-done((f32[32,8,256]{2,1,0:T(8,128)S(1)}, f32[32,8,256]{2,1,0:T(8,128)}, u32[]{:S(2)}) %copy-start.12) | copy-done | bytes 262168
  25.1 11.0 %rest.1 = (f32[32,256]{1,0:T(8,128)}, f32[8,128]{1,0:T(8,128)S(1)}) custom-call(f32[5,32,256]{2,1,0:T(8,128)S(1)} %collective-permute-done.below, f32[5,32,256]{2,1,0:T(8,128)S(1)} %collective-permute-done.1.above, f32[128,128]{1,0:T(8,128)S(1)} %bitcast.5, bf16[32,128,256]{2,1,0:T(8,128)(2,1)S(1)} %get-tuple-element.11.b_ref, f32[32,8,256]{2,1,0:T(8,128)S(1)} %copy-done.10, ...), custom_call_target="tpu_custom_call" | custom-call | flops 536870912 | bytes 2097152 | tf_op jit(solution)/shard_map/rest/pallas_call | solution.py:427
  36.1 8.7 %all_to_all.20 = f32[8,1,128]{2,1,0:T(1,128)S(1)} all-to-all(f32[8,1,128]{2,1,0:T(1,128)S(1)} %bitcast.6), channel_id=1, replica_groups=mesh['sub'=4,'blk'=8] {'blk'}, dimensions={0} | all-to-all | bytes 8192 | tf_op jit(solution)/shard_map/all_to_all | solution.py:466
  44.8 0.5 %reduce_sum.9 = f32[128]{0:T(128)} reduce(f32[8,1,128]{2,1,0:T(1,128)S(1)} %all_to_all.20, f32[]{:T(128)} %constant.0.clone.1), dimensions={0,1}, to_apply=%region_0.0 | reduce | flops 896 | bytes 4612 | tf_op jit(solution)/shard_map/reduce_sum | solution.py:467
  (13 shorter events, 0.0 us)
Async XLA Ops:
  3.1 20.0 %collective-permute-start.1 = (f32[5,32,256]{2,1,0:T(8,128)}, f32[5,32,256]{2,1,0:T(8,128)S(1)}, u32[]{:S(2)}, u32[]{:S(2)}) collective-permute-start(f32[5,32,256]{2,1,0:T(8,128)} %get-tuple-element.9.payload), channel_id=1, source_target_pairs={{8,0},{16,8},{24,16},{9,1},{17,9},{25,17},{10,2},{18,10},{26,18},{... | collective-permute-start | bytes 491528 | tf_op jit(solution)/shard_map/ppermute | solution.py:401
  5.0 18.1 %collective-permute-start = (f32[5,32,256]{2,1,0:T(8,128)}, f32[5,32,256]{2,1,0:T(8,128)S(1)}, u32[]{:S(2)}, u32[]{:S(2)}) collective-permute-start(f32[5,32,256]{2,1,0:T(8,128)} %get-tuple-element.9.payload), channel_id=1, source_target_pairs={{0,8},{8,16},{16,24},{1,9},{9,17},{17,25},{2,10},{10,18},{18,26},{... | collective-permute-start | bytes 491528 | tf_op jit(solution)/shard_map/ppermute | solution.py:400
  8.9 14.1 %all-to-all-start = ((f32[8,16,128]{2,1,0:T(8,128)}), f32[8,16,128]{2,1,0:T(8,128)S(1)}, u32[]{:S(2)}, u32[]{:S(2)}) async-start(f32[8,16,128]{2,1,0:T(8,128)} %bitcast.7), calls=%async_computation | async-start | bytes 131072 | tf_op jit(solution)/shard_map/all_to_all | solution.py:402
  12.7 0.9 %copy-start.3 = (f32[5,32,256]{2,1,0:T(8,128)S(1)}, f32[5,32,256]{2,1,0:T(8,128)}, u32[]{:S(2)}) copy-start(f32[5,32,256]{2,1,0:T(8,128)} %get-tuple-element.9.payload) | copy-start | bytes 491524
  13.6 9.5 %copy-start = (s32[2,8]{1,0:T(2,128)S(1)}, s32[2,8]{1,0:T(2,128)}, u32[]{:S(2)}) copy-start(s32[2,8]{1,0:T(2,128)} %remote_pairs_in.3) | copy-start | bytes 196
  13.6 9.5 %copy-start.1 = (s32[8]{0:T(128)S(1)}, s32[8]{0:T(128)}, u32[]{:S(2)}) copy-start(s32[8]{0:T(128)} %send_tile_in.3) | copy-start | bytes 100
  13.6 9.5 %copy-start.2 = (f32[24,32,256]{2,1,0:T(8,128)S(1)}, f32[24,32,256]{2,1,0:T(8,128)}, u32[]{:S(2)}) copy-start(f32[24,32,256]{2,1,0:T(8,128)} %corner_load.1) | copy-start | bytes 2359300
  13.6 9.5 %copy-start.4 = (f32[5,32,256]{2,1,0:T(8,128)S(1)}, f32[5,32,256]{2,1,0:T(8,128)}, u32[]{:S(2)}) copy-start(f32[5,32,256]{2,1,0:T(8,128)} %get-tuple-element.9.payload) | copy-start | bytes 491524
  13.6 9.5 %copy-start.5 = (f32[32,256]{1,0:T(8,128)S(1)}, f32[32,256]{1,0:T(8,128)}, u32[]{:S(2)}) copy-start(f32[32,256]{1,0:T(8,128)} %history.1) | copy-start | bytes 98308
  13.6 9.5 %copy-start.6 = (s32[4,24]{1,0:T(4,128)S(1)}, s32[4,24]{1,0:T(4,128)}, u32[]{:S(2)}) copy-start(s32[4,24]{1,0:T(4,128)} %corner_map.1) | copy-start | bytes 1156
  13.6 9.5 %copy-start.7 = (f32[128]{0:T(128)S(1)}, f32[128]{0:T(128)}, u32[]{:S(2)}) copy-start(f32[128]{0:T(128)} %external.1) | copy-start | bytes 1540
  13.6 9.5 %copy-start.8 = (s32[32]{0:T(128)S(1)}, s32[32]{0:T(128)}, u32[]{:S(2)}) copy-start(s32[32]{0:T(128)} %tile_sub.1) | copy-start | bytes 388
  21.7 0.7 %copy-start.9 = (f32[32,8,256]{2,1,0:T(8,128)}, f32[32,8,256]{2,1,0:T(8,128)S(1)}, u32[]{:S(2)}) copy-start(f32[32,8,256]{2,1,0:T(8,128)S(1)} %get-tuple-element.12.num_in) | copy-start | bytes 786436
  22.4 0.7 %copy-start.11 = (f32[32,8,256]{2,1,0:T(8,128)}, f32[32,8,256]{2,1,0:T(8,128)S(1)}, u32[]{:S(2)}) copy-start(f32[32,8,256]{2,1,0:T(8,128)S(1)} %get-tuple-element.13.den_in) | copy-start | bytes 786436
  23.2 1.0 %copy-start.10 = (f32[32,8,256]{2,1,0:T(8,128)S(1)}, f32[32,8,256]{2,1,0:T(8,128)}, u32[]{:S(2)}) copy-start(f32[32,8,256]{2,1,0:T(8,128)} %copy-done.9) | copy-start | bytes 786436
  24.1 0.9 %copy-start.12 = (f32[32,8,256]{2,1,0:T(8,128)S(1)}, f32[32,8,256]{2,1,0:T(8,128)}, u32[]{:S(2)}) copy-start(f32[32,8,256]{2,1,0:T(8,128)} %copy-done.11) | copy-start | bytes 786436

commit v7 on v6

--- a/solution.py
+++ b/solution.py
@@ -11,11 +11,11 @@
 gauss_rate = 4.0
 keep_share = 0.05
 softening = 0.5
-coord_scale = math.sqrt(gauss_rate * math.log2(math.e))
+coord_scale = math.sqrt(gauss_rate)
 far_off = 2048.0
 depth = 32
 pitch = depth + 1
-grant = 24 * 1024 * 1024
+grant = 48 * 1024 * 1024
 whole_grant = 60 * 1024 * 1024
 
 f32 = jnp.float32
@@ -95,17 +95,13 @@
     return fold(weight * load), fold(weight)
 
 
-def pair_sums(a, s, b):
-    return column_sums(jnp.exp2(jnp.dot(a, b, preferred_element_type=f32)), s)
-
-
-def both_sums(a, s, b, s_row):
-    weight = jnp.exp2(jnp.dot(a, b, preferred_element_type=f32))
-    cuts = [slice(lo, lo + 128) for lo in range(0, weight.shape[1], 128)]
-    den_row = sum(weight[:, cut] for cut in cuts)
-    num_row = sum(weight[:, cut] * s_row[:, cut] for cut in cuts)
-    turned = [jnp.concatenate([fold(x[cut].T) for cut in cuts], axis=1) for x in (num_row, den_row)]
-    return column_sums(weight, s), turned
+def pair_sums(a, s, b, step):
+    num, den = 0.0, 0.0
+    for lo in range(0, a.shape[0], step):
+        weight = jnp.exp(jnp.dot(a[lo : lo + step], b, preferred_element_type=f32))
+        more_num, more_den = column_sums(weight, s[lo : lo + step])
+        num, den = num + more_num, den + more_den
+    return num, den
 
 
 def fetch(sources, targets, sems):
@@ -176,7 +172,7 @@
     return jnp.broadcast_to(wide, (128, 128)).T[0:n]
 
 
-def own_kernel(pairs, payload, b_ref, num_ref, den_ref, rows_ref, a_ref, s_ref, local_pairs, sems):
+def own_kernel(pairs, payload, b_ref, sums_ref, rows_ref, a_ref, s_ref, local_pairs, sems):
     tiles = payload.shape[1]
     copies = fetch((payload.at[4, 0:8, 0:128],), (local_pairs,), sems)
     planes = [payload[k] for k in range(4)]
@@ -201,9 +197,9 @@
             t = group * 4 + i
             a_ref[t] = a
             s_ref[t] = s
-            num, den = pair_sums(a, s, b_ref[t])
-            num_ref[t] = num
-            den_ref[t] = den
+            num, den = pair_sums(a, s, b_ref[t], 64)
+            sums_ref[0, t] = num
+            sums_ref[1, t] = den
         return carry
 
     lax.fori_loop(0, tiles // 4, own, 0)
@@ -213,12 +209,11 @@
         for i in range(4):
             one = local_pairs[0, step * 4 + i].astype(jnp.int32)
             two = local_pairs[1, step * 4 + i].astype(jnp.int32)
-            group.append((one, two))
-        sums = [both_sums(a_ref[one], s_ref[one], b_ref[two], payload[3, pl.ds(two, 1), :]) for one, two in group]
-        for (one, two), (for_two, for_one) in zip(group, sums):
-            for t, (num, den) in ((two, for_two), (one, for_one)):
-                num_ref[t] = num_ref[t] + num
-                den_ref[t] = den_ref[t] + den
+            group += [(one, two), (two, one)]
+        sums = [pair_sums(a_ref[src], s_ref[src], b_ref[dst], 64) for src, dst in group]
+        for (src, dst), (num, den) in zip(group, sums):
+            sums_ref[0, dst] = sums_ref[0, dst] + num
+            sums_ref[1, dst] = sums_ref[1, dst] + den
         return carry
 
     lax.fori_loop(0, pairs // 4, listed, 0)
@@ -230,8 +225,7 @@
     above,
     inbox,
     b_ref,
-    num_in,
-    den_in,
+    sums_in,
     payload,
     history,
     corner_load,
@@ -245,8 +239,7 @@
     parts_ref,
     rows_ref,
     far_rows,
-    num_ref,
-    den_ref,
+    sums_ref,
     send_tile,
     remote_pairs,
     remote_count,
@@ -265,8 +258,7 @@
         sems,
     )
 
-    num_ref[...] = num_in[...]
-    den_ref[...] = den_in[...]
+    sums_ref[...] = sums_in[...]
 
     def border(shift):
         def some(group, carry):
@@ -274,14 +266,14 @@
             for i, (a, s) in enumerate(turn_group(rows_ref, group)):
                 places = (i, i + shift)
                 targets = [lax.rem(group * 4 + place + tiles, tiles) for place in places]
-                num, den = pair_sums(a, s, jnp.concatenate([b_ref[t] for t in targets], axis=1))
+                num, den = pair_sums(a, s, jnp.concatenate([b_ref[t] for t in targets], axis=1), points)
                 for j, (place, t) in enumerate(zip(places, targets)):
                     cut = slice(j * points, (j + 1) * points)
                     held = sums.get(place, (t, 0.0, 0.0))
                     sums[place] = (t, held[1] + num[:, cut], held[2] + den[:, cut])
             for t, num, den in sums.values():
-                num_ref[t] = num_ref[t] + num
-                den_ref[t] = den_ref[t] + den
+                sums_ref[0, t] = sums_ref[0, t] + num
+                sums_ref[1, t] = sums_ref[1, t] + den
             return carry
 
         lax.fori_loop(0, groups, some, 0)
@@ -321,16 +313,15 @@
         for i, (a, s) in enumerate(turn_group(far_rows, group)):
             t = far_tile[group * 4 + i]
             live = far_live[group * 4 + i].astype(f32)
-            num, den = pair_sums(a, s, b_ref[t])
-            num_ref[t] = num_ref[t] + num * live
-            den_ref[t] = den_ref[t] + den * live
+            num, den = pair_sums(a, s, b_ref[t], points)
+            sums_ref[0, t] = sums_ref[0, t] + num * live
+            sums_ref[1, t] = sums_ref[1, t] + den * live
         return carry
 
     lax.fori_loop(0, 2 * peers // 4, far, 0)
 
     valid = (payload[3] > 0.0).astype(f32)
-    num = jnp.sum(num_ref[...], axis=1) * valid
-    den = jnp.sum(den_ref[...], axis=1) * valid
+    num, den = jnp.sum(sums_ref[...], axis=2)
     strain_bar = num / (den + 1.0 - valid)
     kappa = jnp.maximum(strain_bar, history[...])
     damage = 1.0 - (keep_share + (1.0 - keep_share) * jnp.exp(-softening * (kappa - 1.0))) / kappa
@@ -401,15 +392,14 @@
     above = lax.ppermute(payload, "sub", [(i + 1, i) for i in range(layers - 1)])
     inbox = lax.all_to_all(outbox, "blk", split_axis=0, concat_axis=0, tiled=True)
 
-    b_own, num, den = pl.pallas_call(
+    b_own, sums = pl.pallas_call(
         functools.partial(own_kernel, local_pairs.shape[1]),
         out_shape=(
             jax.ShapeDtypeStruct((tiles, 4 * depth, points), bf16),
-            jax.ShapeDtypeStruct((tiles, 8, points), f32),
-            jax.ShapeDtypeStruct((tiles, 8, points), f32),
+            jax.ShapeDtypeStruct((2, tiles, 8, points), f32),
         ),
         in_specs=[in_vmem],
-        out_specs=(in_vmem,) * 3,
+        out_specs=(in_vmem,) * 2,
         scratch_shapes=[
             pltpu.VMEM((halves, tiles * pitch, 128), f32),
             pltpu.VMEM((tiles, points, 4 * depth), bf16),
@@ -430,13 +420,12 @@
             jax.ShapeDtypeStruct((tiles, points), f32),
             jax.ShapeDtypeStruct((peers, 128), f32),
         ),
-        in_specs=[in_vmem] * 12 + [anywhere] * 3,
+        in_specs=[in_vmem] * 11 + [anywhere] * 3,
         out_specs=(in_vmem,) * 2,
         scratch_shapes=[
             pltpu.VMEM((halves, tiles * pitch, 128), f32),
             pltpu.VMEM((halves, 2 * peers * pitch, 128), f32),
-            pltpu.VMEM(num.shape, f32),
-            pltpu.VMEM(den.shape, f32),
+            pltpu.VMEM(sums.shape, f32),
         ]
         + [pltpu.SMEM(v.shape, jnp.int32) for v in (send_tile, remote_pairs, remote_count)]
         + [pltpu.SMEM((2 * peers,), jnp.int32)] * 2
@@ -451,8 +440,7 @@
         above,
         inbox,
         b_own,
-        num,
-        den,
+        sums,
         payload,
         history,
         corner_load,

time: 45.7 us -> 45.2 us (0.989)
  local copies, waits for them, and re-layouts: 4.21 us -> 2.77 us
  Pallas kernels: 20.9 us -> 21.8 us
    unnamed x26 -> x22, local copies, waits for them, and re-layouts: 4.21 us -> 2.77 us
    pallas_call x1, Pallas kernels: 11 us -> 12 us  [per_device(): pl.pallas_call(functools.partial(rest_kernel, peers), out_shape=(jax.Shap...]
where the time goes in v7:
time: 45.2 us; the launch traced here: 44.8 us
  Pallas kernels  21.8 us (48%)
  starting transfers between devices  9.58 us (21%)
  blocking collectives  8.63 us (19%)
  local copies, waits for them, and re-layouts  2.77 us (6%)
  between operations  1.44 us (3%)
  other arithmetic  0.54 us (1%)
    pallas_call x1, Pallas kernels, per_device(): pl.pallas_call(functools.partial(rest_kernel, peers), out_shape=(jax.Shap...  12 us
    all_to_all x1, blocking collectives, per_device(): lax.all_to_all(parts, 'blk', split_axis=0, concat_axis=0, tiled=True)  8.63 us
    pallas_call x1, Pallas kernels, per_device(): pl.pallas_call(functools.partial(own_kernel, local_pairs.shape[1]), out_s...  8.05 us
    ppermute x1, starting transfers between devices, per_device(): lax.ppermute(payload, 'sub', [(i, i + 1) for i in range(layers - 1)])  3.92 us
    all_to_all x1, starting transfers between devices, per_device(): lax.all_to_all(outbox, 'blk', split_axis=0, concat_axis=0, tiled=True)  3.74 us
    unnamed x22, local copies, waits for them, and re-layouts  2.77 us
    ppermute x1, starting transfers between devices, per_device(): lax.ppermute(payload, 'sub', [(i + 1, i) for i in range(layers - 1)])  1.92 us
    pallas_call x1, Pallas kernels, per_device(): pl.pallas_call(functools.partial(pack_kernel, peers), out_shape=(jax.Shap...  1.79 us
  transfers between devices with their start and end apart: 3, of which 0 were waited for; matrix products, arithmetic and copies ran while one was open for 0% of the time, Pallas kernels for 18%

profile of v7, /device:TPU:8, one launch (start us, length us, event | category | flops | bytes accessed | tf_op | source)
XLA Modules:
  0.0 44.8 jit_solution(7120926066587578968)
XLA Ops:
  1.3 1.8 %pack.1 = (f32[5,32,256]{2,1,0:T(8,128)}, f32[128,128]{1,0:T(8,128)}) custom-call(f32[3,32,256]{2,1,0:T(8,128)} %coords.1, f32[32,256]{1,0:T(8,128)} %strain.1, s32[32]{0:T(128)} %tile_count_in.1, s32[8]{0:T(128)} %send_tile_in.3, s32[2,8]{1,0:T(2,128)} %remote_pairs_in.3, s32[1]{0:T(128)S(6)} %copy.15.remote_count_in, s32[2,32]{1,0:T(2,128)} %local_pairs_in.1), custom_call_target="tpu_custom_call" | custom-call | tf_op jit(solution)/shard_map/pack/pallas_call | solution.py:375
  3.1 1.9 %collective-permute-start.1 = (f32[5,32,256]{2,1,0:T(8,128)}, f32[5,32,256]{2,1,0:T(8,128)S(1)}, u32[]{:S(2)}, u32[]{:S(2)}) collective-permute-start(f32[5,32,256]{2,1,0:T(8,128)} %get-tuple-element.8.payload), channel_id=1, source_target_pairs={{8,0},{16,8},{24,16},{9,1},{17,9},{25,17},{10,2},{18,10},{26,18},{... | collective-permute-start | bytes 491528 | tf_op jit(solution)/shard_map/ppermute | solution.py:392
  5.0 3.9 %collective-permute-start = (f32[5,32,256]{2,1,0:T(8,128)}, f32[5,32,256]{2,1,0:T(8,128)S(1)}, u32[]{:S(2)}, u32[]{:S(2)}) collective-permute-start(f32[5,32,256]{2,1,0:T(8,128)} %get-tuple-element.8.payload), channel_id=1, source_target_pairs={{0,8},{8,16},{16,24},{1,9},{9,17},{17,25},{2,10},{10,18},{18,26},{... | collective-permute-start | bytes 491528 | tf_op jit(solution)/shard_map/ppermute | solution.py:391
  8.9 3.7 %all-to-all-start = ((f32[8,16,128]{2,1,0:T(8,128)}), f32[8,16,128]{2,1,0:T(8,128)S(1)}, u32[]{:S(2)}, u32[]{:S(2)}) async-start(f32[8,16,128]{2,1,0:T(8,128)} %bitcast.7), calls=%async_computation | async-start | bytes 131072 | tf_op jit(solution)/shard_map/all_to_all | solution.py:393
  12.7 0.9 %copy-done.3 = f32[5,32,256]{2,1,0:T(8,128)S(1)} copy-done((f32[5,32,256]{2,1,0:T(8,128)S(1)}, f32[5,32,256]{2,1,0:T(8,128)}, u32[]{:S(2)}) %copy-start.3) | copy-done | bytes 163864
  13.6 0.0 copy-start.5
  13.6 0.0 copy-start.6
  13.6 0.0 copy-start.7
  13.6 0.0 copy-start.8
  13.6 8.1 %own.1 = (bf16[32,128,256]{2,1,0:T(8,128)(2,1)S(1)}, f32[2,32,8,256]{3,2,1,0:T(8,128)S(1)}) custom-call(f32[5,32,256]{2,1,0:T(8,128)S(1)} %copy-done.3), custom_call_target="tpu_custom_call" | custom-call | flops 402653184 | bytes 1048576 | tf_op jit(solution)/shard_map/own/pallas_call | solution.py:395
  21.7 0.0 copy-start.9
  21.7 0.8 %copy-done.9 = f32[2,32,8,256]{3,2,1,0:T(8,128)} copy-done((f32[2,32,8,256]{3,2,1,0:T(8,128)}, f32[2,32,8,256]{3,2,1,0:T(8,128)S(1)}, u32[]{:S(2)}) %copy-start.9) | copy-done | bytes 524312
  22.5 0.0 all-to-all-done
  22.5 0.0 collective-permute-done.1.above
  22.5 0.0 collective-permute-done.below
  22.5 0.0 copy-done
  22.5 0.0 copy-done.1
  22.5 0.0 copy-done.2
  22.5 0.0 copy-done.4
  22.5 0.0 copy-done.5
  22.6 1.0 %copy-done.10 = f32[2,32,8,256]{3,2,1,0:T(8,128)S(1)} copy-done((f32[2,32,8,256]{3,2,1,0:T(8,128)S(1)}, f32[2,32,8,256]{3,2,1,0:T(8,128)}, u32[]{:S(2)}) %copy-start.10) | copy-done | bytes 524312
  23.6 12.0 %rest.1 = (f32[32,256]{1,0:T(8,128)}, f32[8,128]{1,0:T(8,128)S(1)}) custom-call(f32[5,32,256]{2,1,0:T(8,128)S(1)} %collective-permute-done.below, f32[5,32,256]{2,1,0:T(8,128)S(1)} %collective-permute-done.1.above, f32[128,128]{1,0:T(8,128)S(1)} %bitcast.5, bf16[32,128,256]{2,1,0:T(8,128)(2,1)S(1)} %get-tuple-element.10.b_ref, ...), custom_call_target="tpu_custom_call" | custom-call | flops 536870912 | bytes 2097152 | tf_op jit(solution)/shard_map/rest/pallas_call | solution.py:417
  35.6 8.6 %all_to_all.20 = f32[8,1,128]{2,1,0:T(1,128)S(1)} all-to-all(f32[8,1,128]{2,1,0:T(1,128)S(1)} %bitcast.6), channel_id=1, replica_groups=mesh['sub'=4,'blk'=8] {'blk'}, dimensions={0} | all-to-all | bytes 8192 | tf_op jit(solution)/shard_map/all_to_all | solution.py:454
  44.2 0.5 %reduce_sum.9 = f32[128]{0:T(128)} reduce(f32[8,1,128]{2,1,0:T(1,128)S(1)} %all_to_all.20, f32[]{:T(128)} %constant.0.clone.1), dimensions={0,1}, to_apply=%region_0.0 | reduce | flops 896 | bytes 4612 | tf_op jit(solution)/shard_map/reduce_sum | solution.py:455
  (9 shorter events, 0.0 us)
Async XLA Ops:
  3.1 19.4 %collective-permute-start.1 = (f32[5,32,256]{2,1,0:T(8,128)}, f32[5,32,256]{2,1,0:T(8,128)S(1)}, u32[]{:S(2)}, u32[]{:S(2)}) collective-permute-start(f32[5,32,256]{2,1,0:T(8,128)} %get-tuple-element.8.payload), channel_id=1, source_target_pairs={{8,0},{16,8},{24,16},{9,1},{17,9},{25,17},{10,2},{18,10},{26,18},{... | collective-permute-start | bytes 491528 | tf_op jit(solution)/shard_map/ppermute | solution.py:392
  5.0 17.5 %collective-permute-start = (f32[5,32,256]{2,1,0:T(8,128)}, f32[5,32,256]{2,1,0:T(8,128)S(1)}, u32[]{:S(2)}, u32[]{:S(2)}) collective-permute-start(f32[5,32,256]{2,1,0:T(8,128)} %get-tuple-element.8.payload), channel_id=1, source_target_pairs={{0,8},{8,16},{16,24},{1,9},{9,17},{17,25},{2,10},{10,18},{18,26},{... | collective-permute-start | bytes 491528 | tf_op jit(solution)/shard_map/ppermute | solution.py:391
  8.9 13.6 %all-to-all-start = ((f32[8,16,128]{2,1,0:T(8,128)}), f32[8,16,128]{2,1,0:T(8,128)S(1)}, u32[]{:S(2)}, u32[]{:S(2)}) async-start(f32[8,16,128]{2,1,0:T(8,128)} %bitcast.7), calls=%async_computation | async-start | bytes 131072 | tf_op jit(solution)/shard_map/all_to_all | solution.py:393
  12.7 0.9 %copy-start.3 = (f32[5,32,256]{2,1,0:T(8,128)S(1)}, f32[5,32,256]{2,1,0:T(8,128)}, u32[]{:S(2)}) copy-start(f32[5,32,256]{2,1,0:T(8,128)} %get-tuple-element.8.payload) | copy-start | bytes 491524
  13.6 8.9 %copy-start = (s32[2,8]{1,0:T(2,128)S(1)}, s32[2,8]{1,0:T(2,128)}, u32[]{:S(2)}) copy-start(s32[2,8]{1,0:T(2,128)} %remote_pairs_in.3) | copy-start | bytes 196
  13.6 8.9 %copy-start.1 = (s32[8]{0:T(128)S(1)}, s32[8]{0:T(128)}, u32[]{:S(2)}) copy-start(s32[8]{0:T(128)} %send_tile_in.3) | copy-start | bytes 100
  13.6 8.9 %copy-start.2 = (f32[24,32,256]{2,1,0:T(8,128)S(1)}, f32[24,32,256]{2,1,0:T(8,128)}, u32[]{:S(2)}) copy-start(f32[24,32,256]{2,1,0:T(8,128)} %corner_load.1) | copy-start | bytes 2359300
  13.6 8.9 %copy-start.4 = (f32[5,32,256]{2,1,0:T(8,128)S(1)}, f32[5,32,256]{2,1,0:T(8,128)}, u32[]{:S(2)}) copy-start(f32[5,32,256]{2,1,0:T(8,128)} %get-tuple-element.8.payload) | copy-start | bytes 491524
  13.6 9.0 %copy-start.5 = (f32[32,256]{1,0:T(8,128)S(1)}, f32[32,256]{1,0:T(8,128)}, u32[]{:S(2)}) copy-start(f32[32,256]{1,0:T(8,128)} %history.1) | copy-start | bytes 98308
  13.6 8.9 %copy-start.6 = (s32[4,24]{1,0:T(4,128)S(1)}, s32[4,24]{1,0:T(4,128)}, u32[]{:S(2)}) copy-start(s32[4,24]{1,0:T(4,128)} %corner_map.1) | copy-start | bytes 1156
  13.6 8.9 %copy-start.7 = (f32[128]{0:T(128)S(1)}, f32[128]{0:T(128)}, u32[]{:S(2)}) copy-start(f32[128]{0:T(128)} %external.1) | copy-start | bytes 1540
  13.6 8.9 %copy-start.8 = (s32[32]{0:T(128)S(1)}, s32[32]{0:T(128)}, u32[]{:S(2)}) copy-start(s32[32]{0:T(128)} %tile_sub.1) | copy-start | bytes 388
  21.7 0.8 %copy-start.9 = (f32[2,32,8,256]{3,2,1,0:T(8,128)}, f32[2,32,8,256]{3,2,1,0:T(8,128)S(1)}, u32[]{:S(2)}) copy-start(f32[2,32,8,256]{3,2,1,0:T(8,128)S(1)} %get-tuple-element.11.sums_in) | copy-start | bytes 1572868
  22.6 1.0 %copy-start.10 = (f32[2,32,8,256]{3,2,1,0:T(8,128)S(1)}, f32[2,32,8,256]{3,2,1,0:T(8,128)}, u32[]{:S(2)}) copy-start(f32[2,32,8,256]{3,2,1,0:T(8,128)} %copy-done.9) | copy-start | bytes 1572868

commit v8 on v7

--- a/solution.py
+++ b/solution.py
@@ -11,11 +11,11 @@
 gauss_rate = 4.0
 keep_share = 0.05
 softening = 0.5
-coord_scale = math.sqrt(gauss_rate)
+coord_scale = math.sqrt(gauss_rate * math.log2(math.e))
 far_off = 2048.0
 depth = 32
 pitch = depth + 1
-grant = 48 * 1024 * 1024
+grant = 24 * 1024 * 1024
 whole_grant = 60 * 1024 * 1024
 
 f32 = jnp.float32
@@ -95,13 +95,24 @@
     return fold(weight * load), fold(weight)
 
 
-def pair_sums(a, s, b, step):
-    num, den = 0.0, 0.0
-    for lo in range(0, a.shape[0], step):
-        weight = jnp.exp(jnp.dot(a[lo : lo + step], b, preferred_element_type=f32))
-        more_num, more_den = column_sums(weight, s[lo : lo + step])
-        num, den = num + more_num, den + more_den
-    return num, den
+def add_pair(sums_ref, t, a, s, b, live=None):
+    weight = jnp.exp2(jnp.dot(a, b, preferred_element_type=f32))
+    num, den = column_sums(weight, s)
+    if live is not None:
+        num, den = num * live, den * live
+    sums_ref[0, t] = sums_ref[0, t] + num
+    sums_ref[1, t] = sums_ref[1, t] + den
+
+
+def repeat_target(compact, b_ref):
+    def some_tiles(step, carry):
+        for t in [step * 4 + i for i in range(4)]:
+            block = compact[t]
+            for j in range(4):
+                b_ref[t, depth * j : depth * (j + 1), :] = block
+        return carry
+
+    lax.fori_loop(0, compact.shape[0] // 4, some_tiles, 0)
 
 
 def fetch(sources, targets, sems):
@@ -172,7 +183,7 @@
     return jnp.broadcast_to(wide, (128, 128)).T[0:n]
 
 
-def own_kernel(pairs, payload, b_ref, sums_ref, rows_ref, a_ref, s_ref, local_pairs, sems):
+def own_kernel(pairs, payload, b_out, sums_ref, rows_ref, a_ref, s_ref, b_ref, local_pairs, sems):
     tiles = payload.shape[1]
     copies = fetch((payload.at[4, 0:8, 0:128],), (local_pairs,), sems)
     planes = [payload[k] for k in range(4)]
@@ -182,41 +193,36 @@
         for t in [group * 4 + i for i in range(4)]:
             rows = pl.ds(t * pitch, depth)
             for half in range(rows_ref.shape[0]):
-                block = rows_ref[half, rows, :].astype(bf16)
-                for j in range(4):
-                    b_ref[t, depth * j : depth * (j + 1), half * 128 : (half + 1) * 128] = block
+                b_out[t, :, half * 128 : (half + 1) * 128] = rows_ref[half, rows, :].astype(bf16)
         return carry
 
     lax.fori_loop(0, tiles // 4, set_target, 0)
+    repeat_target(b_out, b_ref)
     put_source(planes, rows_ref, 0)
+    sums_ref[...] = jnp.zeros_like(sums_ref)
     for copy in copies:
         copy.wait()
 
-    def own(group, carry):
-        for i, (a, s) in enumerate(turn_group(rows_ref, group)):
-            t = group * 4 + i
-            a_ref[t] = a
-            s_ref[t] = s
-            num, den = pair_sums(a, s, b_ref[t], 64)
-            sums_ref[0, t] = num
-            sums_ref[1, t] = den
-        return carry
-
-    lax.fori_loop(0, tiles // 4, own, 0)
+    def own(step, carry):
+        for group in (2 * step, 2 * step + 1):
+            for i, (a, s) in enumerate(turn_group(rows_ref, group)):
+                t = group * 4 + i
+                a_ref[t] = a
+                s_ref[t] = s
+                add_pair(sums_ref, t, a, s, b_ref[t])
+        return carry
+
+    lax.fori_loop(0, tiles // 8, own, 0)
 
     def listed(step, carry):
-        group = []
-        for i in range(4):
-            one = local_pairs[0, step * 4 + i].astype(jnp.int32)
-            two = local_pairs[1, step * 4 + i].astype(jnp.int32)
-            group += [(one, two), (two, one)]
-        sums = [pair_sums(a_ref[src], s_ref[src], b_ref[dst], 64) for src, dst in group]
-        for (src, dst), (num, den) in zip(group, sums):
-            sums_ref[0, dst] = sums_ref[0, dst] + num
-            sums_ref[1, dst] = sums_ref[1, dst] + den
-        return carry
-
-    lax.fori_loop(0, pairs // 4, listed, 0)
+        for i in range(8):
+            one = local_pairs[0, step * 8 + i].astype(jnp.int32)
+            two = local_pairs[1, step * 8 + i].astype(jnp.int32)
+            add_pair(sums_ref, two, a_ref[one], s_ref[one], b_ref[two])
+            add_pair(sums_ref, one, a_ref[two], s_ref[two], b_ref[one])
+        return carry
+
+    lax.fori_loop(0, pairs // 8, listed, 0)
 
 
 def rest_kernel(
@@ -224,7 +230,7 @@
     below,
     above,
     inbox,
-    b_ref,
+    b_in,
     sums_in,
     payload,
     history,
@@ -239,6 +245,7 @@
     parts_ref,
     rows_ref,
     far_rows,
+    b_ref,
     sums_ref,
     send_tile,
     remote_pairs,
@@ -259,24 +266,18 @@
     )
 
     sums_ref[...] = sums_in[...]
+    repeat_target(b_in, b_ref)
 
     def border(shift):
-        def some(group, carry):
-            sums = {}
-            for i, (a, s) in enumerate(turn_group(rows_ref, group)):
-                places = (i, i + shift)
-                targets = [lax.rem(group * 4 + place + tiles, tiles) for place in places]
-                num, den = pair_sums(a, s, jnp.concatenate([b_ref[t] for t in targets], axis=1), points)
-                for j, (place, t) in enumerate(zip(places, targets)):
-                    cut = slice(j * points, (j + 1) * points)
-                    held = sums.get(place, (t, 0.0, 0.0))
-                    sums[place] = (t, held[1] + num[:, cut], held[2] + den[:, cut])
-            for t, num, den in sums.values():
-                sums_ref[0, t] = sums_ref[0, t] + num
-                sums_ref[1, t] = sums_ref[1, t] + den
+        def some(step, carry):
+            for group in (2 * step, 2 * step + 1):
+                for i, (a, s) in enumerate(turn_group(rows_ref, group)):
+                    for place in (i, i + shift):
+                        t = lax.rem(group * 4 + place + tiles, tiles)
+                        add_pair(sums_ref, t, a, s, b_ref[t])
             return carry
 
-        lax.fori_loop(0, groups, some, 0)
+        lax.fori_loop(0, groups // 2, some, 0)
 
     @pl.when(layer > 0)
     def lower():
@@ -309,16 +310,14 @@
 
     lax.fori_loop(0, peers, place, 0, unroll=peers <= 8)
 
-    def far(group, carry):
-        for i, (a, s) in enumerate(turn_group(far_rows, group)):
-            t = far_tile[group * 4 + i]
-            live = far_live[group * 4 + i].astype(f32)
-            num, den = pair_sums(a, s, b_ref[t], points)
-            sums_ref[0, t] = sums_ref[0, t] + num * live
-            sums_ref[1, t] = sums_ref[1, t] + den * live
-        return carry
-
-    lax.fori_loop(0, 2 * peers // 4, far, 0)
+    def far(step, carry):
+        for group in (2 * step, 2 * step + 1):
+            for i, (a, s) in enumerate(turn_group(far_rows, group)):
+                t = far_tile[group * 4 + i]
+                add_pair(sums_ref, t, a, s, b_ref[t], far_live[group * 4 + i].astype(f32))
+        return carry
+
+    lax.fori_loop(0, 2 * peers // 8, far, 0)
 
     valid = (payload[3] > 0.0).astype(f32)
     num, den = jnp.sum(sums_ref[...], axis=2)
@@ -395,7 +394,7 @@
     b_own, sums = pl.pallas_call(
         functools.partial(own_kernel, local_pairs.shape[1]),
         out_shape=(
-            jax.ShapeDtypeStruct((tiles, 4 * depth, points), bf16),
+            jax.ShapeDtypeStruct((tiles, depth, points), bf16),
             jax.ShapeDtypeStruct((2, tiles, 8, points), f32),
         ),
         in_specs=[in_vmem],
@@ -404,6 +403,7 @@
             pltpu.VMEM((halves, tiles * pitch, 128), f32),
             pltpu.VMEM((tiles, points, 4 * depth), bf16),
             pltpu.VMEM((tiles, points, 128), f32),
+            pltpu.VMEM((tiles, 4 * depth, points), bf16),
             pltpu.SMEM((8, 128), f32),
             pltpu.SemaphoreType.DMA((1,)),
         ],
@@ -425,6 +425,7 @@
         scratch_shapes=[
             pltpu.VMEM((halves, tiles * pitch, 128), f32),
             pltpu.VMEM((halves, 2 * peers * pitch, 128), f32),
+            pltpu.VMEM((tiles, 4 * depth, points), bf16),
             pltpu.VMEM(sums.shape, f32),
         ]
         + [pltpu.SMEM(v.shape, jnp.int32) for v in (send_tile, remote_pairs, remote_count)]

time: 45.2 us -> 39.1 us (0.87)
  Pallas kernels: 21.8 us -> 17 us
  local copies, waits for them, and re-layouts: 2.77 us -> 1.56 us
    pallas_call x1, Pallas kernels: 12 us -> 9.19 us  [per_device(): pl.pallas_call(functools.partial(rest_kernel, peers), out_shape=(jax.Shap...]
    pallas_call x1, Pallas kernels: 8.05 us -> 6.04 us  [per_device(): pl.pallas_call(functools.partial(own_kernel, local_pairs.shape[1]), out_s...]
    unnamed x22 -> x18, local copies, waits for them, and re-layouts: 2.77 us -> 1.56 us
  transfers between devices with their start and end apart: 3 -> 3, of which waited for: 0 -> 0; matrix products, arithmetic and copies ran while one was open for 0% -> 0% of each run, Pallas kernels for 18% -> 16%
where the time goes in v8:
time: 39.1 us; the launch traced here: 38.8 us
  Pallas kernels  17 us (43%)
  starting transfers between devices  9.58 us (25%)
  blocking collectives  8.65 us (22%)
  local copies, waits for them, and re-layouts  1.56 us (4%)
  between operations  1.42 us (4%)
  other arithmetic  0.54 us (1%)
    pallas_call x1, Pallas kernels, per_device(): pl.pallas_call(functools.partial(rest_kernel, peers), out_shape=(jax.Shap...  9.19 us
    all_to_all x1, blocking collectives, per_device(): lax.all_to_all(parts, 'blk', split_axis=0, concat_axis=0, tiled=True)  8.65 us
    pallas_call x1, Pallas kernels, per_device(): pl.pallas_call(functools.partial(own_kernel, local_pairs.shape[1]), out_s...  6.04 us
    ppermute x1, starting transfers between devices, per_device(): lax.ppermute(payload, 'sub', [(i, i + 1) for i in range(layers - 1)])  3.92 us
    all_to_all x1, starting transfers between devices, per_device(): lax.all_to_all(outbox, 'blk', split_axis=0, concat_axis=0, tiled=True)  3.74 us
    ppermute x1, starting transfers between devices, per_device(): lax.ppermute(payload, 'sub', [(i + 1, i) for i in range(layers - 1)])  1.92 us
    pallas_call x1, Pallas kernels, per_device(): pl.pallas_call(functools.partial(pack_kernel, peers), out_shape=(jax.Shap...  1.79 us
    unnamed x18, local copies, waits for them, and re-layouts  1.56 us
  transfers between devices with their start and end apart: 3, of which 0 were waited for; matrix products, arithmetic and copies ran while one was open for 0% of the time, Pallas kernels for 16%

profile of v8, /device:TPU:8, one launch (start us, length us, event | category | flops | bytes accessed | tf_op | source)
XLA Modules:
  0.0 38.8 jit_solution(7902435662190762097)
XLA Ops:
  1.3 1.8 %pack.1 = (f32[5,32,256]{2,1,0:T(8,128)}, f32[128,128]{1,0:T(8,128)}) custom-call(f32[3,32,256]{2,1,0:T(8,128)} %coords.1, f32[32,256]{1,0:T(8,128)} %strain.1, s32[32]{0:T(128)} %tile_count_in.1, s32[8]{0:T(128)} %send_tile_in.3, s32[2,8]{1,0:T(2,128)} %remote_pairs_in.3, s32[1]{0:T(128)S(6)} %copy.15.remote_count_in, s32[2,32]{1,0:T(2,128)} %local_pairs_in.1), custom_call_target="tpu_custom_call" | custom-call | tf_op jit(solution)/shard_map/pack/pallas_call | solution.py:374
  3.1 1.9 %collective-permute-start.1 = (f32[5,32,256]{2,1,0:T(8,128)}, f32[5,32,256]{2,1,0:T(8,128)S(1)}, u32[]{:S(2)}, u32[]{:S(2)}) collective-permute-start(f32[5,32,256]{2,1,0:T(8,128)} %get-tuple-element.8.payload), channel_id=1, source_target_pairs={{8,0},{16,8},{24,16},{9,1},{17,9},{25,17},{10,2},{18,10},{26,18},{... | collective-permute-start | bytes 491528 | tf_op jit(solution)/shard_map/ppermute | solution.py:391
  5.0 3.9 %collective-permute-start = (f32[5,32,256]{2,1,0:T(8,128)}, f32[5,32,256]{2,1,0:T(8,128)S(1)}, u32[]{:S(2)}, u32[]{:S(2)}) collective-permute-start(f32[5,32,256]{2,1,0:T(8,128)} %get-tuple-element.8.payload), channel_id=1, source_target_pairs={{0,8},{8,16},{16,24},{1,9},{9,17},{17,25},{2,10},{10,18},{18,26},{... | collective-permute-start | bytes 491528 | tf_op jit(solution)/shard_map/ppermute | solution.py:390
  8.9 3.7 %all-to-all-start = ((f32[8,16,128]{2,1,0:T(8,128)}), f32[8,16,128]{2,1,0:T(8,128)S(1)}, u32[]{:S(2)}, u32[]{:S(2)}) async-start(f32[8,16,128]{2,1,0:T(8,128)} %bitcast.7), calls=%async_computation | async-start | bytes 131072 | tf_op jit(solution)/shard_map/all_to_all | solution.py:392
  12.7 0.9 %copy-done.3 = f32[5,32,256]{2,1,0:T(8,128)S(1)} copy-done((f32[5,32,256]{2,1,0:T(8,128)S(1)}, f32[5,32,256]{2,1,0:T(8,128)}, u32[]{:S(2)}) %copy-start.3) | copy-done | bytes 163864
  13.6 0.0 copy-start.8
  13.6 6.0 %own.1 = (bf16[32,32,256]{2,1,0:T(8,128)(2,1)S(1)}, f32[2,32,8,256]{3,2,1,0:T(8,128)S(1)}) custom-call(f32[5,32,256]{2,1,0:T(8,128)S(1)} %copy-done.3), custom_call_target="tpu_custom_call" | custom-call | flops 402653184 | bytes 1048576 | tf_op jit(solution)/shard_map/own/pallas_call | solution.py:394
  19.7 0.0 all-to-all-done
  19.7 0.0 collective-permute-done.1.above
  19.7 0.0 collective-permute-done.below
  19.7 0.0 copy-start.6
  19.7 0.0 copy-start
  19.7 0.0 copy-start.1
  19.7 0.0 copy-done.2
  19.7 0.0 copy-done.4
  19.8 0.0 copy-done.5
  19.8 0.0 copy-done.7
  19.8 0.0 copy-done.8
  19.8 0.6 %copy-done.6 = s32[4,24]{1,0:T(4,128)S(1)} copy-done((s32[4,24]{1,0:T(4,128)S(1)}, s32[4,24]{1,0:T(4,128)}, u32[]{:S(2)}) %copy-start.6) | copy-done | bytes 408
  20.4 0.0 copy-done
  20.4 0.0 copy-done.1
  20.4 9.2 %rest.1 = (f32[32,256]{1,0:T(8,128)}, f32[8,128]{1,0:T(8,128)S(1)}) custom-call(f32[5,32,256]{2,1,0:T(8,128)S(1)} %collective-permute-done.below, f32[5,32,256]{2,1,0:T(8,128)S(1)} %collective-permute-done.1.above, f32[128,128]{1,0:T(8,128)S(1)} %bitcast.5, bf16[32,32,256]{2,1,0:T(8,128)(2,1)S(1)} %get-tuple-element.10.b_in, ...), custom_call_target="tpu_custom_call" | custom-call | flops 536870912 | bytes 2097152 | tf_op jit(solution)/shard_map/rest/pallas_call | solution.py:417
  29.6 8.6 %all_to_all.20 = f32[8,1,128]{2,1,0:T(1,128)S(1)} all-to-all(f32[8,1,128]{2,1,0:T(1,128)S(1)} %bitcast.6), channel_id=1, replica_groups=mesh['sub'=4,'blk'=8] {'blk'}, dimensions={0} | all-to-all | bytes 8192 | tf_op jit(solution)/shard_map/all_to_all | solution.py:455
  38.2 0.5 %reduce_sum.9 = f32[128]{0:T(128)} reduce(f32[8,1,128]{2,1,0:T(1,128)S(1)} %all_to_all.20, f32[]{:T(128)} %constant.0.clone.1), dimensions={0,1}, to_apply=%region_0.0 | reduce | flops 896 | bytes 4612 | tf_op jit(solution)/shard_map/reduce_sum | solution.py:456
  (5 shorter events, 0.0 us)
Async XLA Ops:
  3.1 16.6 %collective-permute-start.1 = (f32[5,32,256]{2,1,0:T(8,128)}, f32[5,32,256]{2,1,0:T(8,128)S(1)}, u32[]{:S(2)}, u32[]{:S(2)}) collective-permute-start(f32[5,32,256]{2,1,0:T(8,128)} %get-tuple-element.8.payload), channel_id=1, source_target_pairs={{8,0},{16,8},{24,16},{9,1},{17,9},{25,17},{10,2},{18,10},{26,18},{... | collective-permute-start | bytes 491528 | tf_op jit(solution)/shard_map/ppermute | solution.py:391
  5.0 14.7 %collective-permute-start = (f32[5,32,256]{2,1,0:T(8,128)}, f32[5,32,256]{2,1,0:T(8,128)S(1)}, u32[]{:S(2)}, u32[]{:S(2)}) collective-permute-start(f32[5,32,256]{2,1,0:T(8,128)} %get-tuple-element.8.payload), channel_id=1, source_target_pairs={{0,8},{8,16},{16,24},{1,9},{9,17},{17,25},{2,10},{10,18},{18,26},{... | collective-permute-start | bytes 491528 | tf_op jit(solution)/shard_map/ppermute | solution.py:390
  8.9 10.7 %all-to-all-start = ((f32[8,16,128]{2,1,0:T(8,128)}), f32[8,16,128]{2,1,0:T(8,128)S(1)}, u32[]{:S(2)}, u32[]{:S(2)}) async-start(f32[8,16,128]{2,1,0:T(8,128)} %bitcast.7), calls=%async_computation | async-start | bytes 131072 | tf_op jit(solution)/shard_map/all_to_all | solution.py:392
  12.7 0.9 %copy-start.3 = (f32[5,32,256]{2,1,0:T(8,128)S(1)}, f32[5,32,256]{2,1,0:T(8,128)}, u32[]{:S(2)}) copy-start(f32[5,32,256]{2,1,0:T(8,128)} %get-tuple-element.8.payload) | copy-start | bytes 491524
  13.6 6.1 %copy-start.2 = (f32[24,32,256]{2,1,0:T(8,128)S(1)}, f32[24,32,256]{2,1,0:T(8,128)}, u32[]{:S(2)}) copy-start(f32[24,32,256]{2,1,0:T(8,128)} %corner_load.1) | copy-start | bytes 2359300
  13.6 6.2 %copy-start.4 = (f32[5,32,256]{2,1,0:T(8,128)S(1)}, f32[5,32,256]{2,1,0:T(8,128)}, u32[]{:S(2)}) copy-start(f32[5,32,256]{2,1,0:T(8,128)} %get-tuple-element.8.payload) | copy-start | bytes 491524
  13.6 6.2 %copy-start.5 = (f32[32,256]{1,0:T(8,128)S(1)}, f32[32,256]{1,0:T(8,128)}, u32[]{:S(2)}) copy-start(f32[32,256]{1,0:T(8,128)} %history.1) | copy-start | bytes 98308
  13.6 6.2 %copy-start.7 = (f32[128]{0:T(128)S(1)}, f32[128]{0:T(128)}, u32[]{:S(2)}) copy-start(f32[128]{0:T(128)} %external.1) | copy-start | bytes 1540
  13.6 6.2 %copy-start.8 = (s32[32]{0:T(128)S(1)}, s32[32]{0:T(128)}, u32[]{:S(2)}) copy-start(s32[32]{0:T(128)} %tile_sub.1) | copy-start | bytes 388
  19.7 0.7 %copy-start.6 = (s32[4,24]{1,0:T(4,128)S(1)}, s32[4,24]{1,0:T(4,128)}, u32[]{:S(2)}) copy-start(s32[4,24]{1,0:T(4,128)} %corner_map.1) | copy-start | bytes 1156
  19.7 0.7 %copy-start = (s32[2,8]{1,0:T(2,128)S(1)}, s32[2,8]{1,0:T(2,128)}, u32[]{:S(2)}) copy-start(s32[2,8]{1,0:T(2,128)} %remote_pairs_in.3) | copy-start | bytes 196
  19.7 0.7 %copy-start.1 = (s32[8]{0:T(128)S(1)}, s32[8]{0:T(128)}, u32[]{:S(2)}) copy-start(s32[8]{0:T(128)} %send_tile_in.3) | copy-start | bytes 100

commit v9 on v8

--- a/solution.py
+++ b/solution.py
@@ -16,12 +16,15 @@
 depth = 32
 pitch = depth + 1
 grant = 24 * 1024 * 1024
-whole_grant = 60 * 1024 * 1024
 
 f32 = jnp.float32
 bf16 = jnp.bfloat16
 in_vmem = pl.BlockSpec(memory_space=pltpu.VMEM)
 anywhere = pl.BlockSpec(memory_space=pl.ANY)
+
+
+def in_hbm(value):
+    return value if value.size == 1 else pltpu.with_memory_space_constraint(value, pltpu.HBM)
 
 
 def pieces(value):
@@ -204,7 +207,7 @@
         copy.wait()
 
     def own(step, carry):
-        for group in (2 * step, 2 * step + 1):
+        for group in [4 * step + g for g in range(4)]:
             for i, (a, s) in enumerate(turn_group(rows_ref, group)):
                 t = group * 4 + i
                 a_ref[t] = a
@@ -212,17 +215,17 @@
                 add_pair(sums_ref, t, a, s, b_ref[t])
         return carry
 
-    lax.fori_loop(0, tiles // 8, own, 0)
+    lax.fori_loop(0, tiles // 16, own, 0)
 
     def listed(step, carry):
-        for i in range(8):
-            one = local_pairs[0, step * 8 + i].astype(jnp.int32)
-            two = local_pairs[1, step * 8 + i].astype(jnp.int32)
+        for i in range(16):
+            one = local_pairs[0, step * 16 + i].astype(jnp.int32)
+            two = local_pairs[1, step * 16 + i].astype(jnp.int32)
             add_pair(sums_ref, two, a_ref[one], s_ref[one], b_ref[two])
             add_pair(sums_ref, one, a_ref[two], s_ref[two], b_ref[one])
         return carry
 
-    lax.fori_loop(0, pairs // 8, listed, 0)
+    lax.fori_loop(0, pairs // 16, listed, 0)
 
 
 def rest_kernel(
@@ -233,16 +236,22 @@
     b_in,
     sums_in,
     payload,
+    history_in,
+    corner_load_in,
+    external_in,
+    tile_sub_in,
+    corner_map_in,
+    send_tile_in,
+    remote_pairs_in,
+    remote_count_in,
+    damage_out,
+    parts_ref,
+    damage_ref,
     history,
     corner_load,
     external,
     tile_sub,
     corner_map,
-    send_tile_in,
-    remote_pairs_in,
-    remote_count_in,
-    damage_ref,
-    parts_ref,
     rows_ref,
     far_rows,
     b_ref,
@@ -260,9 +269,18 @@
     count = lax.axis_size("sub")
     layer = lax.axis_index("sub")
     copies = fetch(
-        (send_tile_in, remote_pairs_in, remote_count_in),
-        (send_tile, remote_pairs, remote_count),
-        sems,
+        (
+            send_tile_in,
+            remote_pairs_in,
+            remote_count_in,
+            history_in,
+            corner_load_in,
+            external_in,
+            tile_sub_in,
+            corner_map_in,
+        ),
+        (send_tile, remote_pairs, remote_count, history, corner_load, external, tile_sub, corner_map),
+        sems.at[0:8],
     )
 
     sums_ref[...] = sums_in[...]
@@ -270,14 +288,14 @@
 
     def border(shift):
         def some(step, carry):
-            for group in (2 * step, 2 * step + 1):
+            for group in [4 * step + g for g in range(4)]:
                 for i, (a, s) in enumerate(turn_group(rows_ref, group)):
                     for place in (i, i + shift):
                         t = lax.rem(group * 4 + place + tiles, tiles)
                         add_pair(sums_ref, t, a, s, b_ref[t])
             return carry
 
-        lax.fori_loop(0, groups // 2, some, 0)
+        lax.fori_loop(0, groups // 4, some, 0)
 
     @pl.when(layer > 0)
     def lower():
@@ -325,6 +343,8 @@
     kappa = jnp.maximum(strain_bar, history[...])
     damage = 1.0 - (keep_share + (1.0 - keep_share) * jnp.exp(-softening * (kappa - 1.0))) / kappa
     damage_ref[...] = damage
+    leaving = pltpu.make_async_copy(damage_ref, damage_out, sems.at[8])
+    leaving.start()
     intact = (1.0 - damage) * valid
 
     folded = corner_load[:, :, 0:128] * intact[None, :, 0:128]
@@ -348,6 +368,7 @@
         return carry
 
     lax.fori_loop(0, peers, scatter, 0, unroll=peers <= 8)
+    leaving.wait()
 
 
 def per_device(
@@ -368,23 +389,22 @@
     halves = points // 128
     peers = lax.axis_size("blk")
     params = pltpu.CompilerParams(vmem_limit_bytes=grant)
-    whole_params = pltpu.CompilerParams(vmem_limit_bytes=whole_grant)
     block = 2 * points * points
 
     payload, outbox = pl.pallas_call(
         functools.partial(pack_kernel, peers),
         out_shape=(
-            jax.ShapeDtypeStruct((5, tiles, points), f32),
-            jax.ShapeDtypeStruct((peers * halves * 8, 128), f32),
+            pltpu.VMEM((5, tiles, points), f32),
+            pltpu.VMEM((peers * halves * 8, 128), f32),
         ),
         in_specs=[anywhere] * 7,
         out_specs=(in_vmem, in_vmem),
         scratch_shapes=[pltpu.VMEM((tiles, points), f32)]
         + [pltpu.SMEM(v.shape, jnp.int32) for v in (tile_count, send_tile, remote_pairs, remote_count)]
         + [pltpu.VMEM(local_pairs.shape, jnp.int32), pltpu.SemaphoreType.DMA((7,))],
-        compiler_params=whole_params,
+        compiler_params=params,
         name="pack",
-    )(coords, strain, tile_count, send_tile, remote_pairs, remote_count, local_pairs)
+    )(*(in_hbm(v) for v in (coords, strain, tile_count, send_tile, remote_pairs, remote_count, local_pairs)))
 
     layers = lax.axis_size("sub")
     below = lax.ppermute(payload, "sub", [(i, i + 1) for i in range(layers - 1)])
@@ -420,9 +440,10 @@
             jax.ShapeDtypeStruct((tiles, points), f32),
             jax.ShapeDtypeStruct((peers, 128), f32),
         ),
-        in_specs=[in_vmem] * 11 + [anywhere] * 3,
-        out_specs=(in_vmem,) * 2,
-        scratch_shapes=[
+        in_specs=[in_vmem] * 6 + [anywhere] * 8,
+        out_specs=(anywhere, in_vmem),
+        scratch_shapes=[pltpu.VMEM(v.shape, v.dtype) for v in (strain, history, corner_load, external, tile_sub, corner_map)]
+        + [
             pltpu.VMEM((halves, tiles * pitch, 128), f32),
             pltpu.VMEM((halves, 2 * peers * pitch, 128), f32),
             pltpu.VMEM((tiles, 4 * depth, points), bf16),
@@ -430,7 +451,7 @@
         ]
         + [pltpu.SMEM(v.shape, jnp.int32) for v in (send_tile, remote_pairs, remote_count)]
         + [pltpu.SMEM((2 * peers,), jnp.int32)] * 2
-        + [pltpu.SemaphoreType.DMA((3,))],
+        + [pltpu.SemaphoreType.DMA((9,))],
         compiler_params=params,
         cost_estimate=pl.CostEstimate(
             flops=4 * tiles * block * depth, bytes_accessed=1 << 21, transcendentals=4 * tiles * points * points
@@ -443,14 +464,19 @@
         b_own,
         sums,
         payload,
-        history,
-        corner_load,
-        external,
-        tile_sub,
-        corner_map,
-        send_tile,
-        remote_pairs,
-        remote_count,
+        *(
+            in_hbm(v)
+            for v in (
+                history,
+                corner_load,
+                external,
+                tile_sub,
+                corner_map,
+                send_tile,
+                remote_pairs,
+                remote_count,
+            )
+        ),
     )
     gathered = lax.all_to_all(parts, "blk", split_axis=0, concat_axis=0, tiled=True)
     return damage, jnp.sum(gathered, axis=0)

time: 39.1 us -> 36.4 us (0.931)
  local copies, waits for them, and re-layouts: 1.56 us -> 0 us
  Pallas kernels: 17 us -> 16 us
    unnamed x18 -> x0, local copies, waits for them, and re-layouts: 1.56 us -> none
    pallas_call x1, Pallas kernels: 6.04 us -> 5.39 us  [per_device(): pl.pallas_call(functools.partial(own_kernel, local_pairs.shape[1]), out_s...]
  transfers between devices with their start and end apart: 3 -> 3, of which waited for: 0 -> 0; matrix products, arithmetic and copies ran while one was open for 0% -> 0% of each run, Pallas kernels for 16% -> 15%
where the time goes in v9:
time: 36.4 us; the launch traced here: 36.1 us
  Pallas kernels  16 us (44%)
  starting transfers between devices  9.58 us (26%)
  blocking collectives  8.65 us (24%)
  between operations  1.34 us (4%)
  other arithmetic  0.54 us (1%)
    pallas_call x1, Pallas kernels, per_device(): pl.pallas_call(functools.partial(rest_kernel, peers), out_shape=(jax.Shap...  8.85 us
    all_to_all x1, blocking collectives, per_device(): lax.all_to_all(parts, 'blk', split_axis=0, concat_axis=0, tiled=True)  8.65 us
    pallas_call x1, Pallas kernels, per_device(): pl.pallas_call(functools.partial(own_kernel, local_pairs.shape[1]), out_s...  5.39 us
    ppermute x1, starting transfers between devices, per_device(): lax.ppermute(payload, 'sub', [(i, i + 1) for i in range(layers - 1)])  3.92 us
    all_to_all x1, starting transfers between devices, per_device(): lax.all_to_all(outbox, 'blk', split_axis=0, concat_axis=0, tiled=True)  3.74 us
    ppermute x1, starting transfers between devices, per_device(): lax.ppermute(payload, 'sub', [(i + 1, i) for i in range(layers - 1)])  1.92 us
    pallas_call x1, Pallas kernels, per_device(): pl.pallas_call(functools.partial(pack_kernel, peers), out_shape=(pltpu.VM...  1.72 us
  transfers between devices with their start and end apart: 3, of which 0 were waited for; matrix products, arithmetic and copies ran while one was open for 0% of the time, Pallas kernels for 15%

profile of v9, /device:TPU:8, one launch (start us, length us, event | category | flops | bytes accessed | tf_op | source)
XLA Modules:
  0.0 36.1 jit_solution(2593449068704181374)
XLA Ops:
  1.3 1.7 %pack.1 = (f32[5,32,256]{2,1,0:T(8,128)S(1)}, f32[128,128]{1,0:T(8,128)}) custom-call(f32[3,32,256]{2,1,0:T(8,128)} %coords.1, f32[32,256]{1,0:T(8,128)} %strain.1, s32[32]{0:T(128)} %tile_count_in.1, s32[8]{0:T(128)} %send_tile_in.3, s32[2,8]{1,0:T(2,128)} %remote_pairs_in.3, s32[1]{0:T(128)S(6)} %copy.15.remote_count_in, s32[2,32]{1,0:T(2,128)} %local_pairs_in.1), custom_call_target="tpu_custom_call" | custom-call | tf_op jit(solution)/shard_map/pack/pallas_call | solution.py:394
  3.0 1.9 %collective-permute-start.1 = (f32[5,32,256]{2,1,0:T(8,128)S(1)}, f32[5,32,256]{2,1,0:T(8,128)S(1)}, u32[]{:S(2)}, u32[]{:S(2)}) collective-permute-start(f32[5,32,256]{2,1,0:T(8,128)S(1)} %get-tuple-element.8.payload), channel_id=1, source_target_pairs={{8,0},{16,8},{24,16},{9,1},{17,9},{25,17},{10,2},{18,10},{26,18},{... | collective-permute-start | bytes 491528 | tf_op jit(solution)/shard_map/ppermute | solution.py:411
  4.9 3.9 %collective-permute-start = (f32[5,32,256]{2,1,0:T(8,128)S(1)}, f32[5,32,256]{2,1,0:T(8,128)S(1)}, u32[]{:S(2)}, u32[]{:S(2)}) collective-permute-start(f32[5,32,256]{2,1,0:T(8,128)S(1)} %get-tuple-element.8.payload), channel_id=1, source_target_pairs={{0,8},{8,16},{16,24},{1,9},{9,17},{17,25},{2,10},{10,18},{18,26},{... | collective-permute-start | bytes 491528 | tf_op jit(solution)/shard_map/ppermute | solution.py:410
  8.9 3.7 %all-to-all-start = ((f32[8,16,128]{2,1,0:T(8,128)}), f32[8,16,128]{2,1,0:T(8,128)S(1)}, u32[]{:S(2)}, u32[]{:S(2)}) async-start(f32[8,16,128]{2,1,0:T(8,128)} %bitcast), calls=%async_computation | async-start | bytes 131072 | tf_op jit(solution)/shard_map/all_to_all | solution.py:412
  12.6 5.4 %own.1 = (bf16[32,32,256]{2,1,0:T(8,128)(2,1)S(1)}, f32[2,32,8,256]{3,2,1,0:T(8,128)S(1)}) custom-call(f32[5,32,256]{2,1,0:T(8,128)S(1)} %get-tuple-element.8.payload), custom_call_target="tpu_custom_call" | custom-call | flops 402653184 | bytes 1048576 | tf_op jit(solution)/shard_map/own/pallas_call | solution.py:414
  18.0 0.0 all-to-all-done
  18.0 0.0 collective-permute-done.1.above
  18.0 0.0 collective-permute-done.below
  18.0 8.9 %rest.1 = (f32[32,256]{1,0:T(8,128)}, f32[8,128]{1,0:T(8,128)S(1)}) custom-call(f32[5,32,256]{2,1,0:T(8,128)S(1)} %collective-permute-done.below, f32[5,32,256]{2,1,0:T(8,128)S(1)} %collective-permute-done.1.above, f32[128,128]{1,0:T(8,128)S(1)} %bitcast.5, bf16[32,32,256]{2,1,0:T(8,128)(2,1)S(1)} %get-tuple-element.10.b_in, ...), custom_call_target="tpu_custom_call" | custom-call | flops 536870912 | bytes 2097152 | tf_op jit(solution)/shard_map/rest/pallas_call | solution.py:437
  26.9 8.6 %all_to_all.20 = f32[8,1,128]{2,1,0:T(1,128)S(1)} all-to-all(f32[8,1,128]{2,1,0:T(1,128)S(1)} %bitcast.6), channel_id=1, replica_groups=mesh['sub'=4,'blk'=8] {'blk'}, dimensions={0} | all-to-all | bytes 8192 | tf_op jit(solution)/shard_map/all_to_all | solution.py:481
  35.5 0.5 %reduce_sum.9 = f32[128]{0:T(128)} reduce(f32[8,1,128]{2,1,0:T(1,128)S(1)} %all_to_all.20, f32[]{:T(128)} %constant.0.clone.1), dimensions={0,1}, to_apply=%region_0.0 | reduce | flops 896 | bytes 4612 | tf_op jit(solution)/shard_map/reduce_sum | solution.py:482
Async XLA Ops:
  3.0 15.0 %collective-permute-start.1 = (f32[5,32,256]{2,1,0:T(8,128)S(1)}, f32[5,32,256]{2,1,0:T(8,128)S(1)}, u32[]{:S(2)}, u32[]{:S(2)}) collective-permute-start(f32[5,32,256]{2,1,0:T(8,128)S(1)} %get-tuple-element.8.payload), channel_id=1, source_target_pairs={{8,0},{16,8},{24,16},{9,1},{17,9},{25,17},{10,2},{18,10},{26,18},{... | collective-permute-start | bytes 491528 | tf_op jit(solution)/shard_map/ppermute | solution.py:411
  4.9 13.1 %collective-permute-start = (f32[5,32,256]{2,1,0:T(8,128)S(1)}, f32[5,32,256]{2,1,0:T(8,128)S(1)}, u32[]{:S(2)}, u32[]{:S(2)}) collective-permute-start(f32[5,32,256]{2,1,0:T(8,128)S(1)} %get-tuple-element.8.payload), channel_id=1, source_target_pairs={{0,8},{8,16},{16,24},{1,9},{9,17},{17,25},{2,10},{10,18},{18,26},{... | collective-permute-start | bytes 491528 | tf_op jit(solution)/shard_map/ppermute | solution.py:410
  8.9 9.1 %all-to-all-start = ((f32[8,16,128]{2,1,0:T(8,128)}), f32[8,16,128]{2,1,0:T(8,128)S(1)}, u32[]{:S(2)}, u32[]{:S(2)}) async-start(f32[8,16,128]{2,1,0:T(8,128)} %bitcast), calls=%async_computation | async-start | bytes 131072 | tf_op jit(solution)/shard_map/all_to_all | solution.py:412

commit v10 on v9

--- a/solution.py
+++ b/solution.py
@@ -105,17 +105,6 @@
         num, den = num * live, den * live
     sums_ref[0, t] = sums_ref[0, t] + num
     sums_ref[1, t] = sums_ref[1, t] + den
-
-
-def repeat_target(compact, b_ref):
-    def some_tiles(step, carry):
-        for t in [step * 4 + i for i in range(4)]:
-            block = compact[t]
-            for j in range(4):
-                b_ref[t, depth * j : depth * (j + 1), :] = block
-        return carry
-
-    lax.fori_loop(0, compact.shape[0] // 4, some_tiles, 0)
 
 
 def fetch(sources, targets, sems):
@@ -186,7 +175,7 @@
     return jnp.broadcast_to(wide, (128, 128)).T[0:n]
 
 
-def own_kernel(pairs, payload, b_out, sums_ref, rows_ref, a_ref, s_ref, b_ref, local_pairs, sems):
+def own_kernel(pairs, payload, b_ref, sums_ref, rows_ref, a_ref, s_ref, local_pairs, sems):
     tiles = payload.shape[1]
     copies = fetch((payload.at[4, 0:8, 0:128],), (local_pairs,), sems)
     planes = [payload[k] for k in range(4)]
@@ -196,11 +185,12 @@
         for t in [group * 4 + i for i in range(4)]:
             rows = pl.ds(t * pitch, depth)
             for half in range(rows_ref.shape[0]):
-                b_out[t, :, half * 128 : (half + 1) * 128] = rows_ref[half, rows, :].astype(bf16)
+                block = rows_ref[half, rows, :].astype(bf16)
+                for j in range(4):
+                    b_ref[t, depth * j : depth * (j + 1), half * 128 : (half + 1) * 128] = block
         return carry
 
     lax.fori_loop(0, tiles // 4, set_target, 0)
-    repeat_target(b_out, b_ref)
     put_source(planes, rows_ref, 0)
     sums_ref[...] = jnp.zeros_like(sums_ref)
     for copy in copies:
@@ -233,7 +223,7 @@
     below,
     above,
     inbox,
-    b_in,
+    b_ref,
     sums_in,
     payload,
     history_in,
@@ -244,9 +234,8 @@
     send_tile_in,
     remote_pairs_in,
     remote_count_in,
-    damage_out,
+    damage_ref,
     parts_ref,
-    damage_ref,
     history,
     corner_load,
     external,
@@ -254,7 +243,6 @@
     corner_map,
     rows_ref,
     far_rows,
-    b_ref,
     sums_ref,
     send_tile,
     remote_pairs,
@@ -280,11 +268,10 @@
             corner_map_in,
         ),
         (send_tile, remote_pairs, remote_count, history, corner_load, external, tile_sub, corner_map),
-        sems.at[0:8],
+        sems,
     )
 
     sums_ref[...] = sums_in[...]
-    repeat_target(b_in, b_ref)
 
     def border(shift):
         def some(step, carry):
@@ -343,8 +330,6 @@
     kappa = jnp.maximum(strain_bar, history[...])
     damage = 1.0 - (keep_share + (1.0 - keep_share) * jnp.exp(-softening * (kappa - 1.0))) / kappa
     damage_ref[...] = damage
-    leaving = pltpu.make_async_copy(damage_ref, damage_out, sems.at[8])
-    leaving.start()
     intact = (1.0 - damage) * valid
 
     folded = corner_load[:, :, 0:128] * intact[None, :, 0:128]
@@ -368,7 +353,12 @@
         return carry
 
     lax.fori_loop(0, peers, scatter, 0, unroll=peers <= 8)
-    leaving.wait()
+
+
+def leave_kernel(damage, damage_out, sem):
+    copy = pltpu.make_async_copy(damage, damage_out, sem)
+    copy.start()
+    copy.wait()
 
 
 def per_device(
@@ -414,7 +404,7 @@
     b_own, sums = pl.pallas_call(
         functools.partial(own_kernel, local_pairs.shape[1]),
         out_shape=(
-            jax.ShapeDtypeStruct((tiles, depth, points), bf16),
+            jax.ShapeDtypeStruct((tiles, 4 * depth, points), bf16),
             jax.ShapeDtypeStruct((2, tiles, 8, points), f32),
         ),
         in_specs=[in_vmem],
@@ -423,7 +413,6 @@
             pltpu.VMEM((halves, tiles * pitch, 128), f32),
             pltpu.VMEM((tiles, points, 4 * depth), bf16),
             pltpu.VMEM((tiles, points, 128), f32),
-            pltpu.VMEM((tiles, 4 * depth, points), bf16),
             pltpu.SMEM((8, 128), f32),
             pltpu.SemaphoreType.DMA((1,)),
         ],
@@ -437,21 +426,20 @@
     damage, parts = pl.pallas_call(
         functools.partial(rest_kernel, peers),
         out_shape=(
-            jax.ShapeDtypeStruct((tiles, points), f32),
-            jax.ShapeDtypeStruct((peers, 128), f32),
+            pltpu.VMEM((tiles, points), f32),
+            pltpu.VMEM((peers, 128), f32),
         ),
         in_specs=[in_vmem] * 6 + [anywhere] * 8,
-        out_specs=(anywhere, in_vmem),
-        scratch_shapes=[pltpu.VMEM(v.shape, v.dtype) for v in (strain, history, corner_load, external, tile_sub, corner_map)]
+        out_specs=(in_vmem, in_vmem),
+        scratch_shapes=[pltpu.VMEM(v.shape, v.dtype) for v in (history, corner_load, external, tile_sub, corner_map)]
         + [
             pltpu.VMEM((halves, tiles * pitch, 128), f32),
             pltpu.VMEM((halves, 2 * peers * pitch, 128), f32),
-            pltpu.VMEM((tiles, 4 * depth, points), bf16),
             pltpu.VMEM(sums.shape, f32),
         ]
         + [pltpu.SMEM(v.shape, jnp.int32) for v in (send_tile, remote_pairs, remote_count)]
         + [pltpu.SMEM((2 * peers,), jnp.int32)] * 2
-        + [pltpu.SemaphoreType.DMA((9,))],
+        + [pltpu.SemaphoreType.DMA((8,))],
         compiler_params=params,
         cost_estimate=pl.CostEstimate(
             flops=4 * tiles * block * depth, bytes_accessed=1 << 21, transcendentals=4 * tiles * points * points
@@ -479,6 +467,16 @@
         ),
     )
     gathered = lax.all_to_all(parts, "blk", split_axis=0, concat_axis=0, tiled=True)
+    damage = pl.pallas_call(
+        leave_kernel,
+        out_shape=jax.ShapeDtypeStruct((tiles, points), f32),
+        in_specs=[in_vmem],
+        out_specs=anywhere,
+        scratch_shapes=[pltpu.SemaphoreType.DMA],
+        compiler_params=params,
+        cost_estimate=pl.CostEstimate(flops=0, bytes_accessed=1 << 22, transcendentals=0),
+        name="leave",
+    )(damage)
     return damage, jnp.sum(gathered, axis=0)
 
 

time: 36.4 us -> 36.8 us (1.011)
  blocking collectives: 8.65 us -> 0 us
  starting transfers between devices: 9.58 us -> 13.8 us
  waiting for transfers between devices: 0.01 us -> 4.03 us
  Pallas kernels: 16 us -> 16.8 us
    all_to_all x1 -> x0, blocking collectives: 8.65 us -> none  [per_device(): lax.all_to_all(parts, 'blk', split_axis=0, concat_axis=0, tiled=True)]
    all_to_all x0 -> x1, starting transfers between devices: none -> 4.23 us  [per_device(): lax.all_to_all(parts, 'blk', split_axis=0, concat_axis=0, tiled=True)]
    all_to_all x0 -> x1, waiting for transfers between devices: none -> 4.03 us  [per_device(): lax.all_to_all(parts, 'blk', split_axis=0, concat_axis=0, tiled=True)]
    pallas_call x1 -> x2, Pallas kernels: 8.85 us -> 9.62 us  [the longest x1 9 us: per_device(): pl.pallas_call(functools.partial(rest_kernel, peers), out_shape=(pltpu.VM...]
  transfers between devices with their start and end apart: 3 -> 4, of which waited for: 0 -> 1; matrix products, arithmetic and copies ran while one was open for 0% -> 0% of each run, Pallas kernels for 15% -> 17%
where the time goes in v10:
time: 36.8 us; the launch traced here: 36.5 us
  Pallas kernels  16.8 us (46%)
  starting transfers between devices  13.8 us (38%)
  waiting for transfers between devices  4.03 us (11%)
  between operations  1.35 us (4%)
  other arithmetic  0.54 us (1%)
    pallas_call x1, Pallas kernels, per_device(): pl.pallas_call(functools.partial(rest_kernel, peers), out_shape=(pltpu.VM...  9 us
    pallas_call x1, Pallas kernels, per_device(): pl.pallas_call(functools.partial(own_kernel, local_pairs.shape[1]), out_s...  5.41 us
    all_to_all x1, starting transfers between devices, per_device(): lax.all_to_all(parts, 'blk', split_axis=0, concat_axis=0, tiled=True)  4.23 us
    all_to_all x1, waiting for transfers between devices, per_device(): lax.all_to_all(parts, 'blk', split_axis=0, concat_axis=0, tiled=True)  4.03 us
    ppermute x1, starting transfers between devices, per_device(): lax.ppermute(payload, 'sub', [(i, i + 1) for i in range(layers - 1)])  3.92 us
    all_to_all x1, starting transfers between devices, per_device(): lax.all_to_all(outbox, 'blk', split_axis=0, concat_axis=0, tiled=True)  3.74 us
    ppermute x1, starting transfers between devices, per_device(): lax.ppermute(payload, 'sub', [(i + 1, i) for i in range(layers - 1)])  1.92 us
    pallas_call x1, Pallas kernels, per_device(): pl.pallas_call(functools.partial(pack_kernel, peers), out_shape=(pltpu.VM...  1.73 us
  transfers between devices with their start and end apart: 4, of which 1 were waited for; matrix products, arithmetic and copies ran while one was open for 0% of the time, Pallas kernels for 17%

profile of v10, /device:TPU:8, one launch (start us, length us, event | category | flops | bytes accessed | tf_op | source)
XLA Modules:
  0.0 36.5 jit_solution(8407514696499199911)
XLA Ops:
  1.3 1.7 %pack.1 = (f32[5,32,256]{2,1,0:T(8,128)S(1)}, f32[128,128]{1,0:T(8,128)}) custom-call(f32[3,32,256]{2,1,0:T(8,128)} %coords.1, f32[32,256]{1,0:T(8,128)} %strain.1, s32[32]{0:T(128)} %tile_count_in.1, s32[8]{0:T(128)} %send_tile_in.3, s32[2,8]{1,0:T(2,128)} %remote_pairs_in.3, s32[1]{0:T(128)S(6)} %copy.15.remote_count_in, s32[2,32]{1,0:T(2,128)} %local_pairs_in.1), custom_call_target="tpu_custom_call" | custom-call | tf_op jit(solution)/shard_map/pack/pallas_call | solution.py:384
  3.0 1.9 %collective-permute-start.1 = (f32[5,32,256]{2,1,0:T(8,128)S(1)}, f32[5,32,256]{2,1,0:T(8,128)S(1)}, u32[]{:S(2)}, u32[]{:S(2)}) collective-permute-start(f32[5,32,256]{2,1,0:T(8,128)S(1)} %get-tuple-element.8.payload), channel_id=1, source_target_pairs={{8,0},{16,8},{24,16},{9,1},{17,9},{25,17},{10,2},{18,10},{26,18},{... | collective-permute-start | bytes 491528 | tf_op jit(solution)/shard_map/ppermute | solution.py:401
  4.9 3.9 %collective-permute-start = (f32[5,32,256]{2,1,0:T(8,128)S(1)}, f32[5,32,256]{2,1,0:T(8,128)S(1)}, u32[]{:S(2)}, u32[]{:S(2)}) collective-permute-start(f32[5,32,256]{2,1,0:T(8,128)S(1)} %get-tuple-element.8.payload), channel_id=1, source_target_pairs={{0,8},{8,16},{16,24},{1,9},{9,17},{17,25},{2,10},{10,18},{18,26},{... | collective-permute-start | bytes 491528 | tf_op jit(solution)/shard_map/ppermute | solution.py:400
  8.9 3.7 %all-to-all-start = ((f32[8,16,128]{2,1,0:T(8,128)}), f32[8,16,128]{2,1,0:T(8,128)S(1)}, u32[]{:S(2)}, u32[]{:S(2)}) async-start(f32[8,16,128]{2,1,0:T(8,128)} %bitcast), calls=%async_computation | async-start | bytes 131072 | tf_op jit(solution)/shard_map/all_to_all | solution.py:402
  12.6 5.4 %own.1 = (bf16[32,128,256]{2,1,0:T(8,128)(2,1)S(1)}, f32[2,32,8,256]{3,2,1,0:T(8,128)S(1)}) custom-call(f32[5,32,256]{2,1,0:T(8,128)S(1)} %get-tuple-element.8.payload), custom_call_target="tpu_custom_call" | custom-call | flops 402653184 | bytes 1048576 | tf_op jit(solution)/shard_map/own/pallas_call | solution.py:404
  18.0 0.0 all-to-all-done
  18.0 0.0 collective-permute-done.1.above
  18.0 0.0 collective-permute-done.below
  18.1 9.0 %rest.1 = (f32[32,256]{1,0:T(8,128)S(1)}, f32[8,128]{1,0:T(8,128)}) custom-call(f32[5,32,256]{2,1,0:T(8,128)S(1)} %collective-permute-done.below, f32[5,32,256]{2,1,0:T(8,128)S(1)} %collective-permute-done.1.above, f32[128,128]{1,0:T(8,128)S(1)} %bitcast.5, bf16[32,128,256]{2,1,0:T(8,128)(2,1)S(1)} %get-tuple-element.10.b_ref, ...), custom_call_target="tpu_custom_call" | custom-call | flops 536870912 | bytes 2097152 | tf_op jit(solution)/shard_map/rest/pallas_call | solution.py:426
  27.1 4.2 %all-to-all-start.1 = ((f32[8,1,128]{2,1,0:T(1,128)}), f32[8,1,128]{2,1,0:T(1,128)S(1)}, u32[]{:S(2)}, u32[]{:S(2)}) async-start(f32[8,1,128]{2,1,0:T(1,128)} %bitcast.3), calls=%async_computation.1 | async-start | bytes 8192 | tf_op jit(solution)/shard_map/all_to_all | solution.py:469
  31.3 0.6 %leave.1 = f32[32,256]{1,0:T(8,128)} custom-call(f32[32,256]{1,0:T(8,128)S(1)} %get-tuple-element.12.damage), custom_call_target="tpu_custom_call" | custom-call | bytes 4194304 | tf_op jit(solution)/shard_map/leave/pallas_call | solution.py:470
  31.9 4.0 %all-to-all-done.1 = f32[8,1,128]{2,1,0:T(1,128)S(1)} async-done(((f32[8,1,128]{2,1,0:T(1,128)}), f32[8,1,128]{2,1,0:T(1,128)S(1)}, u32[]{:S(2)}, u32[]{:S(2)}) %all-to-all-start.1) | async-done | bytes 4128 | tf_op jit(solution)/shard_map/all_to_all | solution.py:469
  36.0 0.5 %reduce_sum.9 = f32[128]{0:T(128)} reduce(f32[8,1,128]{2,1,0:T(1,128)S(1)} %all-to-all-done.1, f32[]{:T(128)} %constant.0.clone.1), dimensions={0,1}, to_apply=%region_0.0 | reduce | flops 896 | bytes 4612 | tf_op jit(solution)/shard_map/reduce_sum | solution.py:480
Async XLA Ops:
  3.0 15.0 %collective-permute-start.1 = (f32[5,32,256]{2,1,0:T(8,128)S(1)}, f32[5,32,256]{2,1,0:T(8,128)S(1)}, u32[]{:S(2)}, u32[]{:S(2)}) collective-permute-start(f32[5,32,256]{2,1,0:T(8,128)S(1)} %get-tuple-element.8.payload), channel_id=1, source_target_pairs={{8,0},{16,8},{24,16},{9,1},{17,9},{25,17},{10,2},{18,10},{26,18},{... | collective-permute-start | bytes 491528 | tf_op jit(solution)/shard_map/ppermute | solution.py:401
  4.9 13.1 %collective-permute-start = (f32[5,32,256]{2,1,0:T(8,128)S(1)}, f32[5,32,256]{2,1,0:T(8,128)S(1)}, u32[]{:S(2)}, u32[]{:S(2)}) collective-permute-start(f32[5,32,256]{2,1,0:T(8,128)S(1)} %get-tuple-element.8.payload), channel_id=1, source_target_pairs={{0,8},{8,16},{16,24},{1,9},{9,17},{17,25},{2,10},{10,18},{18,26},{... | collective-permute-start | bytes 491528 | tf_op jit(solution)/shard_map/ppermute | solution.py:400
  8.9 9.2 %all-to-all-start = ((f32[8,16,128]{2,1,0:T(8,128)}), f32[8,16,128]{2,1,0:T(8,128)S(1)}, u32[]{:S(2)}, u32[]{:S(2)}) async-start(f32[8,16,128]{2,1,0:T(8,128)} %bitcast), calls=%async_computation | async-start | bytes 131072 | tf_op jit(solution)/shard_map/all_to_all | solution.py:402
  27.1 8.9 %all-to-all-start.1 = ((f32[8,1,128]{2,1,0:T(1,128)}), f32[8,1,128]{2,1,0:T(1,128)S(1)}, u32[]{:S(2)}, u32[]{:S(2)}) async-start(f32[8,1,128]{2,1,0:T(1,128)} %bitcast.3), calls=%async_computation.1 | async-start | bytes 8192 | tf_op jit(solution)/shard_map/all_to_all | solution.py:469

commit v11 on v9

--- a/solution.py
+++ b/solution.py
@@ -230,8 +230,8 @@
 
 def rest_kernel(
     peers,
-    below,
-    above,
+    late,
+    soon,
     inbox,
     b_in,
     sums_in,
@@ -286,26 +286,24 @@
     sums_ref[...] = sums_in[...]
     repeat_target(b_in, b_ref)
 
-    def border(shift):
+    def border(tiles_in, partner, shift):
         def some(step, carry):
             for group in [4 * step + g for g in range(4)]:
                 for i, (a, s) in enumerate(turn_group(rows_ref, group)):
-                    for place in (i, i + shift):
-                        t = lax.rem(group * 4 + place + tiles, tiles)
-                        add_pair(sums_ref, t, a, s, b_ref[t])
+                    u = group * 4 + i
+                    add_pair(sums_ref, u, a, s, b_ref[u])
+                    t = lax.rem(u + shift + tiles, tiles)
+                    add_pair(sums_ref, t, a, s, b_ref[t])
             return carry
 
-        lax.fori_loop(0, groups // 4, some, 0)
-
-    @pl.when(layer > 0)
-    def lower():
-        put_source([below[k] for k in range(4)], rows_ref, 0)
-        border(-1)
-
-    @pl.when(layer < count - 1)
-    def upper():
-        put_source([above[k] for k in range(4)], rows_ref, 0)
-        border(1)
+        @pl.when((partner >= 0) & (partner < count))
+        def both():
+            put_source([tiles_in[k] for k in range(4)], rows_ref, 0)
+            lax.fori_loop(0, groups // 4, some, 0)
+
+    up = 1 - 2 * lax.rem(layer, 2)
+    border(soon, layer - up, -up)
+    border(late, layer + up, up)
 
     for copy in copies:
         copy.wait()
@@ -329,13 +327,13 @@
     lax.fori_loop(0, peers, place, 0, unroll=peers <= 8)
 
     def far(step, carry):
-        for group in (2 * step, 2 * step + 1):
+        for group in [4 * step + g for g in range(4)]:
             for i, (a, s) in enumerate(turn_group(far_rows, group)):
                 t = far_tile[group * 4 + i]
                 add_pair(sums_ref, t, a, s, b_ref[t], far_live[group * 4 + i].astype(f32))
         return carry
 
-    lax.fori_loop(0, 2 * peers // 8, far, 0)
+    lax.fori_loop(0, 2 * peers // 16, far, 0)
 
     valid = (payload[3] > 0.0).astype(f32)
     num, den = jnp.sum(sums_ref[...], axis=2)
@@ -407,8 +405,10 @@
     )(*(in_hbm(v) for v in (coords, strain, tile_count, send_tile, remote_pairs, remote_count, local_pairs)))
 
     layers = lax.axis_size("sub")
-    below = lax.ppermute(payload, "sub", [(i, i + 1) for i in range(layers - 1)])
-    above = lax.ppermute(payload, "sub", [(i + 1, i) for i in range(layers - 1)])
+    late, soon = [
+        lax.ppermute(payload, "sub", [p for i in range(first, layers - 1, 2) for p in ((i, i + 1), (i + 1, i))])
+        for first in (0, 1)
+    ]
     inbox = lax.all_to_all(outbox, "blk", split_axis=0, concat_axis=0, tiled=True)
 
     b_own, sums = pl.pallas_call(
@@ -458,8 +458,8 @@
         ),
         name="rest",
     )(
-        below,
-        above,
+        late,
+        soon,
         inbox,
         b_own,
         sums,

time: 36.4 us -> 34 us (0.934)
  starting transfers between devices: 9.58 us -> 7.29 us
    ppermute x2, starting transfers between devices: 5.84 us -> 3.56 us  [per_device(): lax.ppermute(payload, 'sub', [p for i in range(first, layers - 1, 2) for...]
  transfers between devices with their start and end apart: 3 -> 3, of which waited for: 0 -> 0; matrix products, arithmetic and copies ran while one was open for 0% -> 0% of each run, Pallas kernels for 15% -> 16%
where the time goes in v11:
time: 34 us; the launch traced here: 33.7 us
  Pallas kernels  15.8 us (46%)
  blocking collectives  8.66 us (25%)
  starting transfers between devices  7.29 us (21%)
  between operations  1.34 us (4%)
  other arithmetic  0.54 us (2%)
    pallas_call x1, Pallas kernels, per_device(): pl.pallas_call(functools.partial(rest_kernel, peers), out_shape=(jax.Shap...  8.72 us
    all_to_all x1, blocking collectives, per_device(): lax.all_to_all(parts, 'blk', split_axis=0, concat_axis=0, tiled=True)  8.66 us
    pallas_call x1, Pallas kernels, per_device(): pl.pallas_call(functools.partial(own_kernel, local_pairs.shape[1]), out_s...  5.4 us
    all_to_all x1, starting transfers between devices, per_device(): lax.all_to_all(outbox, 'blk', split_axis=0, concat_axis=0, tiled=True)  3.74 us
    ppermute x2, starting transfers between devices, per_device(): lax.ppermute(payload, 'sub', [p for i in range(first, layers - 1, 2) for...  3.56 us
    pallas_call x1, Pallas kernels, per_device(): pl.pallas_call(functools.partial(pack_kernel, peers), out_shape=(pltpu.VM...  1.72 us
  transfers between devices with their start and end apart: 3, of which 0 were waited for; matrix products, arithmetic and copies ran while one was open for 0% of the time, Pallas kernels for 16%

profile of v11, /device:TPU:8, one launch (start us, length us, event | category | flops | bytes accessed | tf_op | source)
XLA Modules:
  0.0 33.7 jit_solution(9136728228940779484)
XLA Ops:
  1.3 1.7 %pack.1 = (f32[5,32,256]{2,1,0:T(8,128)S(1)}, f32[128,128]{1,0:T(8,128)}) custom-call(f32[3,32,256]{2,1,0:T(8,128)} %coords.1, f32[32,256]{1,0:T(8,128)} %strain.1, s32[32]{0:T(128)} %tile_count_in.1, s32[8]{0:T(128)} %send_tile_in.3, s32[2,8]{1,0:T(2,128)} %remote_pairs_in.3, s32[1]{0:T(128)S(6)} %copy.15.remote_count_in, s32[2,32]{1,0:T(2,128)} %local_pairs_in.1), custom_call_target="tpu_custom_call" | custom-call | tf_op jit(solution)/shard_map/pack/pallas_call | solution.py:392
  3.0 3.5 %collective-permute-start.1 = (f32[5,32,256]{2,1,0:T(8,128)S(1)}, f32[5,32,256]{2,1,0:T(8,128)S(1)}, u32[]{:S(2)}, u32[]{:S(2)}) collective-permute-start(f32[5,32,256]{2,1,0:T(8,128)S(1)} %get-tuple-element.8.payload), channel_id=1, source_target_pairs={{8,16},{16,8},{9,17},{17,9},{10,18},{18,10},{11,19},{19,11},{12,20... | collective-permute-start | bytes 491528 | tf_op jit(solution)/shard_map/ppermute | solution.py:409
  6.5 0.1 collective-permute-start
  6.6 3.7 %all-to-all-start = ((f32[8,16,128]{2,1,0:T(8,128)}), f32[8,16,128]{2,1,0:T(8,128)S(1)}, u32[]{:S(2)}, u32[]{:S(2)}) async-start(f32[8,16,128]{2,1,0:T(8,128)} %bitcast), calls=%async_computation | async-start | bytes 131072 | tf_op jit(solution)/shard_map/all_to_all | solution.py:412
  10.3 5.4 %own.1 = (bf16[32,32,256]{2,1,0:T(8,128)(2,1)S(1)}, f32[2,32,8,256]{3,2,1,0:T(8,128)S(1)}) custom-call(f32[5,32,256]{2,1,0:T(8,128)S(1)} %get-tuple-element.8.payload), custom_call_target="tpu_custom_call" | custom-call | flops 402653184 | bytes 1048576 | tf_op jit(solution)/shard_map/own/pallas_call | solution.py:414
  15.7 0.0 all-to-all-done
  15.7 0.0 collective-permute-done.1.soon
  15.7 0.0 collective-permute-done.late
  15.8 8.7 %rest.1 = (f32[32,256]{1,0:T(8,128)}, f32[8,128]{1,0:T(8,128)S(1)}) custom-call(f32[5,32,256]{2,1,0:T(8,128)S(1)} %collective-permute-done.late, f32[5,32,256]{2,1,0:T(8,128)S(1)} %collective-permute-done.1.soon, f32[128,128]{1,0:T(8,128)S(1)} %bitcast.5, bf16[32,32,256]{2,1,0:T(8,128)(2,1)S(1)} %get-tuple-element.10.b_in, ...), custom_call_target="tpu_custom_call" | custom-call | flops 536870912 | bytes 2097152 | tf_op jit(solution)/shard_map/rest/pallas_call | solution.py:437
  24.5 8.7 %all_to_all.20 = f32[8,1,128]{2,1,0:T(1,128)S(1)} all-to-all(f32[8,1,128]{2,1,0:T(1,128)S(1)} %bitcast.6), channel_id=1, replica_groups=mesh['sub'=4,'blk'=8] {'blk'}, dimensions={0} | all-to-all | bytes 8192 | tf_op jit(solution)/shard_map/all_to_all | solution.py:481
  33.1 0.5 %reduce_sum.9 = f32[128]{0:T(128)} reduce(f32[8,1,128]{2,1,0:T(1,128)S(1)} %all_to_all.20, f32[]{:T(128)} %constant.0.clone.1), dimensions={0,1}, to_apply=%region_0.0 | reduce | flops 896 | bytes 4612 | tf_op jit(solution)/shard_map/reduce_sum | solution.py:482
Async XLA Ops:
  3.0 12.7 %collective-permute-start.1 = (f32[5,32,256]{2,1,0:T(8,128)S(1)}, f32[5,32,256]{2,1,0:T(8,128)S(1)}, u32[]{:S(2)}, u32[]{:S(2)}) collective-permute-start(f32[5,32,256]{2,1,0:T(8,128)S(1)} %get-tuple-element.8.payload), channel_id=1, source_target_pairs={{8,16},{16,8},{9,17},{17,9},{10,18},{18,10},{11,19},{19,11},{12,20... | collective-permute-start | bytes 491528 | tf_op jit(solution)/shard_map/ppermute | solution.py:409
  6.5 9.2 %collective-permute-start = (f32[5,32,256]{2,1,0:T(8,128)S(1)}, f32[5,32,256]{2,1,0:T(8,128)S(1)}, u32[]{:S(2)}, u32[]{:S(2)}) collective-permute-start(f32[5,32,256]{2,1,0:T(8,128)S(1)} %get-tuple-element.8.payload), channel_id=1, source_target_pairs={{0,8},{8,0},{16,24},{24,16},{1,9},{9,1},{17,25},{25,17},{2,10},{10... | collective-permute-start | bytes 491528 | tf_op jit(solution)/shard_map/ppermute | solution.py:409
  6.6 9.1 %all-to-all-start = ((f32[8,16,128]{2,1,0:T(8,128)}), f32[8,16,128]{2,1,0:T(8,128)S(1)}, u32[]{:S(2)}, u32[]{:S(2)}) async-start(f32[8,16,128]{2,1,0:T(8,128)} %bitcast), calls=%async_computation | async-start | bytes 131072 | tf_op jit(solution)/shard_map/all_to_all | solution.py:412

commit v12 on v11

--- a/solution.py
+++ b/solution.py
@@ -79,14 +79,13 @@
         ],
         axis=0,
     )
-    left = turned.astype(bf16)
-    column = lax.broadcasted_iota(jnp.int32, (1, 128), 1) // depth
-    operands = []
-    for j in range(4):
-        mask = (column == j).astype(f32).astype(bf16)
-        lane = depth * j + 24
-        operands.append((left * mask, jnp.broadcast_to(turned[:, lane : lane + 1], turned.shape)))
-    return operands
+    lanes = [depth * j + 24 for j in range(4)]
+    return turned.astype(bf16), [jnp.broadcast_to(turned[:, n : n + 1], turned.shape) for n in lanes]
+
+
+def placed(b, j):
+    above, below = [jnp.zeros((depth * n, b.shape[1]), bf16) for n in (j, 3 - j)]
+    return jnp.concatenate([above] * (j > 0) + [b] + [below] * (j < 3), axis=0)
 
 
 def fold(x):
@@ -206,26 +205,30 @@
     for copy in copies:
         copy.wait()
 
+    column = lax.broadcasted_iota(jnp.int32, (1, 4 * depth), 1) // depth
+
     def own(step, carry):
-        for group in [4 * step + g for g in range(4)]:
-            for i, (a, s) in enumerate(turn_group(rows_ref, group)):
+        for group in [8 * step + g for g in range(8)]:
+            left, loads = turn_group(rows_ref, group)
+            for i, s in enumerate(loads):
                 t = group * 4 + i
+                a = left * (column == i).astype(f32).astype(bf16)
                 a_ref[t] = a
                 s_ref[t] = s
                 add_pair(sums_ref, t, a, s, b_ref[t])
         return carry
 
-    lax.fori_loop(0, tiles // 16, own, 0)
+    lax.fori_loop(0, tiles // 32, own, 0)
 
     def listed(step, carry):
-        for i in range(16):
-            one = local_pairs[0, step * 16 + i].astype(jnp.int32)
-            two = local_pairs[1, step * 16 + i].astype(jnp.int32)
+        for i in range(32):
+            one = local_pairs[0, step * 32 + i].astype(jnp.int32)
+            two = local_pairs[1, step * 32 + i].astype(jnp.int32)
             add_pair(sums_ref, two, a_ref[one], s_ref[one], b_ref[two])
             add_pair(sums_ref, one, a_ref[two], s_ref[two], b_ref[one])
         return carry
 
-    lax.fori_loop(0, pairs // 16, listed, 0)
+    lax.fori_loop(0, pairs // 32, listed, 0)
 
 
 def rest_kernel(
@@ -233,7 +236,7 @@
     late,
     soon,
     inbox,
-    b_in,
+    b_ref,
     sums_in,
     payload,
     history_in,
@@ -254,7 +257,6 @@
     corner_map,
     rows_ref,
     far_rows,
-    b_ref,
     sums_ref,
     send_tile,
     remote_pairs,
@@ -284,22 +286,22 @@
     )
 
     sums_ref[...] = sums_in[...]
-    repeat_target(b_in, b_ref)
 
     def border(tiles_in, partner, shift):
         def some(step, carry):
-            for group in [4 * step + g for g in range(4)]:
-                for i, (a, s) in enumerate(turn_group(rows_ref, group)):
+            for group in [8 * step + g for g in range(8)]:
+                left, loads = turn_group(rows_ref, group)
+                for i, s in enumerate(loads):
                     u = group * 4 + i
-                    add_pair(sums_ref, u, a, s, b_ref[u])
+                    add_pair(sums_ref, u, left, s, placed(b_ref[u], i))
                     t = lax.rem(u + shift + tiles, tiles)
-                    add_pair(sums_ref, t, a, s, b_ref[t])
+                    add_pair(sums_ref, t, left, s, placed(b_ref[t], i))
             return carry
 
         @pl.when((partner >= 0) & (partner < count))
         def both():
             put_source([tiles_in[k] for k in range(4)], rows_ref, 0)
-            lax.fori_loop(0, groups // 4, some, 0)
+            lax.fori_loop(0, groups // 8, some, 0)
 
     up = 1 - 2 * lax.rem(layer, 2)
     border(soon, layer - up, -up)
@@ -328,9 +330,10 @@
 
     def far(step, carry):
         for group in [4 * step + g for g in range(4)]:
-            for i, (a, s) in enumerate(turn_group(far_rows, group)):
+            left, loads = turn_group(far_rows, group)
+            for i, s in enumerate(loads):
                 t = far_tile[group * 4 + i]
-                add_pair(sums_ref, t, a, s, b_ref[t], far_live[group * 4 + i].astype(f32))
+                add_pair(sums_ref, t, left, s, placed(b_ref[t], i), far_live[group * 4 + i].astype(f32))
         return carry
 
     lax.fori_loop(0, 2 * peers // 16, far, 0)
@@ -446,7 +449,6 @@
         + [
             pltpu.VMEM((halves, tiles * pitch, 128), f32),
             pltpu.VMEM((halves, 2 * peers * pitch, 128), f32),
-            pltpu.VMEM((tiles, 4 * depth, points), bf16),
             pltpu.VMEM(sums.shape, f32),
         ]
         + [pltpu.SMEM(v.shape, jnp.int32) for v in (send_tile, remote_pairs, remote_count)]

time: 34 us -> 33.5 us (0.985)
  Pallas kernels: 15.8 us -> 15.4 us
where the time goes in v12:
time: 33.5 us; the launch traced here: 33.2 us
  Pallas kernels  15.4 us (46%)
  blocking collectives  8.66 us (26%)
  starting transfers between devices  7.29 us (22%)
  between operations  1.34 us (4%)
  other arithmetic  0.54 us (2%)
    all_to_all x1, blocking collectives, per_device(): lax.all_to_all(parts, 'blk', split_axis=0, concat_axis=0, tiled=True)  8.66 us
    pallas_call x1, Pallas kernels, per_device(): pl.pallas_call(functools.partial(rest_kernel, peers), out_shape=(jax.Shap...  8.41 us
    pallas_call x1, Pallas kernels, per_device(): pl.pallas_call(functools.partial(own_kernel, local_pairs.shape[1]), out_s...  5.28 us
    all_to_all x1, starting transfers between devices, per_device(): lax.all_to_all(outbox, 'blk', split_axis=0, concat_axis=0, tiled=True)  3.74 us
    ppermute x2, starting transfers between devices, per_device(): lax.ppermute(payload, 'sub', [p for i in range(first, layers - 1, 2) for...  3.56 us
    pallas_call x1, Pallas kernels, per_device(): pl.pallas_call(functools.partial(pack_kernel, peers), out_shape=(pltpu.VM...  1.72 us
  transfers between devices with their start and end apart: 3, of which 0 were waited for; matrix products, arithmetic and copies ran while one was open for 0% of the time, Pallas kernels for 16%

profile of v12, /device:TPU:8, one launch (start us, length us, event | category | flops | bytes accessed | tf_op | source)
XLA Modules:
  0.0 33.2 jit_solution(1547597607570035381)
XLA Ops:
  1.3 1.7 %pack.1 = (f32[5,32,256]{2,1,0:T(8,128)S(1)}, f32[128,128]{1,0:T(8,128)}) custom-call(f32[3,32,256]{2,1,0:T(8,128)} %coords.1, f32[32,256]{1,0:T(8,128)} %strain.1, s32[32]{0:T(128)} %tile_count_in.1, s32[8]{0:T(128)} %send_tile_in.3, s32[2,8]{1,0:T(2,128)} %remote_pairs_in.3, s32[1]{0:T(128)S(6)} %copy.15.remote_count_in, s32[2,32]{1,0:T(2,128)} %local_pairs_in.1), custom_call_target="tpu_custom_call" | custom-call | tf_op jit(solution)/shard_map/pack/pallas_call | solution.py:395
  3.0 3.5 %collective-permute-start.1 = (f32[5,32,256]{2,1,0:T(8,128)S(1)}, f32[5,32,256]{2,1,0:T(8,128)S(1)}, u32[]{:S(2)}, u32[]{:S(2)}) collective-permute-start(f32[5,32,256]{2,1,0:T(8,128)S(1)} %get-tuple-element.8.payload), channel_id=1, source_target_pairs={{8,16},{16,8},{9,17},{17,9},{10,18},{18,10},{11,19},{19,11},{12,20... | collective-permute-start | bytes 491528 | tf_op jit(solution)/shard_map/ppermute | solution.py:412
  6.5 0.1 collective-permute-start
  6.6 3.7 %all-to-all-start = ((f32[8,16,128]{2,1,0:T(8,128)}), f32[8,16,128]{2,1,0:T(8,128)S(1)}, u32[]{:S(2)}, u32[]{:S(2)}) async-start(f32[8,16,128]{2,1,0:T(8,128)} %bitcast), calls=%async_computation | async-start | bytes 131072 | tf_op jit(solution)/shard_map/all_to_all | solution.py:415
  10.3 5.3 %own.1 = (bf16[32,32,256]{2,1,0:T(8,128)(2,1)S(1)}, f32[2,32,8,256]{3,2,1,0:T(8,128)S(1)}) custom-call(f32[5,32,256]{2,1,0:T(8,128)S(1)} %get-tuple-element.8.payload), custom_call_target="tpu_custom_call" | custom-call | flops 402653184 | bytes 1048576 | tf_op jit(solution)/shard_map/own/pallas_call | solution.py:417
  15.6 0.0 all-to-all-done
  15.6 0.0 collective-permute-done.1.soon
  15.6 0.0 collective-permute-done.late
  15.6 8.4 %rest.1 = (f32[32,256]{1,0:T(8,128)}, f32[8,128]{1,0:T(8,128)S(1)}) custom-call(f32[5,32,256]{2,1,0:T(8,128)S(1)} %collective-permute-done.late, f32[5,32,256]{2,1,0:T(8,128)S(1)} %collective-permute-done.1.soon, f32[128,128]{1,0:T(8,128)S(1)} %bitcast.5, bf16[32,32,256]{2,1,0:T(8,128)(2,1)S(1)} %get-tuple-element.10.b_ref, ...), custom_call_target="tpu_custom_call" | custom-call | flops 536870912 | bytes 2097152 | tf_op jit(solution)/shard_map/rest/pallas_call | solution.py:440
  24.0 8.7 %all_to_all.20 = f32[8,1,128]{2,1,0:T(1,128)S(1)} all-to-all(f32[8,1,128]{2,1,0:T(1,128)S(1)} %bitcast.6), channel_id=1, replica_groups=mesh['sub'=4,'blk'=8] {'blk'}, dimensions={0} | all-to-all | bytes 8192 | tf_op jit(solution)/shard_map/all_to_all | solution.py:483
  32.7 0.5 %reduce_sum.9 = f32[128]{0:T(128)} reduce(f32[8,1,128]{2,1,0:T(1,128)S(1)} %all_to_all.20, f32[]{:T(128)} %constant.0.clone.1), dimensions={0,1}, to_apply=%region_0.0 | reduce | flops 896 | bytes 4612 | tf_op jit(solution)/shard_map/reduce_sum | solution.py:484
Async XLA Ops:
  3.0 12.6 %collective-permute-start.1 = (f32[5,32,256]{2,1,0:T(8,128)S(1)}, f32[5,32,256]{2,1,0:T(8,128)S(1)}, u32[]{:S(2)}, u32[]{:S(2)}) collective-permute-start(f32[5,32,256]{2,1,0:T(8,128)S(1)} %get-tuple-element.8.payload), channel_id=1, source_target_pairs={{8,16},{16,8},{9,17},{17,9},{10,18},{18,10},{11,19},{19,11},{12,20... | collective-permute-start | bytes 491528 | tf_op jit(solution)/shard_map/ppermute | solution.py:412
  6.5 9.1 %collective-permute-start = (f32[5,32,256]{2,1,0:T(8,128)S(1)}, f32[5,32,256]{2,1,0:T(8,128)S(1)}, u32[]{:S(2)}, u32[]{:S(2)}) collective-permute-start(f32[5,32,256]{2,1,0:T(8,128)S(1)} %get-tuple-element.8.payload), channel_id=1, source_target_pairs={{0,8},{8,0},{16,24},{24,16},{1,9},{9,1},{17,25},{25,17},{2,10},{10... | collective-permute-start | bytes 491528 | tf_op jit(solution)/shard_map/ppermute | solution.py:412
  6.6 9.0 %all-to-all-start = ((f32[8,16,128]{2,1,0:T(8,128)}), f32[8,16,128]{2,1,0:T(8,128)S(1)}, u32[]{:S(2)}, u32[]{:S(2)}) async-start(f32[8,16,128]{2,1,0:T(8,128)} %bitcast), calls=%async_computation | async-start | bytes 131072 | tf_op jit(solution)/shard_map/all_to_all | solution.py:415

commit v13 on v12

--- a/solution.py
+++ b/solution.py
@@ -140,6 +140,9 @@
     send_tile,
     remote_pairs,
     remote_count,
+    own_tile,
+    own_live,
+    blocks,
     local_pairs,
     sems,
 ):
@@ -158,25 +161,32 @@
         payload[3, t : t + 1, :] = jnp.where(lane < tile_count[t], strain_here[t : t + 1, :], 0.0)
 
     halves = points // 128
-
-    def put(h, first, t, live):
-        for k in range(4):
-            row = payload[k, pl.ds(t, 1), :]
-            if k == 3 and live is not None:
-                row = row * live
-            for half in range(halves):
-                outbox[pl.ds((h * halves + half) * 8 + first + k, 1), :] = row[:, half * 128 : (half + 1) * 128]
-
-    def sent(h, carry):
-        put(h, 0, send_tile[h], None)
-        return carry
+    for k in range(4):
+        for half in range(halves):
+            rows = payload[k, 0:4, half * 128 : (half + 1) * 128]
+            for first in (0, 4):
+                blocks[pl.ds(half * 8 + first + k, 4, stride=8 * halves), :] = rows
 
     def listed(i, carry):
-        put(remote_pairs[1, i], 4, remote_pairs[0, i], (i < remote_count[0]).astype(f32))
-        return carry
-
-    lax.fori_loop(0, peers, sent, 0, unroll=peers <= 8)
+        h = remote_pairs[1, i]
+        own_tile[h] = remote_pairs[0, i]
+        own_live[h] = (i < remote_count[0]).astype(jnp.int32)
+        return carry
+
     lax.fori_loop(0, peers, listed, 0, unroll=peers <= 8)
+    row = lax.broadcasted_iota(jnp.int32, (8, 128), 0)
+
+    def message(h, carry):
+        masked = (row == 7) & (own_live[h] == 0)
+        for half in range(halves):
+            sent, own = [
+                blocks[pl.ds(pl.multiple_of((t * halves + half) * 8, 8), 8), :] for t in (send_tile[h], own_tile[h])
+            ]
+            both = jnp.where(row < 4, sent, jnp.where(masked, 0.0, own))
+            outbox[pl.ds(pl.multiple_of((h * halves + half) * 8, 8), 8), :] = both
+        return carry
+
+    lax.fori_loop(0, peers, message, 0, unroll=peers <= 8)
 
 
 def spread_rows(values):
@@ -402,6 +412,8 @@
         out_specs=(in_vmem, in_vmem),
         scratch_shapes=[pltpu.VMEM((tiles, points), f32)]
         + [pltpu.SMEM(v.shape, jnp.int32) for v in (tile_count, send_tile, remote_pairs, remote_count)]
+        + [pltpu.SMEM((peers,), jnp.int32)] * 2
+        + [pltpu.VMEM((4 * halves * 8, 128), f32)]
         + [pltpu.VMEM(local_pairs.shape, jnp.int32), pltpu.SemaphoreType.DMA((7,))],
         compiler_params=params,
         name="pack",

time: 33.5 us -> 33.5 us (level)
  no operation moved by 1% of the time
where the time goes in v13:
time: 33.5 us; the launch traced here: 33.2 us
  Pallas kernels  15.4 us (46%)
  blocking collectives  8.66 us (26%)
  starting transfers between devices  7.29 us (22%)
  between operations  1.34 us (4%)
  other arithmetic  0.54 us (2%)
    all_to_all x1, blocking collectives, per_device(): lax.all_to_all(parts, 'blk', split_axis=0, concat_axis=0, tiled=True)  8.66 us
    pallas_call x1, Pallas kernels, per_device(): pl.pallas_call(functools.partial(rest_kernel, peers), out_shape=(jax.Shap...  8.41 us
    pallas_call x1, Pallas kernels, per_device(): pl.pallas_call(functools.partial(own_kernel, local_pairs.shape[1]), out_s...  5.27 us
    all_to_all x1, starting transfers between devices, per_device(): lax.all_to_all(outbox, 'blk', split_axis=0, concat_axis=0, tiled=True)  3.74 us
    ppermute x2, starting transfers between devices, per_device(): lax.ppermute(payload, 'sub', [p for i in range(first, layers - 1, 2) for...  3.56 us
    pallas_call x1, Pallas kernels, per_device(): pl.pallas_call(functools.partial(pack_kernel, peers), out_shape=(pltpu.VM...  1.69 us
  transfers between devices with their start and end apart: 3, of which 0 were waited for; matrix products, arithmetic and copies ran while one was open for 0% of the time, Pallas kernels for 16%

profile of v13, /device:TPU:8, one launch (start us, length us, event | category | flops | bytes accessed | tf_op | source)
XLA Modules:
  0.0 33.2 jit_solution(15204068765231999528)
XLA Ops:
  1.3 1.7 %pack.1 = (f32[5,32,256]{2,1,0:T(8,128)S(1)}, f32[128,128]{1,0:T(8,128)}) custom-call(f32[3,32,256]{2,1,0:T(8,128)} %coords.1, f32[32,256]{1,0:T(8,128)} %strain.1, s32[32]{0:T(128)} %tile_count_in.1, s32[8]{0:T(128)} %send_tile_in.3, s32[2,8]{1,0:T(2,128)} %remote_pairs_in.3, s32[1]{0:T(128)S(6)} %copy.15.remote_count_in, s32[2,32]{1,0:T(2,128)} %local_pairs_in.1), custom_call_target="tpu_custom_call" | custom-call | tf_op jit(solution)/shard_map/pack/pallas_call | solution.py:405
  3.0 3.5 %collective-permute-start.1 = (f32[5,32,256]{2,1,0:T(8,128)S(1)}, f32[5,32,256]{2,1,0:T(8,128)S(1)}, u32[]{:S(2)}, u32[]{:S(2)}) collective-permute-start(f32[5,32,256]{2,1,0:T(8,128)S(1)} %get-tuple-element.8.payload), channel_id=1, source_target_pairs={{8,16},{16,8},{9,17},{17,9},{10,18},{18,10},{11,19},{19,11},{12,20... | collective-permute-start | bytes 491528 | tf_op jit(solution)/shard_map/ppermute | solution.py:424
  6.5 0.1 collective-permute-start
  6.6 3.7 %all-to-all-start = ((f32[8,16,128]{2,1,0:T(8,128)}), f32[8,16,128]{2,1,0:T(8,128)S(1)}, u32[]{:S(2)}, u32[]{:S(2)}) async-start(f32[8,16,128]{2,1,0:T(8,128)} %bitcast), calls=%async_computation | async-start | bytes 131072 | tf_op jit(solution)/shard_map/all_to_all | solution.py:427
  10.3 5.3 %own.1 = (bf16[32,32,256]{2,1,0:T(8,128)(2,1)S(1)}, f32[2,32,8,256]{3,2,1,0:T(8,128)S(1)}) custom-call(f32[5,32,256]{2,1,0:T(8,128)S(1)} %get-tuple-element.8.payload), custom_call_target="tpu_custom_call" | custom-call | flops 402653184 | bytes 1048576 | tf_op jit(solution)/shard_map/own/pallas_call | solution.py:429
  15.6 0.0 all-to-all-done
  15.6 0.0 collective-permute-done.1.soon
  15.6 0.0 collective-permute-done.late
  15.6 8.4 %rest.1 = (f32[32,256]{1,0:T(8,128)}, f32[8,128]{1,0:T(8,128)S(1)}) custom-call(f32[5,32,256]{2,1,0:T(8,128)S(1)} %collective-permute-done.late, f32[5,32,256]{2,1,0:T(8,128)S(1)} %collective-permute-done.1.soon, f32[128,128]{1,0:T(8,128)S(1)} %bitcast.5, bf16[32,32,256]{2,1,0:T(8,128)(2,1)S(1)} %get-tuple-element.10.b_ref, ...), custom_call_target="tpu_custom_call" | custom-call | flops 536870912 | bytes 2097152 | tf_op jit(solution)/shard_map/rest/pallas_call | solution.py:452
  24.0 8.7 %all_to_all.20 = f32[8,1,128]{2,1,0:T(1,128)S(1)} all-to-all(f32[8,1,128]{2,1,0:T(1,128)S(1)} %bitcast.6), channel_id=1, replica_groups=mesh['sub'=4,'blk'=8] {'blk'}, dimensions={0} | all-to-all | bytes 8192 | tf_op jit(solution)/shard_map/all_to_all | solution.py:495
  32.7 0.5 %reduce_sum.9 = f32[128]{0:T(128)} reduce(f32[8,1,128]{2,1,0:T(1,128)S(1)} %all_to_all.20, f32[]{:T(128)} %constant.0.clone.1), dimensions={0,1}, to_apply=%region_0.0 | reduce | flops 896 | bytes 4612 | tf_op jit(solution)/shard_map/reduce_sum | solution.py:496
Async XLA Ops:
  3.0 12.6 %collective-permute-start.1 = (f32[5,32,256]{2,1,0:T(8,128)S(1)}, f32[5,32,256]{2,1,0:T(8,128)S(1)}, u32[]{:S(2)}, u32[]{:S(2)}) collective-permute-start(f32[5,32,256]{2,1,0:T(8,128)S(1)} %get-tuple-element.8.payload), channel_id=1, source_target_pairs={{8,16},{16,8},{9,17},{17,9},{10,18},{18,10},{11,19},{19,11},{12,20... | collective-permute-start | bytes 491528 | tf_op jit(solution)/shard_map/ppermute | solution.py:424
  6.5 9.1 %collective-permute-start = (f32[5,32,256]{2,1,0:T(8,128)S(1)}, f32[5,32,256]{2,1,0:T(8,128)S(1)}, u32[]{:S(2)}, u32[]{:S(2)}) collective-permute-start(f32[5,32,256]{2,1,0:T(8,128)S(1)} %get-tuple-element.8.payload), channel_id=1, source_target_pairs={{0,8},{8,0},{16,24},{24,16},{1,9},{9,1},{17,25},{25,17},{2,10},{10... | collective-permute-start | bytes 491528 | tf_op jit(solution)/shard_map/ppermute | solution.py:424
  6.6 9.0 %all-to-all-start = ((f32[8,16,128]{2,1,0:T(8,128)}), f32[8,16,128]{2,1,0:T(8,128)S(1)}, u32[]{:S(2)}, u32[]{:S(2)}) async-start(f32[8,16,128]{2,1,0:T(8,128)} %bitcast), calls=%async_computation | async-start | bytes 131072 | tf_op jit(solution)/shard_map/all_to_all | solution.py:427

commit v14 on v13

--- a/solution.py
+++ b/solution.py
@@ -124,7 +124,7 @@
     return copies
 
 
-def pack_kernel(
+def pack(
     peers,
     coords,
     strain,
@@ -189,13 +189,31 @@
     lax.fori_loop(0, peers, message, 0, unroll=peers <= 8)
 
 
+def my_turn(parity):
+    return lax.rem(lax.axis_index("sub"), 2) == parity
+
+
+def pack_odd_kernel(peers, *refs):
+    pl.when(my_turn(1))(lambda: pack(peers, *refs))
+
+
+def pack_even_kernel(peers, *refs):
+    arguments, (payload_in, outbox_in, payload, outbox), scratch = refs[:7], refs[7:11], refs[11:]
+    pl.when(my_turn(0))(lambda: pack(peers, *arguments, payload, outbox, *scratch))
+
+    @pl.when(my_turn(1))
+    def take():
+        payload[...] = payload_in[...]
+        outbox[...] = outbox_in[...]
+
+
 def spread_rows(values):
     n = values.shape[1]
     wide = jnp.concatenate([values.astype(f32), jnp.zeros((1, 128 - n), f32)], axis=1)
     return jnp.broadcast_to(wide, (128, 128)).T[0:n]
 
 
-def own_kernel(pairs, payload, b_out, sums_ref, rows_ref, a_ref, s_ref, b_ref, local_pairs, sems):
+def own(pairs, payload, b_out, sums_ref, rows_ref, a_ref, s_ref, b_ref, local_pairs, sems):
     tiles = payload.shape[1]
     copies = fetch((payload.at[4, 0:8, 0:128],), (local_pairs,), sems)
     planes = [payload[k] for k in range(4)]
@@ -217,7 +235,7 @@
 
     column = lax.broadcasted_iota(jnp.int32, (1, 4 * depth), 1) // depth
 
-    def own(step, carry):
+    def alone(step, carry):
         for group in [8 * step + g for g in range(8)]:
             left, loads = turn_group(rows_ref, group)
             for i, s in enumerate(loads):
@@ -228,7 +246,7 @@
                 add_pair(sums_ref, t, a, s, b_ref[t])
         return carry
 
-    lax.fori_loop(0, tiles // 32, own, 0)
+    lax.fori_loop(0, tiles // 32, alone, 0)
 
     def listed(step, carry):
         for i in range(32):
@@ -241,10 +259,27 @@
     lax.fori_loop(0, pairs // 32, listed, 0)
 
 
+def own_even_kernel(pairs, payload, outbox, payload_out, outbox_out, b_out, sums_ref, *scratch):
+    payload_out[...] = payload[...]
+    outbox_out[...] = outbox[...]
+    pl.when(my_turn(0))(lambda: own(pairs, payload, b_out, sums_ref, *scratch))
+
+
+def own_odd_kernel(pairs, payload, b_in, sums_in, odd_up, odd_down, b_out, sums_ref, *scratch):
+    pl.when(my_turn(1))(lambda: own(pairs, payload, b_out, sums_ref, *scratch))
+
+    @pl.when(my_turn(0))
+    def take():
+        b_out[...] = b_in[...]
+        sums_ref[...] = sums_in[...]
+
+
 def rest_kernel(
     peers,
-    late,
-    soon,
+    odd_up,
+    odd_down,
+    even_up,
+    even_down,
     inbox,
     b_ref,
     sums_in,
@@ -297,7 +332,7 @@
 
     sums_ref[...] = sums_in[...]
 
-    def border(tiles_in, partner, shift):
+    def border(from_odd, from_even, partner, shift):
         def some(step, carry):
             for group in [8 * step + g for g in range(8)]:
                 left, loads = turn_group(rows_ref, group)
@@ -310,12 +345,11 @@
 
         @pl.when((partner >= 0) & (partner < count))
         def both():
-            put_source([tiles_in[k] for k in range(4)], rows_ref, 0)
+            put_source([jnp.where(my_turn(0), from_odd[k], from_even[k]) for k in range(4)], rows_ref, 0)
             lax.fori_loop(0, groups // 8, some, 0)
 
-    up = 1 - 2 * lax.rem(layer, 2)
-    border(soon, layer - up, -up)
-    border(late, layer + up, up)
+    border(odd_up, even_up, layer - 1, -1)
+    border(odd_down, even_down, layer + 1, 1)
 
     for copy in copies:
         copy.wait()
@@ -402,52 +436,81 @@
     params = pltpu.CompilerParams(vmem_limit_bytes=grant)
     block = 2 * points * points
 
-    payload, outbox = pl.pallas_call(
-        functools.partial(pack_kernel, peers),
-        out_shape=(
-            pltpu.VMEM((5, tiles, points), f32),
-            pltpu.VMEM((peers * halves * 8, 128), f32),
-        ),
-        in_specs=[anywhere] * 7,
-        out_specs=(in_vmem, in_vmem),
-        scratch_shapes=[pltpu.VMEM((tiles, points), f32)]
+    arguments = [in_hbm(v) for v in (coords, strain, tile_count, send_tile, remote_pairs, remote_count, local_pairs)]
+    messages = (pltpu.VMEM((5, tiles, points), f32), pltpu.VMEM((peers * halves * 8, 128), f32))
+    pack_scratch = (
+        [pltpu.VMEM((tiles, points), f32)]
         + [pltpu.SMEM(v.shape, jnp.int32) for v in (tile_count, send_tile, remote_pairs, remote_count)]
         + [pltpu.SMEM((peers,), jnp.int32)] * 2
         + [pltpu.VMEM((4 * halves * 8, 128), f32)]
-        + [pltpu.VMEM(local_pairs.shape, jnp.int32), pltpu.SemaphoreType.DMA((7,))],
+        + [pltpu.VMEM(local_pairs.shape, jnp.int32), pltpu.SemaphoreType.DMA((7,))]
+    )
+    payload, outbox = pl.pallas_call(
+        functools.partial(pack_odd_kernel, peers),
+        out_shape=messages,
+        in_specs=[anywhere] * 7,
+        out_specs=(in_vmem, in_vmem),
+        scratch_shapes=pack_scratch,
         compiler_params=params,
-        name="pack",
-    )(*(in_hbm(v) for v in (coords, strain, tile_count, send_tile, remote_pairs, remote_count, local_pairs)))
-
-    layers = lax.axis_size("sub")
-    late, soon = [
-        lax.ppermute(payload, "sub", [p for i in range(first, layers - 1, 2) for p in ((i, i + 1), (i + 1, i))])
-        for first in (0, 1)
+        name="pack_odd",
+    )(*arguments)
+
+    def send(tile_data, parity, step):
+        layers = lax.axis_size("sub")
+        return lax.ppermute(
+            tile_data, "sub", [(i, i + step) for i in range(parity, layers, 2) if 0 <= i + step < layers]
+        )
+
+    odd_up, odd_down = send(payload, 1, 1), send(payload, 1, -1)
+
+    payload, outbox = pl.pallas_call(
+        functools.partial(pack_even_kernel, peers),
+        out_shape=messages,
+        in_specs=[anywhere] * 7 + [in_vmem] * 2,
+        out_specs=(in_vmem, in_vmem),
+        scratch_shapes=pack_scratch,
+        compiler_params=params,
+        cost_estimate=pl.CostEstimate(flops=1 << 36, bytes_accessed=1 << 20, transcendentals=0),
+        name="pack_even",
+    )(*arguments, payload, outbox)
+
+    own_results = (
+        jax.ShapeDtypeStruct((tiles, depth, points), bf16),
+        jax.ShapeDtypeStruct((2, tiles, 8, points), f32),
+    )
+    own_scratch = [
+        pltpu.VMEM((halves, tiles * pitch, 128), f32),
+        pltpu.VMEM((tiles, points, 4 * depth), bf16),
+        pltpu.VMEM((tiles, points, 128), f32),
+        pltpu.VMEM((tiles, 4 * depth, points), bf16),
+        pltpu.SMEM((8, 128), f32),
+        pltpu.SemaphoreType.DMA((1,)),
     ]
+    own_cost = pl.CostEstimate(flops=0, bytes_accessed=1 << 16, transcendentals=0)
+    payload, outbox, b_own, sums = pl.pallas_call(
+        functools.partial(own_even_kernel, local_pairs.shape[1]),
+        out_shape=messages + own_results,
+        in_specs=[in_vmem] * 2,
+        out_specs=(in_vmem,) * 4,
+        scratch_shapes=own_scratch,
+        compiler_params=params,
+        cost_estimate=own_cost,
+        name="own_even",
+    )(payload, outbox)
+
+    even_up, even_down = send(payload, 0, 1), send(payload, 0, -1)
     inbox = lax.all_to_all(outbox, "blk", split_axis=0, concat_axis=0, tiled=True)
 
     b_own, sums = pl.pallas_call(
-        functools.partial(own_kernel, local_pairs.shape[1]),
-        out_shape=(
-            jax.ShapeDtypeStruct((tiles, depth, points), bf16),
-            jax.ShapeDtypeStruct((2, tiles, 8, points), f32),
-        ),
-        in_specs=[in_vmem],
+        functools.partial(own_odd_kernel, local_pairs.shape[1]),
+        out_shape=own_results,
+        in_specs=[in_vmem] * 3 + [anywhere] * 2,
         out_specs=(in_vmem,) * 2,
-        scratch_shapes=[
-            pltpu.VMEM((halves, tiles * pitch, 128), f32),
-            pltpu.VMEM((tiles, points, 4 * depth), bf16),
-            pltpu.VMEM((tiles, points, 128), f32),
-            pltpu.VMEM((tiles, 4 * depth, points), bf16),
-            pltpu.SMEM((8, 128), f32),
-            pltpu.SemaphoreType.DMA((1,)),
-        ],
+        scratch_shapes=own_scratch,
         compiler_params=params,
-        cost_estimate=pl.CostEstimate(
-            flops=3 * tiles * block * depth, bytes_accessed=1 << 20, transcendentals=3 * tiles * points * points
-        ),
-        name="own",
-    )(payload)
+        cost_estimate=own_cost,
+        name="own_odd",
+    )(payload, b_own, sums, odd_up, odd_down)
 
     damage, parts = pl.pallas_call(
         functools.partial(rest_kernel, peers),
@@ -455,7 +518,7 @@
             jax.ShapeDtypeStruct((tiles, points), f32),
             jax.ShapeDtypeStruct((peers, 128), f32),
         ),
-        in_specs=[in_vmem] * 6 + [anywhere] * 8,
+        in_specs=[in_vmem] * 8 + [anywhere] * 8,
         out_specs=(anywhere, in_vmem),
         scratch_shapes=[pltpu.VMEM(v.shape, v.dtype) for v in (strain, history, corner_load, external, tile_sub, corner_map)]
         + [
@@ -472,8 +535,10 @@
         ),
         name="rest",
     )(
-        late,
-        soon,
+        odd_up,
+        odd_down,
+        even_up,
+        even_down,
         inbox,
         b_own,
         sums,

time: 33.5 us -> 38.7 us (1.16)
  the two profiles are of different devices: /device:TPU:8 before, /device:TPU:16 now
where the time goes in v14:
time: 38.7 us; the launch traced here: 38.4 us
  Pallas kernels  15.6 us (40%)
  starting transfers between devices  8.92 us (23%)
  blocking collectives  7.02 us (18%)
  waiting for transfers between devices  4.9 us (13%)
  between operations  1.36 us (4%)
  other arithmetic  0.54 us (1%)
    pallas_call x1, Pallas kernels, per_device(): pl.pallas_call(functools.partial(rest_kernel, peers), out_shape=(jax.Shap...  8.44 us
    all_to_all x1, blocking collectives, per_device(): lax.all_to_all(parts, 'blk', split_axis=0, concat_axis=0, tiled=True)  7.02 us
    pallas_call x1, Pallas kernels, per_device(): pl.pallas_call(functools.partial(own_even_kernel, local_pairs.shape[1]),...  5.91 us
    ppermute x4, starting transfers between devices, send(): lax.ppermute(tile_data, 'sub', [(i, i + step) for i in range(parity, laye...  5.18 us
    all_to_all x1, waiting for transfers between devices, per_device(): lax.all_to_all(outbox, 'blk', split_axis=0, concat_axis=0, tiled=True)  4.89 us
    all_to_all x1, starting transfers between devices, per_device(): lax.all_to_all(outbox, 'blk', split_axis=0, concat_axis=0, tiled=True)  3.74 us
    pallas_call x1, Pallas kernels, per_device(): pl.pallas_call(functools.partial(pack_even_kernel, peers), out_shape=mess...  1.1 us
  transfers between devices with their start and end apart: 5, of which 1 were waited for; matrix products, arithmetic and copies ran while one was open for 0% of the time, Pallas kernels for 19%

profile of v14, /device:TPU:16, one launch (start us, length us, event | category | flops | bytes accessed | tf_op | source)
XLA Modules:
  0.0 38.4 jit_solution(7800023423950967601)
XLA Ops:
  1.3 0.1 pack_odd.1
  1.4 1.3 %collective-permute-start = (f32[5,32,256]{2,1,0:T(8,128)S(1)}, f32[5,32,256]{2,1,0:T(8,128)S(1)}, u32[]{:S(2)}, u32[]{:S(2)}) collective-permute-start(f32[5,32,256]{2,1,0:T(8,128)S(1)} %get-tuple-element.14.refs_7_), channel_id=1, source_target_pairs={{8,16},{9,17},{10,18},{11,19},{12,20},{13,21},{14,22},{15,23}} | collective-permute-start | bytes 491528 | tf_op jit(solution)/shard_map/ppermute | solution.py:460
  2.7 1.3 %collective-permute-start.1 = (f32[5,32,256]{2,1,0:T(8,128)S(1)}, f32[5,32,256]{2,1,0:T(8,128)S(1)}, u32[]{:S(2)}, u32[]{:S(2)}) collective-permute-start(f32[5,32,256]{2,1,0:T(8,128)S(1)} %get-tuple-element.14.refs_7_), channel_id=1, source_target_pairs={{8,0},{24,16},{9,1},{25,17},{10,2},{26,18},{11,3},{27,19},{12,4},{... | collective-permute-start | bytes 491528 | tf_op jit(solution)/shard_map/ppermute | solution.py:460
  4.0 1.1 %pack_even.1 = (f32[5,32,256]{2,1,0:T(8,128)S(1)}, f32[128,128]{1,0:T(8,128)S(1)}) custom-call(f32[3,32,256]{2,1,0:T(8,128)} %refs_0_.3, f32[32,256]{1,0:T(8,128)} %refs_1_.3, s32[32]{0:T(128)} %refs_2_.3, s32[8]{0:T(128)} %send_tile_in.1, s32[2,8]{1,0:T(2,128)} %remote_pairs_in.1, s32[1]{0:T(128)S(6)} %copy.15.refs_5_.remote_count_in, s32[2,32]{1,0:T(2,128)} %refs_6_.3, ...), custom_call_target="tpu_custom_call" | custom-call | flops 68719476736 | bytes 1048576 | tf_op jit(solution)/shard_map/pack_even/pallas_call | solution.py:466
  5.1 5.9 %own_even.1 = (f32[5,32,256]{2,1,0:T(8,128)S(1)}, f32[128,128]{1,0:T(8,128)}, bf16[32,32,256]{2,1,0:T(8,128)(2,1)S(1)}, f32[2,32,8,256]{3,2,1,0:T(8,128)S(1)}) custom-call(f32[5,32,256]{2,1,0:T(8,128)S(1)} %get-tuple-element.16.payload, f32[128,128]{1,0:T(8,128)S(1)} %get-tuple-element.17.outbox), custom_call_target="tpu_custom_call" | custom-call | bytes 65536 | tf_op jit(solution)/shard_map/own_even/pallas_call | solution.py:490
  11.0 1.3 %collective-permute-start.2 = (f32[5,32,256]{2,1,0:T(8,128)S(1)}, f32[5,32,256]{2,1,0:T(8,128)S(1)}, u32[]{:S(2)}, u32[]{:S(2)}) collective-permute-start(f32[5,32,256]{2,1,0:T(8,128)S(1)} %get-tuple-element.18.payload), channel_id=1, source_target_pairs={{0,8},{16,24},{1,9},{17,25},{2,10},{18,26},{3,11},{19,27},{4,12},{... | collective-permute-start | bytes 491528 | tf_op jit(solution)/shard_map/ppermute | solution.py:460
  12.3 1.3 %collective-permute-start.3 = (f32[5,32,256]{2,1,0:T(8,128)S(1)}, f32[5,32,256]{2,1,0:T(8,128)S(1)}, u32[]{:S(2)}, u32[]{:S(2)}) collective-permute-start(f32[5,32,256]{2,1,0:T(8,128)S(1)} %get-tuple-element.18.payload), channel_id=1, source_target_pairs={{16,8},{17,9},{18,10},{19,11},{20,12},{21,13},{22,14},{23,15}} | collective-permute-start | bytes 491528 | tf_op jit(solution)/shard_map/ppermute | solution.py:460
  13.6 3.7 %all-to-all-start = ((f32[8,16,128]{2,1,0:T(8,128)}), f32[8,16,128]{2,1,0:T(8,128)S(1)}, u32[]{:S(2)}, u32[]{:S(2)}) async-start(f32[8,16,128]{2,1,0:T(8,128)} %bitcast), calls=%async_computation | async-start | bytes 131072 | tf_op jit(solution)/shard_map/all_to_all | solution.py:502
  17.3 0.0 collective-permute-done.odd_up
  17.4 0.0 collective-permute-done.1.odd_down
  17.4 0.1 own_odd.1
  17.5 4.9 %all-to-all-done = f32[8,16,128]{2,1,0:T(8,128)S(1)} async-done(((f32[8,16,128]{2,1,0:T(8,128)}), f32[8,16,128]{2,1,0:T(8,128)S(1)}, u32[]{:S(2)}, u32[]{:S(2)}) %all-to-all-start) | async-done | bytes 65568 | tf_op jit(solution)/shard_map/all_to_all | solution.py:502
  22.4 0.0 collective-permute-done.2.even_up
  22.4 0.0 collective-permute-done.3.even_down
  22.4 8.4 %rest.1 = (f32[32,256]{1,0:T(8,128)}, f32[8,128]{1,0:T(8,128)S(1)}) custom-call(f32[5,32,256]{2,1,0:T(8,128)S(1)} %collective-permute-done.odd_up, f32[5,32,256]{2,1,0:T(8,128)S(1)} %collective-permute-done.1.odd_down, f32[5,32,256]{2,1,0:T(8,128)S(1)} %collective-permute-done.2.even_up, f32[5,32,256]{2,1,0:T(8,128)S(1)} %collective-permute-done.3.even_down, ...), custom_call_target="tpu_custom_call" | custom-call | flops 536870912 | bytes 2097152 | tf_op jit(solution)/shard_map/rest/pallas_call | solution.py:515
  30.8 7.0 %all_to_all.20 = f32[8,1,128]{2,1,0:T(1,128)S(1)} all-to-all(f32[8,1,128]{2,1,0:T(1,128)S(1)} %bitcast.6), channel_id=1, replica_groups=mesh['sub'=4,'blk'=8] {'blk'}, dimensions={0} | all-to-all | bytes 8192 | tf_op jit(solution)/shard_map/all_to_all | solution.py:560
  37.8 0.5 %reduce_sum.9 = f32[128]{0:T(128)} reduce(f32[8,1,128]{2,1,0:T(1,128)S(1)} %all_to_all.20, f32[]{:T(128)} %constant.0.clone.1), dimensions={0,1}, to_apply=%region_0.0 | reduce | flops 896 | bytes 4612 | tf_op jit(solution)/shard_map/reduce_sum | solution.py:561
Async XLA Ops:
  1.4 16.0 %collective-permute-start = (f32[5,32,256]{2,1,0:T(8,128)S(1)}, f32[5,32,256]{2,1,0:T(8,128)S(1)}, u32[]{:S(2)}, u32[]{:S(2)}) collective-permute-start(f32[5,32,256]{2,1,0:T(8,128)S(1)} %get-tuple-element.14.refs_7_), channel_id=1, source_target_pairs={{8,16},{9,17},{10,18},{11,19},{12,20},{13,21},{14,22},{15,23}} | collective-permute-start | bytes 491528 | tf_op jit(solution)/shard_map/ppermute | solution.py:460
  2.7 14.7 %collective-permute-start.1 = (f32[5,32,256]{2,1,0:T(8,128)S(1)}, f32[5,32,256]{2,1,0:T(8,128)S(1)}, u32[]{:S(2)}, u32[]{:S(2)}) collective-permute-start(f32[5,32,256]{2,1,0:T(8,128)S(1)} %get-tuple-element.14.refs_7_), channel_id=1, source_target_pairs={{8,0},{24,16},{9,1},{25,17},{10,2},{26,18},{11,3},{27,19},{12,4},{... | collective-permute-start | bytes 491528 | tf_op jit(solution)/shard_map/ppermute | solution.py:460
  11.0 11.4 %collective-permute-start.2 = (f32[5,32,256]{2,1,0:T(8,128)S(1)}, f32[5,32,256]{2,1,0:T(8,128)S(1)}, u32[]{:S(2)}, u32[]{:S(2)}) collective-permute-start(f32[5,32,256]{2,1,0:T(8,128)S(1)} %get-tuple-element.18.payload), channel_id=1, source_target_pairs={{0,8},{16,24},{1,9},{17,25},{2,10},{18,26},{3,11},{19,27},{4,12},{... | collective-permute-start | bytes 491528 | tf_op jit(solution)/shard_map/ppermute | solution.py:460
  12.3 10.1 %collective-permute-start.3 = (f32[5,32,256]{2,1,0:T(8,128)S(1)}, f32[5,32,256]{2,1,0:T(8,128)S(1)}, u32[]{:S(2)}, u32[]{:S(2)}) collective-permute-start(f32[5,32,256]{2,1,0:T(8,128)S(1)} %get-tuple-element.18.payload), channel_id=1, source_target_pairs={{16,8},{17,9},{18,10},{19,11},{20,12},{21,13},{22,14},{23,15}} | collective-permute-start | bytes 491528 | tf_op jit(solution)/shard_map/ppermute | solution.py:460
  13.6 8.8 %all-to-all-start = ((f32[8,16,128]{2,1,0:T(8,128)}), f32[8,16,128]{2,1,0:T(8,128)S(1)}, u32[]{:S(2)}, u32[]{:S(2)}) async-start(f32[8,16,128]{2,1,0:T(8,128)} %bitcast), calls=%async_computation | async-start | bytes 131072 | tf_op jit(solution)/shard_map/all_to_all | solution.py:502

commit v15 on v13

--- a/solution.py
+++ b/solution.py
@@ -69,6 +69,13 @@
     rows += [ones, ones, ones] + list(pieces(-norm))
     rows += [jnp.zeros_like(norm)] * (depth - len(rows))
     put_rows(rows_ref, 0, rows)
+
+
+def steps(count, body):
+    if count == 1:
+        body(0, 0)
+    else:
+        lax.fori_loop(0, count, body, 0)
 
 
 def turn_group(rows_ref, group):
@@ -104,17 +111,6 @@
         num, den = num * live, den * live
     sums_ref[0, t] = sums_ref[0, t] + num
     sums_ref[1, t] = sums_ref[1, t] + den
-
-
-def repeat_target(compact, b_ref):
-    def some_tiles(step, carry):
-        for t in [step * 4 + i for i in range(4)]:
-            block = compact[t]
-            for j in range(4):
-                b_ref[t, depth * j : depth * (j + 1), :] = block
-        return carry
-
-    lax.fori_loop(0, compact.shape[0] // 4, some_tiles, 0)
 
 
 def fetch(sources, targets, sems):
@@ -201,15 +197,14 @@
     planes = [payload[k] for k in range(4)]
     put_target(planes, rows_ref)
 
-    def set_target(group, carry):
-        for t in [group * 4 + i for i in range(4)]:
-            rows = pl.ds(t * pitch, depth)
-            for half in range(rows_ref.shape[0]):
-                b_out[t, :, half * 128 : (half + 1) * 128] = rows_ref[half, rows, :].astype(bf16)
-        return carry
-
-    lax.fori_loop(0, tiles // 4, set_target, 0)
-    repeat_target(b_out, b_ref)
+    for t in range(tiles):
+        rows = slice(t * pitch, t * pitch + depth)
+        for half in range(rows_ref.shape[0]):
+            cut = slice(half * 128, (half + 1) * 128)
+            block = rows_ref[half, rows, :].astype(bf16)
+            b_out[t, :, cut] = block
+            for j in range(4):
+                b_ref[t, depth * j : depth * (j + 1), cut] = block
     put_source(planes, rows_ref, 0)
     sums_ref[...] = jnp.zeros_like(sums_ref)
     for copy in copies:
@@ -228,7 +223,7 @@
                 add_pair(sums_ref, t, a, s, b_ref[t])
         return carry
 
-    lax.fori_loop(0, tiles // 32, own, 0)
+    steps(tiles // 32, own)
 
     def listed(step, carry):
         for i in range(32):
@@ -238,7 +233,7 @@
             add_pair(sums_ref, one, a_ref[two], s_ref[two], b_ref[one])
         return carry
 
-    lax.fori_loop(0, pairs // 32, listed, 0)
+    steps(pairs // 32, listed)
 
 
 def rest_kernel(
@@ -311,7 +306,7 @@
         @pl.when((partner >= 0) & (partner < count))
         def both():
             put_source([tiles_in[k] for k in range(4)], rows_ref, 0)
-            lax.fori_loop(0, groups // 8, some, 0)
+            steps(groups // 8, some)
 
     up = 1 - 2 * lax.rem(layer, 2)
     border(soon, layer - up, -up)
@@ -346,7 +341,7 @@
                 add_pair(sums_ref, t, left, s, placed(b_ref[t], i), far_live[group * 4 + i].astype(f32))
         return carry
 
-    lax.fori_loop(0, 2 * peers // 16, far, 0)
+    steps(2 * peers // 16, far)
 
     valid = (payload[3] > 0.0).astype(f32)
     num, den = jnp.sum(sums_ref[...], axis=2)

time: 33.5 us -> 33.7 us (level)
  no operation moved by 1% of the time
where the time goes in v15:
time: 33.7 us; the launch traced here: 33.4 us
  Pallas kernels  15.6 us (46%)
  blocking collectives  8.66 us (26%)
  starting transfers between devices  7.29 us (22%)
  between operations  1.34 us (4%)
  other arithmetic  0.54 us (2%)
    all_to_all x1, blocking collectives, per_device(): lax.all_to_all(parts, 'blk', split_axis=0, concat_axis=0, tiled=True)  8.66 us
    pallas_call x1, Pallas kernels, per_device(): pl.pallas_call(functools.partial(rest_kernel, peers), out_shape=(jax.Shap...  8.58 us
    pallas_call x1, Pallas kernels, per_device(): pl.pallas_call(functools.partial(own_kernel, local_pairs.shape[1]), out_s...  5.28 us
    all_to_all x1, starting transfers between devices, per_device(): lax.all_to_all(outbox, 'blk', split_axis=0, concat_axis=0, tiled=True)  3.74 us
    ppermute x2, starting transfers between devices, per_device(): lax.ppermute(payload, 'sub', [p for i in range(first, layers - 1, 2) for...  3.56 us
    pallas_call x1, Pallas kernels, per_device(): pl.pallas_call(functools.partial(pack_kernel, peers), out_shape=(pltpu.VM...  1.69 us
  transfers between devices with their start and end apart: 3, of which 0 were waited for; matrix products, arithmetic and copies ran while one was open for 0% of the time, Pallas kernels for 16%

profile of v15, /device:TPU:8, one launch (start us, length us, event | category | flops | bytes accessed | tf_op | source)
XLA Modules:
  0.0 33.4 jit_solution(9042266658102690726)
XLA Ops:
  1.3 1.7 %pack.1 = (f32[5,32,256]{2,1,0:T(8,128)S(1)}, f32[128,128]{1,0:T(8,128)}) custom-call(f32[3,32,256]{2,1,0:T(8,128)} %coords.1, f32[32,256]{1,0:T(8,128)} %strain.1, s32[32]{0:T(128)} %tile_count_in.1, s32[8]{0:T(128)} %send_tile_in.3, s32[2,8]{1,0:T(2,128)} %remote_pairs_in.3, s32[1]{0:T(128)S(6)} %copy.15.remote_count_in, s32[2,32]{1,0:T(2,128)} %local_pairs_in.1), custom_call_target="tpu_custom_call" | custom-call | tf_op jit(solution)/shard_map/pack/pallas_call | solution.py:400
  3.0 3.5 %collective-permute-start.1 = (f32[5,32,256]{2,1,0:T(8,128)S(1)}, f32[5,32,256]{2,1,0:T(8,128)S(1)}, u32[]{:S(2)}, u32[]{:S(2)}) collective-permute-start(f32[5,32,256]{2,1,0:T(8,128)S(1)} %get-tuple-element.8.payload), channel_id=1, source_target_pairs={{8,16},{16,8},{9,17},{17,9},{10,18},{18,10},{11,19},{19,11},{12,20... | collective-permute-start | bytes 491528 | tf_op jit(solution)/shard_map/ppermute | solution.py:419
  6.5 0.1 collective-permute-start
  6.6 3.7 %all-to-all-start = ((f32[8,16,128]{2,1,0:T(8,128)}), f32[8,16,128]{2,1,0:T(8,128)S(1)}, u32[]{:S(2)}, u32[]{:S(2)}) async-start(f32[8,16,128]{2,1,0:T(8,128)} %bitcast), calls=%async_computation | async-start | bytes 131072 | tf_op jit(solution)/shard_map/all_to_all | solution.py:422
  10.3 5.3 %own.1 = (bf16[32,32,256]{2,1,0:T(8,128)(2,1)S(1)}, f32[2,32,8,256]{3,2,1,0:T(8,128)S(1)}) custom-call(f32[5,32,256]{2,1,0:T(8,128)S(1)} %get-tuple-element.8.payload), custom_call_target="tpu_custom_call" | custom-call | flops 402653184 | bytes 1048576 | tf_op jit(solution)/shard_map/own/pallas_call | solution.py:424
  15.6 0.0 all-to-all-done
  15.6 0.0 collective-permute-done.1.soon
  15.6 0.0 collective-permute-done.late
  15.6 8.6 %rest.1 = (f32[32,256]{1,0:T(8,128)}, f32[8,128]{1,0:T(8,128)S(1)}) custom-call(f32[5,32,256]{2,1,0:T(8,128)S(1)} %collective-permute-done.late, f32[5,32,256]{2,1,0:T(8,128)S(1)} %collective-permute-done.1.soon, f32[128,128]{1,0:T(8,128)S(1)} %bitcast.5, bf16[32,32,256]{2,1,0:T(8,128)(2,1)S(1)} %get-tuple-element.10.b_ref, ...), custom_call_target="tpu_custom_call" | custom-call | flops 536870912 | bytes 2097152 | tf_op jit(solution)/shard_map/rest/pallas_call | solution.py:447
  24.2 8.7 %all_to_all.20 = f32[8,1,128]{2,1,0:T(1,128)S(1)} all-to-all(f32[8,1,128]{2,1,0:T(1,128)S(1)} %bitcast.6), channel_id=1, replica_groups=mesh['sub'=4,'blk'=8] {'blk'}, dimensions={0} | all-to-all | bytes 8192 | tf_op jit(solution)/shard_map/all_to_all | solution.py:490
  32.9 0.5 %reduce_sum.9 = f32[128]{0:T(128)} reduce(f32[8,1,128]{2,1,0:T(1,128)S(1)} %all_to_all.20, f32[]{:T(128)} %constant.0.clone.1), dimensions={0,1}, to_apply=%region_0.0 | reduce | flops 896 | bytes 4612 | tf_op jit(solution)/shard_map/reduce_sum | solution.py:491
Async XLA Ops:
  3.0 12.6 %collective-permute-start.1 = (f32[5,32,256]{2,1,0:T(8,128)S(1)}, f32[5,32,256]{2,1,0:T(8,128)S(1)}, u32[]{:S(2)}, u32[]{:S(2)}) collective-permute-start(f32[5,32,256]{2,1,0:T(8,128)S(1)} %get-tuple-element.8.payload), channel_id=1, source_target_pairs={{8,16},{16,8},{9,17},{17,9},{10,18},{18,10},{11,19},{19,11},{12,20... | collective-permute-start | bytes 491528 | tf_op jit(solution)/shard_map/ppermute | solution.py:419
  6.5 9.1 %collective-permute-start = (f32[5,32,256]{2,1,0:T(8,128)S(1)}, f32[5,32,256]{2,1,0:T(8,128)S(1)}, u32[]{:S(2)}, u32[]{:S(2)}) collective-permute-start(f32[5,32,256]{2,1,0:T(8,128)S(1)} %get-tuple-element.8.payload), channel_id=1, source_target_pairs={{0,8},{8,0},{16,24},{24,16},{1,9},{9,1},{17,25},{25,17},{2,10},{10... | collective-permute-start | bytes 491528 | tf_op jit(solution)/shard_map/ppermute | solution.py:419
  6.6 9.0 %all-to-all-start = ((f32[8,16,128]{2,1,0:T(8,128)}), f32[8,16,128]{2,1,0:T(8,128)S(1)}, u32[]{:S(2)}, u32[]{:S(2)}) async-start(f32[8,16,128]{2,1,0:T(8,128)} %bitcast), calls=%async_computation | async-start | bytes 131072 | tf_op jit(solution)/shard_map/all_to_all | solution.py:422

commit v16 on v13

--- a/solution.py
+++ b/solution.py
@@ -133,7 +133,7 @@
     remote_pairs_in,
     remote_count_in,
     local_pairs_in,
-    payload,
+    twice,
     outbox,
     strain_here,
     tile_count,
@@ -147,6 +147,7 @@
     sems,
 ):
     tiles, points = strain.shape
+    payload = twice.at[0]
     copies = fetch(
         (coords, strain, tile_count_in, send_tile_in, remote_pairs_in, remote_count_in, local_pairs_in),
         (payload.at[0:3], strain_here, tile_count, send_tile, remote_pairs, remote_count, local_pairs),
@@ -160,6 +161,7 @@
     for t in range(tiles):
         payload[3, t : t + 1, :] = jnp.where(lane < tile_count[t], strain_here[t : t + 1, :], 0.0)
 
+    twice[1] = twice[0]
     halves = points // 128
     for k in range(4):
         for half in range(halves):
@@ -195,7 +197,8 @@
     return jnp.broadcast_to(wide, (128, 128)).T[0:n]
 
 
-def own_kernel(pairs, payload, b_out, sums_ref, rows_ref, a_ref, s_ref, b_ref, local_pairs, sems):
+def own_kernel(pairs, twice, b_out, sums_ref, rows_ref, a_ref, s_ref, b_ref, local_pairs, sems):
+    payload = twice.at[0]
     tiles = payload.shape[1]
     copies = fetch((payload.at[4, 0:8, 0:128],), (local_pairs,), sems)
     planes = [payload[k] for k in range(4)]
@@ -248,7 +251,7 @@
     inbox,
     b_ref,
     sums_in,
-    payload,
+    twice,
     history_in,
     corner_load_in,
     external_in,
@@ -276,6 +279,7 @@
     sems,
 ):
     tiles, points = history.shape
+    payload = twice.at[0]
     halves = points // 128
     groups = tiles // 4
     count = lax.axis_size("sub")
@@ -297,7 +301,7 @@
 
     sums_ref[...] = sums_in[...]
 
-    def border(tiles_in, partner, shift):
+    def border(tiles_in, place, partner, shift):
         def some(step, carry):
             for group in [8 * step + g for g in range(8)]:
                 left, loads = turn_group(rows_ref, group)
@@ -310,12 +314,13 @@
 
         @pl.when((partner >= 0) & (partner < count))
         def both():
-            put_source([tiles_in[k] for k in range(4)], rows_ref, 0)
+            put_source([tiles_in[place, k] for k in range(4)], rows_ref, 0)
             lax.fori_loop(0, groups // 8, some, 0)
 
     up = 1 - 2 * lax.rem(layer, 2)
-    border(soon, layer - up, -up)
-    border(late, layer + up, up)
+    odd = lax.rem(layer, 2)
+    border(soon, odd, layer - up, -up)
+    border(late, 1 - odd, layer + up, up)
 
     for copy in copies:
         copy.wait()
@@ -405,7 +410,7 @@
     payload, outbox = pl.pallas_call(
         functools.partial(pack_kernel, peers),
         out_shape=(
-            pltpu.VMEM((5, tiles, points), f32),
+            pltpu.VMEM((2, 5, tiles, points), f32),
             pltpu.VMEM((peers * halves * 8, 128), f32),
         ),
         in_specs=[anywhere] * 7,
@@ -420,9 +425,16 @@
     )(*(in_hbm(v) for v in (coords, strain, tile_count, send_tile, remote_pairs, remote_count, local_pairs)))
 
     layers = lax.axis_size("sub")
-    late, soon = [
-        lax.ppermute(payload, "sub", [p for i in range(first, layers - 1, 2) for p in ((i, i + 1), (i + 1, i))])
-        for first in (0, 1)
+    soon, late = [
+        lax.all_to_all(
+            payload,
+            "sub",
+            split_axis=0,
+            concat_axis=0,
+            axis_index_groups=[sorted((i, (i + 1) % layers)) for i in range(first, layers, 2)],
+            tiled=True,
+        )
+        for first in (1, 0)
     ]
     inbox = lax.all_to_all(outbox, "blk", split_axis=0, concat_axis=0, tiled=True)
 

time: 33.5 us -> 51.6 us (1.54)
  blocking collectives: 8.66 us -> 28.5 us
  starting transfers between devices: 7.29 us -> 3.45 us
  Pallas kernels: 15.4 us -> 17.4 us
    all_to_all x0 -> x2, blocking collectives: none -> 21.4 us  [the longest x1 12.9 us: per_device(): lax.all_to_all(payload, 'sub', split_axis=0, concat_axis=0, axis_index_gr...]
    ppermute x2 -> x0, starting transfers between devices: 3.56 us -> none  [per_device(): lax.ppermute(payload, 'sub', [p for i in range(first, layers - 1, 2) for...]
    all_to_all x1, blocking collectives: 8.66 us -> 7.02 us  [per_device(): lax.all_to_all(parts, 'blk', split_axis=0, concat_axis=0, tiled=True)]
    pallas_call x1, Pallas kernels: 5.27 us -> 6.25 us  [per_device(): pl.pallas_call(functools.partial(own_kernel, local_pairs.shape[1]), out_s...]
    pallas_call x1, Pallas kernels: 8.41 us -> 9.39 us  [per_device(): pl.pallas_call(functools.partial(rest_kernel, peers), out_shape=(jax.Shap...]
  transfers between devices with their start and end apart: 3 -> 1, of which waited for: 0 -> 0; matrix products, arithmetic and copies ran while one was open for 0% -> 0% of each run, Pallas kernels for 16% -> 12%
where the time goes in v16:
time: 51.6 us; the launch traced here: 51.2 us
  blocking collectives  28.5 us (55%)
  Pallas kernels  17.4 us (34%)
  starting transfers between devices  3.45 us (7%)
  between operations  1.32 us (3%)
  other arithmetic  0.54 us (1%)
    all_to_all x1, blocking collectives, per_device(): lax.all_to_all(payload, 'sub', split_axis=0, concat_axis=0, axis_index_gr...  12.9 us
    pallas_call x1, Pallas kernels, per_device(): pl.pallas_call(functools.partial(rest_kernel, peers), out_shape=(jax.Shap...  9.39 us
    all_to_all x1, blocking collectives, per_device(): lax.all_to_all(outbox, 'blk', split_axis=0, concat_axis=0, tiled=True)  8.54 us
    all_to_all x1, blocking collectives, per_device(): lax.all_to_all(parts, 'blk', split_axis=0, concat_axis=0, tiled=True)  7.02 us
    pallas_call x1, Pallas kernels, per_device(): pl.pallas_call(functools.partial(own_kernel, local_pairs.shape[1]), out_s...  6.25 us
    all_to_all x1, starting transfers between devices, per_device(): lax.all_to_all(payload, 'sub', split_axis=0, concat_axis=0, axis_index_gr...  3.45 us
    pallas_call x1, Pallas kernels, per_device(): pl.pallas_call(functools.partial(pack_kernel, peers), out_shape=(pltpu.VM...  1.8 us
  transfers between devices with their start and end apart: 1, of which 0 were waited for; matrix products, arithmetic and copies ran while one was open for 0% of the time, Pallas kernels for 12%

profile of v16, /device:TPU:8, one launch (start us, length us, event | category | flops | bytes accessed | tf_op | source)
XLA Modules:
  0.0 51.2 jit_solution(17927341201015961078)
XLA Ops:
  1.3 1.8 %pack.1 = (f32[2,5,32,256]{3,2,1,0:T(8,128)}, f32[128,128]{1,0:T(8,128)S(1)}) custom-call(f32[3,32,256]{2,1,0:T(8,128)} %coords.1, f32[32,256]{1,0:T(8,128)} %strain.1, s32[32]{0:T(128)} %tile_count_in.1, s32[8]{0:T(128)} %send_tile_in.3, s32[2,8]{1,0:T(2,128)} %remote_pairs_in.3, s32[1]{0:T(128)S(6)} %copy.15.remote_count_in, s32[2,32]{1,0:T(2,128)} %local_pairs_in.1), custom_call_target="tpu_custom_call" | custom-call | tf_op jit(solution)/shard_map/pack/pallas_call | solution.py:410
  3.1 8.5 %all_to_all.30 = f32[8,16,128]{2,1,0:T(8,128)S(1)} all-to-all(f32[8,16,128]{2,1,0:T(8,128)S(1)} %bitcast.6), channel_id=1, replica_groups=mesh['sub'=4,'blk'=8] {'blk'}, dimensions={0} | all-to-all | bytes 131072 | tf_op jit(solution)/shard_map/all_to_all | solution.py:439
  11.6 12.9 %all_to_all.31.soon = f32[2,5,32,256]{3,2,1,0:T(8,128)S(1)} all-to-all(f32[2,5,32,256]{3,2,1,0:T(8,128)} %get-tuple-element.8.twice), channel_id=1, replica_groups={{8,16},{0,24},{9,17},{1,25},{10,18},{2,26},{11,19},{3,27},{12,20},{4,28..., dimensions={0} | all-to-all | bytes 655360 | tf_op jit(solution)/shard_map/all_to_all | solution.py:429
  24.5 3.4 %all-to-all-start = ((f32[2,5,32,256]{3,2,1,0:T(8,128)}), f32[2,5,32,256]{3,2,1,0:T(8,128)S(1)}, u32[]{:S(2)}, u32[]{:S(2)}) async-start(f32[2,5,32,256]{3,2,1,0:T(8,128)} %get-tuple-element.8.twice), calls=%async_computation | async-start | bytes 655360 | tf_op jit(solution)/shard_map/all_to_all | solution.py:429
  28.0 6.2 %own.1 = (bf16[32,32,256]{2,1,0:T(8,128)(2,1)S(1)}, f32[2,32,8,256]{3,2,1,0:T(8,128)S(1)}) custom-call(f32[2,5,32,256]{3,2,1,0:T(8,128)} %get-tuple-element.8.twice), custom_call_target="tpu_custom_call" | custom-call | flops 402653184 | bytes 1048576 | tf_op jit(solution)/shard_map/own/pallas_call | solution.py:441
  34.2 0.0 all-to-all-done.late
  34.3 9.4 %rest.1 = (f32[32,256]{1,0:T(8,128)}, f32[8,128]{1,0:T(8,128)S(1)}) custom-call(f32[2,5,32,256]{3,2,1,0:T(8,128)S(1)} %all-to-all-done.late, f32[2,5,32,256]{3,2,1,0:T(8,128)S(1)} %all_to_all.31.soon, f32[128,128]{1,0:T(8,128)S(1)} %bitcast.5, bf16[32,32,256]{2,1,0:T(8,128)(2,1)S(1)} %get-tuple-element.10.b_ref, ...), custom_call_target="tpu_custom_call" | custom-call | flops 536870912 | bytes 2097152 | tf_op jit(solution)/shard_map/rest/pallas_call | solution.py:464
  43.6 7.0 %all_to_all.32 = f32[8,1,128]{2,1,0:T(1,128)S(1)} all-to-all(f32[8,1,128]{2,1,0:T(1,128)S(1)} %bitcast.7), channel_id=1, replica_groups=mesh['sub'=4,'blk'=8] {'blk'}, dimensions={0} | all-to-all | bytes 8192 | tf_op jit(solution)/shard_map/all_to_all | solution.py:507
  50.7 0.5 %reduce_sum.9 = f32[128]{0:T(128)} reduce(f32[8,1,128]{2,1,0:T(1,128)S(1)} %all_to_all.32, f32[]{:T(128)} %constant.0.clone.1), dimensions={0,1}, to_apply=%region_0.0 | reduce | flops 896 | bytes 4612 | tf_op jit(solution)/shard_map/reduce_sum | solution.py:508
Async XLA Ops:
  24.5 9.7 %all-to-all-start = ((f32[2,5,32,256]{3,2,1,0:T(8,128)}), f32[2,5,32,256]{3,2,1,0:T(8,128)S(1)}, u32[]{:S(2)}, u32[]{:S(2)}) async-start(f32[2,5,32,256]{3,2,1,0:T(8,128)} %get-tuple-element.8.twice), calls=%async_computation | async-start | bytes 655360 | tf_op jit(solution)/shard_map/all_to_all | solution.py:429

commit v17 on v13

--- a/solution.py
+++ b/solution.py
@@ -97,13 +97,19 @@
     return fold(weight * load), fold(weight)
 
 
-def add_pair(sums_ref, t, a, s, b, live=None):
-    weight = jnp.exp2(jnp.dot(a, b, preferred_element_type=f32))
-    num, den = column_sums(weight, s)
+def add_pair(sums_ref, t, a, s, b, live=None, first=False, rows=None):
+    num, den = 0.0, 0.0
+    rows = rows or a.shape[0]
+    for lo in range(0, a.shape[0], rows):
+        weight = jnp.exp2(jnp.dot(a[lo : lo + rows], b, preferred_element_type=f32))
+        more_num, more_den = column_sums(weight, s[lo : lo + rows])
+        num, den = num + more_num, den + more_den
     if live is not None:
         num, den = num * live, den * live
-    sums_ref[0, t] = sums_ref[0, t] + num
-    sums_ref[1, t] = sums_ref[1, t] + den
+    if not first:
+        num, den = sums_ref[0, t] + num, sums_ref[1, t] + den
+    sums_ref[0, t] = num
+    sums_ref[1, t] = den
 
 
 def repeat_target(compact, b_ref):
@@ -211,7 +217,6 @@
     lax.fori_loop(0, tiles // 4, set_target, 0)
     repeat_target(b_out, b_ref)
     put_source(planes, rows_ref, 0)
-    sums_ref[...] = jnp.zeros_like(sums_ref)
     for copy in copies:
         copy.wait()
 
@@ -225,7 +230,7 @@
                 a = left * (column == i).astype(f32).astype(bf16)
                 a_ref[t] = a
                 s_ref[t] = s
-                add_pair(sums_ref, t, a, s, b_ref[t])
+                add_pair(sums_ref, t, a, s, b_ref[t], first=True, rows=128)
         return carry
 
     lax.fori_loop(0, tiles // 32, own, 0)
@@ -234,8 +239,8 @@
         for i in range(32):
             one = local_pairs[0, step * 32 + i].astype(jnp.int32)
             two = local_pairs[1, step * 32 + i].astype(jnp.int32)
-            add_pair(sums_ref, two, a_ref[one], s_ref[one], b_ref[two])
-            add_pair(sums_ref, one, a_ref[two], s_ref[two], b_ref[one])
+            add_pair(sums_ref, two, a_ref[one], s_ref[one], b_ref[two], rows=128)
+            add_pair(sums_ref, one, a_ref[two], s_ref[two], b_ref[one], rows=128)
         return carry
 
     lax.fori_loop(0, pairs // 32, listed, 0)
@@ -297,7 +302,12 @@
 
     sums_ref[...] = sums_in[...]
 
-    def border(tiles_in, partner, shift):
+    up = 1 - 2 * lax.rem(layer, 2)
+
+    def border(side, carry):
+        shift = jnp.where(side == 0, -up, up)
+        partner = layer + shift
+
         def some(step, carry):
             for group in [8 * step + g for g in range(8)]:
                 left, loads = turn_group(rows_ref, group)
@@ -310,12 +320,12 @@
 
         @pl.when((partner >= 0) & (partner < count))
         def both():
-            put_source([tiles_in[k] for k in range(4)], rows_ref, 0)
+            put_source([jnp.where(side == 0, soon[k], late[k]) for k in range(4)], rows_ref, 0)
             lax.fori_loop(0, groups // 8, some, 0)
 
-    up = 1 - 2 * lax.rem(layer, 2)
-    border(soon, layer - up, -up)
-    border(late, layer + up, up)
+        return carry
+
+    lax.fori_loop(0, 2, border, 0)
 
     for copy in copies:
         copy.wait()

time: 33.5 us -> 33.4 us (level)
  no operation moved by 1% of the time
where the time goes in v17:
time: 33.4 us; the launch traced here: 33.1 us
  Pallas kernels  15.3 us (46%)
  blocking collectives  8.65 us (26%)
  starting transfers between devices  7.29 us (22%)
  between operations  1.34 us (4%)
  other arithmetic  0.54 us (2%)
    all_to_all x1, blocking collectives, per_device(): lax.all_to_all(parts, 'blk', split_axis=0, concat_axis=0, tiled=True)  8.65 us
    pallas_call x1, Pallas kernels, per_device(): pl.pallas_call(functools.partial(rest_kernel, peers), out_shape=(jax.Shap...  8.42 us
    pallas_call x1, Pallas kernels, per_device(): pl.pallas_call(functools.partial(own_kernel, local_pairs.shape[1]), out_s...  5.16 us
    all_to_all x1, starting transfers between devices, per_device(): lax.all_to_all(outbox, 'blk', split_axis=0, concat_axis=0, tiled=True)  3.74 us
    ppermute x2, starting transfers between devices, per_device(): lax.ppermute(payload, 'sub', [p for i in range(first, layers - 1, 2) for...  3.56 us
    pallas_call x1, Pallas kernels, per_device(): pl.pallas_call(functools.partial(pack_kernel, peers), out_shape=(pltpu.VM...  1.69 us
  transfers between devices with their start and end apart: 3, of which 0 were waited for; matrix products, arithmetic and copies ran while one was open for 0% of the time, Pallas kernels for 16%

profile of v17, /device:TPU:8, one launch (start us, length us, event | category | flops | bytes accessed | tf_op | source)
XLA Modules:
  0.0 33.1 jit_solution(10568585500318233260)
XLA Ops:
  1.3 1.7 %pack.1 = (f32[5,32,256]{2,1,0:T(8,128)S(1)}, f32[128,128]{1,0:T(8,128)}) custom-call(f32[3,32,256]{2,1,0:T(8,128)} %coords.1, f32[32,256]{1,0:T(8,128)} %strain.1, s32[32]{0:T(128)} %tile_count_in.1, s32[8]{0:T(128)} %send_tile_in.3, s32[2,8]{1,0:T(2,128)} %remote_pairs_in.3, s32[1]{0:T(128)S(6)} %copy.15.remote_count_in, s32[2,32]{1,0:T(2,128)} %local_pairs_in.1), custom_call_target="tpu_custom_call" | custom-call | tf_op jit(solution)/shard_map/pack/pallas_call | solution.py:415
  3.0 3.5 %collective-permute-start.1 = (f32[5,32,256]{2,1,0:T(8,128)S(1)}, f32[5,32,256]{2,1,0:T(8,128)S(1)}, u32[]{:S(2)}, u32[]{:S(2)}) collective-permute-start(f32[5,32,256]{2,1,0:T(8,128)S(1)} %get-tuple-element.8.payload), channel_id=1, source_target_pairs={{8,16},{16,8},{9,17},{17,9},{10,18},{18,10},{11,19},{19,11},{12,20... | collective-permute-start | bytes 491528 | tf_op jit(solution)/shard_map/ppermute | solution.py:434
  6.5 0.1 collective-permute-start
  6.6 3.7 %all-to-all-start = ((f32[8,16,128]{2,1,0:T(8,128)}), f32[8,16,128]{2,1,0:T(8,128)S(1)}, u32[]{:S(2)}, u32[]{:S(2)}) async-start(f32[8,16,128]{2,1,0:T(8,128)} %bitcast), calls=%async_computation | async-start | bytes 131072 | tf_op jit(solution)/shard_map/all_to_all | solution.py:437
  10.3 5.2 %own.1 = (bf16[32,32,256]{2,1,0:T(8,128)(2,1)S(1)}, f32[2,32,8,256]{3,2,1,0:T(8,128)S(1)}) custom-call(f32[5,32,256]{2,1,0:T(8,128)S(1)} %get-tuple-element.8.payload), custom_call_target="tpu_custom_call" | custom-call | flops 402653184 | bytes 1048576 | tf_op jit(solution)/shard_map/own/pallas_call | solution.py:439
  15.5 0.0 all-to-all-done
  15.5 0.0 collective-permute-done.1.soon
  15.5 0.0 collective-permute-done.late
  15.5 8.4 %rest.1 = (f32[32,256]{1,0:T(8,128)}, f32[8,128]{1,0:T(8,128)S(1)}) custom-call(f32[5,32,256]{2,1,0:T(8,128)S(1)} %collective-permute-done.late, f32[5,32,256]{2,1,0:T(8,128)S(1)} %collective-permute-done.1.soon, f32[128,128]{1,0:T(8,128)S(1)} %bitcast.5, bf16[32,32,256]{2,1,0:T(8,128)(2,1)S(1)} %get-tuple-element.10.b_ref, ...), custom_call_target="tpu_custom_call" | custom-call | flops 536870912 | bytes 2097152 | tf_op jit(solution)/shard_map/rest/pallas_call | solution.py:462
  23.9 8.6 %all_to_all.20 = f32[8,1,128]{2,1,0:T(1,128)S(1)} all-to-all(f32[8,1,128]{2,1,0:T(1,128)S(1)} %bitcast.6), channel_id=1, replica_groups=mesh['sub'=4,'blk'=8] {'blk'}, dimensions={0} | all-to-all | bytes 8192 | tf_op jit(solution)/shard_map/all_to_all | solution.py:505
  32.6 0.5 %reduce_sum.9 = f32[128]{0:T(128)} reduce(f32[8,1,128]{2,1,0:T(1,128)S(1)} %all_to_all.20, f32[]{:T(128)} %constant.0.clone.1), dimensions={0,1}, to_apply=%region_0.0 | reduce | flops 896 | bytes 4612 | tf_op jit(solution)/shard_map/reduce_sum | solution.py:506
Async XLA Ops:
  3.0 12.5 %collective-permute-start.1 = (f32[5,32,256]{2,1,0:T(8,128)S(1)}, f32[5,32,256]{2,1,0:T(8,128)S(1)}, u32[]{:S(2)}, u32[]{:S(2)}) collective-permute-start(f32[5,32,256]{2,1,0:T(8,128)S(1)} %get-tuple-element.8.payload), channel_id=1, source_target_pairs={{8,16},{16,8},{9,17},{17,9},{10,18},{18,10},{11,19},{19,11},{12,20... | collective-permute-start | bytes 491528 | tf_op jit(solution)/shard_map/ppermute | solution.py:434
  6.5 9.0 %collective-permute-start = (f32[5,32,256]{2,1,0:T(8,128)S(1)}, f32[5,32,256]{2,1,0:T(8,128)S(1)}, u32[]{:S(2)}, u32[]{:S(2)}) collective-permute-start(f32[5,32,256]{2,1,0:T(8,128)S(1)} %get-tuple-element.8.payload), channel_id=1, source_target_pairs={{0,8},{8,0},{16,24},{24,16},{1,9},{9,1},{17,25},{25,17},{2,10},{10... | collective-permute-start | bytes 491528 | tf_op jit(solution)/shard_map/ppermute | solution.py:434
  6.6 8.9 %all-to-all-start = ((f32[8,16,128]{2,1,0:T(8,128)}), f32[8,16,128]{2,1,0:T(8,128)S(1)}, u32[]{:S(2)}, u32[]{:S(2)}) async-start(f32[8,16,128]{2,1,0:T(8,128)} %bitcast), calls=%async_computation | async-start | bytes 131072 | tf_op jit(solution)/shard_map/all_to_all | solution.py:437

commit v18 on v17

--- a/solution.py
+++ b/solution.py
@@ -348,6 +348,33 @@
 
     lax.fori_loop(0, peers, place, 0, unroll=peers <= 8)
 
+    owner = spread_rows(tile_sub[...].reshape(1, tiles))
+    subs, corners = corner_map.shape
+    map_rows = spread_rows(jnp.concatenate([corner_map[m : m + 1, :] for m in range(subs)], axis=1))
+    leaving = []
+
+    def finish(lo, hi):
+        valid = (payload[3, lo:hi] > 0.0).astype(f32)
+        num, den = jnp.sum(sums_ref[:, lo:hi], axis=2)
+        strain_bar = num / (den + 1.0 - valid)
+        kappa = jnp.maximum(strain_bar, history[lo:hi])
+        damage = 1.0 - (keep_share + (1.0 - keep_share) * jnp.exp(-softening * (kappa - 1.0))) / kappa
+        damage_ref[lo:hi] = damage
+        leaving.append(
+            pltpu.make_async_copy(damage_ref.at[lo:hi], damage_out.at[lo:hi], sems.at[8 + len(leaving)])
+        )
+        leaving[-1].start()
+        intact = (1.0 - damage) * valid
+        folded = 0.0
+        for half in range(halves):
+            cut = slice(half * 128, (half + 1) * 128)
+            folded = folded + corner_load[:, lo:hi, cut] * intact[None, :, cut]
+        sums = []
+        for m in range(subs):
+            chosen = jnp.where((owner[lo:hi] == float(m))[None], folded, 0.0)
+            sums.append(jnp.sum(chosen.reshape(corners, (hi - lo) // 8, 8, 128), axis=1))
+        return sums
+
     def far(step, carry):
         for group in [4 * step + g for g in range(4)]:
             left, loads = turn_group(far_rows, group)
@@ -356,30 +383,15 @@
                 add_pair(sums_ref, t, left, s, placed(b_ref[t], i), far_live[group * 4 + i].astype(f32))
         return carry
 
-    lax.fori_loop(0, 2 * peers // 16, far, 0)
-
-    valid = (payload[3] > 0.0).astype(f32)
-    num, den = jnp.sum(sums_ref[...], axis=2)
-    strain_bar = num / (den + 1.0 - valid)
-    kappa = jnp.maximum(strain_bar, history[...])
-    damage = 1.0 - (keep_share + (1.0 - keep_share) * jnp.exp(-softening * (kappa - 1.0))) / kappa
-    damage_ref[...] = damage
-    leaving = pltpu.make_async_copy(damage_ref, damage_out, sems.at[8])
-    leaving.start()
-    intact = (1.0 - damage) * valid
-
-    folded = corner_load[:, :, 0:128] * intact[None, :, 0:128]
-    for half in range(1, points // 128):
-        cut = slice(half * 128, (half + 1) * 128)
-        folded = folded + corner_load[:, :, cut] * intact[None, :, cut]
-    owner = spread_rows(tile_sub[...].reshape(1, tiles))
-    subs, corners = corner_map.shape
-    map_rows = spread_rows(jnp.concatenate([corner_map[m : m + 1, :] for m in range(subs)], axis=1))
-    sums = []
-    for m in range(subs):
-        chosen = jnp.where((owner == float(m))[None], folded, 0.0)
-        sums.append(jnp.sum(jnp.sum(chosen, axis=1), axis=1, keepdims=True))
-    sub_part = jnp.broadcast_to(jnp.concatenate(sums, axis=0), (subs * corners, 128))
+    settled = finish(8, tiles)
+    turns = 2 * peers // 16
+    if turns == 1:
+        far(0, 0)
+    else:
+        lax.fori_loop(0, turns, far, 0)
+    sums = [jnp.sum(x + y, axis=1) for x, y in zip(settled, finish(0, 8))]
+    sub_part = jnp.concatenate([jnp.sum(x, axis=1, keepdims=True) for x in sums], axis=0)
+    sub_part = jnp.broadcast_to(sub_part, (subs * corners, 128))
     target = map_rows.astype(jnp.int32) - lax.broadcasted_iota(jnp.int32, (subs * corners, 128), 1)
 
     def scatter(j, carry):
@@ -389,7 +401,8 @@
         return carry
 
     lax.fori_loop(0, peers, scatter, 0, unroll=peers <= 8)
-    leaving.wait()
+    for copy in leaving:
+        copy.wait()
 
 
 def per_device(
@@ -475,7 +488,7 @@
         ]
         + [pltpu.SMEM(v.shape, jnp.int32) for v in (send_tile, remote_pairs, remote_count)]
         + [pltpu.SMEM((2 * peers,), jnp.int32)] * 2
-        + [pltpu.SemaphoreType.DMA((9,))],
+        + [pltpu.SemaphoreType.DMA((10,))],
         compiler_params=params,
         cost_estimate=pl.CostEstimate(
             flops=4 * tiles * block * depth, bytes_accessed=1 << 21, transcendentals=4 * tiles * points * points

time: 33.4 us -> 33.3 us (level)
  no operation moved by 1% of the time
where the time goes in v18:
time: 33.3 us; the launch traced here: 33 us
  Pallas kernels  15.2 us (46%)
  blocking collectives  8.66 us (26%)
  starting transfers between devices  7.29 us (22%)
  between operations  1.34 us (4%)
  other arithmetic  0.54 us (2%)
    all_to_all x1, blocking collectives, per_device(): lax.all_to_all(parts, 'blk', split_axis=0, concat_axis=0, tiled=True)  8.66 us
    pallas_call x1, Pallas kernels, per_device(): pl.pallas_call(functools.partial(rest_kernel, peers), out_shape=(jax.Shap...  8.35 us
    pallas_call x1, Pallas kernels, per_device(): pl.pallas_call(functools.partial(own_kernel, local_pairs.shape[1]), out_s...  5.15 us
    all_to_all x1, starting transfers between devices, per_device(): lax.all_to_all(outbox, 'blk', split_axis=0, concat_axis=0, tiled=True)  3.74 us
    ppermute x2, starting transfers between devices, per_device(): lax.ppermute(payload, 'sub', [p for i in range(first, layers - 1, 2) for...  3.56 us
    pallas_call x1, Pallas kernels, per_device(): pl.pallas_call(functools.partial(pack_kernel, peers), out_shape=(pltpu.VM...  1.69 us
  transfers between devices with their start and end apart: 3, of which 0 were waited for; matrix products, arithmetic and copies ran while one was open for 0% of the time, Pallas kernels for 16%

profile of v18, /device:TPU:8, one launch (start us, length us, event | category | flops | bytes accessed | tf_op | source)
XLA Modules:
  0.0 33.0 jit_solution(12267579926901947321)
XLA Ops:
  1.3 1.7 %pack.1 = (f32[5,32,256]{2,1,0:T(8,128)S(1)}, f32[128,128]{1,0:T(8,128)}) custom-call(f32[3,32,256]{2,1,0:T(8,128)} %coords.1, f32[32,256]{1,0:T(8,128)} %strain.1, s32[32]{0:T(128)} %tile_count_in.1, s32[8]{0:T(128)} %send_tile_in.3, s32[2,8]{1,0:T(2,128)} %remote_pairs_in.3, s32[1]{0:T(128)S(6)} %copy.15.remote_count_in, s32[2,32]{1,0:T(2,128)} %local_pairs_in.1), custom_call_target="tpu_custom_call" | custom-call | tf_op jit(solution)/shard_map/pack/pallas_call | solution.py:428
  3.0 3.5 %collective-permute-start.1 = (f32[5,32,256]{2,1,0:T(8,128)S(1)}, f32[5,32,256]{2,1,0:T(8,128)S(1)}, u32[]{:S(2)}, u32[]{:S(2)}) collective-permute-start(f32[5,32,256]{2,1,0:T(8,128)S(1)} %get-tuple-element.8.payload), channel_id=1, source_target_pairs={{8,16},{16,8},{9,17},{17,9},{10,18},{18,10},{11,19},{19,11},{12,20... | collective-permute-start | bytes 491528 | tf_op jit(solution)/shard_map/ppermute | solution.py:447
  6.5 0.1 collective-permute-start
  6.6 3.7 %all-to-all-start = ((f32[8,16,128]{2,1,0:T(8,128)}), f32[8,16,128]{2,1,0:T(8,128)S(1)}, u32[]{:S(2)}, u32[]{:S(2)}) async-start(f32[8,16,128]{2,1,0:T(8,128)} %bitcast), calls=%async_computation | async-start | bytes 131072 | tf_op jit(solution)/shard_map/all_to_all | solution.py:450
  10.3 5.2 %own.1 = (bf16[32,32,256]{2,1,0:T(8,128)(2,1)S(1)}, f32[2,32,8,256]{3,2,1,0:T(8,128)S(1)}) custom-call(f32[5,32,256]{2,1,0:T(8,128)S(1)} %get-tuple-element.8.payload), custom_call_target="tpu_custom_call" | custom-call | flops 402653184 | bytes 1048576 | tf_op jit(solution)/shard_map/own/pallas_call | solution.py:452
  15.4 0.0 all-to-all-done
  15.5 0.0 collective-permute-done.1.soon
  15.5 0.0 collective-permute-done.late
  15.5 8.3 %rest.1 = (f32[32,256]{1,0:T(8,128)}, f32[8,128]{1,0:T(8,128)S(1)}) custom-call(f32[5,32,256]{2,1,0:T(8,128)S(1)} %collective-permute-done.late, f32[5,32,256]{2,1,0:T(8,128)S(1)} %collective-permute-done.1.soon, f32[128,128]{1,0:T(8,128)S(1)} %bitcast.5, bf16[32,32,256]{2,1,0:T(8,128)(2,1)S(1)} %get-tuple-element.10.b_ref, ...), custom_call_target="tpu_custom_call" | custom-call | flops 536870912 | bytes 2097152 | tf_op jit(solution)/shard_map/rest/pallas_call | solution.py:475
  23.8 8.7 %all_to_all.20 = f32[8,1,128]{2,1,0:T(1,128)S(1)} all-to-all(f32[8,1,128]{2,1,0:T(1,128)S(1)} %bitcast.6), channel_id=1, replica_groups=mesh['sub'=4,'blk'=8] {'blk'}, dimensions={0} | all-to-all | bytes 8192 | tf_op jit(solution)/shard_map/all_to_all | solution.py:518
  32.5 0.5 %reduce_sum.9 = f32[128]{0:T(128)} reduce(f32[8,1,128]{2,1,0:T(1,128)S(1)} %all_to_all.20, f32[]{:T(128)} %constant.0.clone.1), dimensions={0,1}, to_apply=%region_0.0 | reduce | flops 896 | bytes 4612 | tf_op jit(solution)/shard_map/reduce_sum | solution.py:519
Async XLA Ops:
  3.0 12.5 %collective-permute-start.1 = (f32[5,32,256]{2,1,0:T(8,128)S(1)}, f32[5,32,256]{2,1,0:T(8,128)S(1)}, u32[]{:S(2)}, u32[]{:S(2)}) collective-permute-start(f32[5,32,256]{2,1,0:T(8,128)S(1)} %get-tuple-element.8.payload), channel_id=1, source_target_pairs={{8,16},{16,8},{9,17},{17,9},{10,18},{18,10},{11,19},{19,11},{12,20... | collective-permute-start | bytes 491528 | tf_op jit(solution)/shard_map/ppermute | solution.py:447
  6.5 9.0 %collective-permute-start = (f32[5,32,256]{2,1,0:T(8,128)S(1)}, f32[5,32,256]{2,1,0:T(8,128)S(1)}, u32[]{:S(2)}, u32[]{:S(2)}) collective-permute-start(f32[5,32,256]{2,1,0:T(8,128)S(1)} %get-tuple-element.8.payload), channel_id=1, source_target_pairs={{0,8},{8,0},{16,24},{24,16},{1,9},{9,1},{17,25},{25,17},{2,10},{10... | collective-permute-start | bytes 491528 | tf_op jit(solution)/shard_map/ppermute | solution.py:447
  6.6 8.9 %all-to-all-start = ((f32[8,16,128]{2,1,0:T(8,128)}), f32[8,16,128]{2,1,0:T(8,128)S(1)}, u32[]{:S(2)}, u32[]{:S(2)}) async-start(f32[8,16,128]{2,1,0:T(8,128)} %bitcast), calls=%async_computation | async-start | bytes 131072 | tf_op jit(solution)/shard_map/all_to_all | solution.py:450

commit v19 on v18

--- a/solution.py
+++ b/solution.py
@@ -141,6 +141,7 @@
     local_pairs_in,
     payload,
     outbox,
+    listing,
     strain_here,
     tile_count,
     send_tile,
@@ -158,10 +159,10 @@
         (payload.at[0:3], strain_here, tile_count, send_tile, remote_pairs, remote_count, local_pairs),
         sems,
     )
-    payload[4] = jnp.zeros((tiles, points), f32)
+    listing[...] = jnp.zeros((8, 128), f32)
     for copy in copies:
         copy.wait()
-    payload[4, 0:2, 0 : local_pairs.shape[1]] = local_pairs[...].astype(f32)
+    listing[0:2, 0 : local_pairs.shape[1]] = local_pairs[...].astype(f32)
     lane = lax.broadcasted_iota(jnp.int32, (1, points), 1)
     for t in range(tiles):
         payload[3, t : t + 1, :] = jnp.where(lane < tile_count[t], strain_here[t : t + 1, :], 0.0)
@@ -201,9 +202,9 @@
     return jnp.broadcast_to(wide, (128, 128)).T[0:n]
 
 
-def own_kernel(pairs, payload, b_out, sums_ref, rows_ref, a_ref, s_ref, b_ref, local_pairs, sems):
+def own_kernel(pairs, payload, listing, b_out, sums_ref, rows_ref, a_ref, s_ref, b_ref, local_pairs, sems):
     tiles = payload.shape[1]
-    copies = fetch((payload.at[4, 0:8, 0:128],), (local_pairs,), sems)
+    copies = fetch((listing,), (local_pairs,), sems)
     planes = [payload[k] for k in range(4)]
     put_target(planes, rows_ref)
 
@@ -425,14 +426,15 @@
     params = pltpu.CompilerParams(vmem_limit_bytes=grant)
     block = 2 * points * points
 
-    payload, outbox = pl.pallas_call(
+    payload, outbox, listing = pl.pallas_call(
         functools.partial(pack_kernel, peers),
         out_shape=(
-            pltpu.VMEM((5, tiles, points), f32),
+            pltpu.VMEM((4, tiles, points), f32),
             pltpu.VMEM((peers * halves * 8, 128), f32),
+            pltpu.VMEM((8, 128), f32),
         ),
         in_specs=[anywhere] * 7,
-        out_specs=(in_vmem, in_vmem),
+        out_specs=(in_vmem,) * 3,
         scratch_shapes=[pltpu.VMEM((tiles, points), f32)]
         + [pltpu.SMEM(v.shape, jnp.int32) for v in (tile_count, send_tile, remote_pairs, remote_count)]
         + [pltpu.SMEM((peers,), jnp.int32)] * 2
@@ -455,7 +457,7 @@
             jax.ShapeDtypeStruct((tiles, depth, points), bf16),
             jax.ShapeDtypeStruct((2, tiles, 8, points), f32),
         ),
-        in_specs=[in_vmem],
+        in_specs=[in_vmem] * 2,
         out_specs=(in_vmem,) * 2,
         scratch_shapes=[
             pltpu.VMEM((halves, tiles * pitch, 128), f32),
@@ -470,7 +472,7 @@
             flops=3 * tiles * block * depth, bytes_accessed=1 << 20, transcendentals=3 * tiles * points * points
         ),
         name="own",
-    )(payload)
+    )(payload, listing)
 
     damage, parts = pl.pallas_call(
         functools.partial(rest_kernel, peers),

time: 33.3 us -> 33.5 us (level)
  no operation moved by 1% of the time
where the time goes in v19:
time: 33.5 us; the launch traced here: 33.2 us
  Pallas kernels  15.3 us (46%)
  blocking collectives  8.66 us (26%)
  starting transfers between devices  7.29 us (22%)
  between operations  1.34 us (4%)
  other arithmetic  0.54 us (2%)
    all_to_all x1, blocking collectives, per_device(): lax.all_to_all(parts, 'blk', split_axis=0, concat_axis=0, tiled=True)  8.66 us
    pallas_call x1, Pallas kernels, per_device(): pl.pallas_call(functools.partial(rest_kernel, peers), out_shape=(jax.Shap...  8.46 us
    pallas_call x1, Pallas kernels, per_device(): pl.pallas_call(functools.partial(own_kernel, local_pairs.shape[1]), out_s...  5.2 us
    all_to_all x1, starting transfers between devices, per_device(): lax.all_to_all(outbox, 'blk', split_axis=0, concat_axis=0, tiled=True)  3.74 us
    ppermute x2, starting transfers between devices, per_device(): lax.ppermute(payload, 'sub', [p for i in range(first, layers - 1, 2) for...  3.56 us
    pallas_call x1, Pallas kernels, per_device(): pl.pallas_call(functools.partial(pack_kernel, peers), out_shape=(pltpu.VM...  1.69 us
  transfers between devices with their start and end apart: 3, of which 0 were waited for; matrix products, arithmetic and copies ran while one was open for 0% of the time, Pallas kernels for 16%

profile of v19, /device:TPU:8, one launch (start us, length us, event | category | flops | bytes accessed | tf_op | source)
XLA Modules:
  0.0 33.2 jit_solution(1410906318521187574)
XLA Ops:
  1.3 1.7 %pack.1 = (f32[4,32,256]{2,1,0:T(8,128)S(1)}, f32[128,128]{1,0:T(8,128)}, f32[8,128]{1,0:T(8,128)S(1)}) custom-call(f32[3,32,256]{2,1,0:T(8,128)} %coords.1, f32[32,256]{1,0:T(8,128)} %strain.1, s32[32]{0:T(128)} %tile_count_in.1, s32[8]{0:T(128)} %send_tile_in.3, s32[2,8]{1,0:T(2,128)} %remote_pairs_in.3, s32[1]{0:T(128)S(6)} %copy.15.remote_count_in, ...), custom_call_target="tpu_custom_call" | custom-call | tf_op jit(solution)/shard_map/pack/pallas_call | solution.py:429
  3.0 3.5 %collective-permute-start.1 = (f32[4,32,256]{2,1,0:T(8,128)S(1)}, f32[4,32,256]{2,1,0:T(8,128)S(1)}, u32[]{:S(2)}, u32[]{:S(2)}) collective-permute-start(f32[4,32,256]{2,1,0:T(8,128)S(1)} %get-tuple-element.9.payload), channel_id=1, source_target_pairs={{8,16},{16,8},{9,17},{17,9},{10,18},{18,10},{11,19},{19,11},{12,20... | collective-permute-start | bytes 393224 | tf_op jit(solution)/shard_map/ppermute | solution.py:449
  6.5 0.1 collective-permute-start
  6.6 3.7 %all-to-all-start = ((f32[8,16,128]{2,1,0:T(8,128)}), f32[8,16,128]{2,1,0:T(8,128)S(1)}, u32[]{:S(2)}, u32[]{:S(2)}) async-start(f32[8,16,128]{2,1,0:T(8,128)} %bitcast), calls=%async_computation | async-start | bytes 131072 | tf_op jit(solution)/shard_map/all_to_all | solution.py:452
  10.3 5.2 %own.1 = (bf16[32,32,256]{2,1,0:T(8,128)(2,1)S(1)}, f32[2,32,8,256]{3,2,1,0:T(8,128)S(1)}) custom-call(f32[4,32,256]{2,1,0:T(8,128)S(1)} %get-tuple-element.9.payload, f32[8,128]{1,0:T(8,128)S(1)} %get-tuple-element.11.listing), custom_call_target="tpu_custom_call" | custom-call | flops 402653184 | bytes 1048576 | tf_op jit(solution)/shard_map/own/pallas_call | solution.py:454
  15.5 0.0 all-to-all-done
  15.5 0.0 collective-permute-done.1.soon
  15.5 0.0 collective-permute-done.late
  15.5 8.5 %rest.1 = (f32[32,256]{1,0:T(8,128)}, f32[8,128]{1,0:T(8,128)S(1)}) custom-call(f32[4,32,256]{2,1,0:T(8,128)S(1)} %collective-permute-done.late, f32[4,32,256]{2,1,0:T(8,128)S(1)} %collective-permute-done.1.soon, f32[128,128]{1,0:T(8,128)S(1)} %bitcast.5, bf16[32,32,256]{2,1,0:T(8,128)(2,1)S(1)} %get-tuple-element.12.b_ref, ...), custom_call_target="tpu_custom_call" | custom-call | flops 536870912 | bytes 2097152 | tf_op jit(solution)/shard_map/rest/pallas_call | solution.py:477
  24.0 8.7 %all_to_all.20 = f32[8,1,128]{2,1,0:T(1,128)S(1)} all-to-all(f32[8,1,128]{2,1,0:T(1,128)S(1)} %bitcast.6), channel_id=1, replica_groups=mesh['sub'=4,'blk'=8] {'blk'}, dimensions={0} | all-to-all | bytes 8192 | tf_op jit(solution)/shard_map/all_to_all | solution.py:520
  32.6 0.5 %reduce_sum.9 = f32[128]{0:T(128)} reduce(f32[8,1,128]{2,1,0:T(1,128)S(1)} %all_to_all.20, f32[]{:T(128)} %constant.0.clone.1), dimensions={0,1}, to_apply=%region_0.0 | reduce | flops 896 | bytes 4612 | tf_op jit(solution)/shard_map/reduce_sum | solution.py:521
Async XLA Ops:
  3.0 12.5 %collective-permute-start.1 = (f32[4,32,256]{2,1,0:T(8,128)S(1)}, f32[4,32,256]{2,1,0:T(8,128)S(1)}, u32[]{:S(2)}, u32[]{:S(2)}) collective-permute-start(f32[4,32,256]{2,1,0:T(8,128)S(1)} %get-tuple-element.9.payload), channel_id=1, source_target_pairs={{8,16},{16,8},{9,17},{17,9},{10,18},{18,10},{11,19},{19,11},{12,20... | collective-permute-start | bytes 393224 | tf_op jit(solution)/shard_map/ppermute | solution.py:449
  6.5 9.0 %collective-permute-start = (f32[4,32,256]{2,1,0:T(8,128)S(1)}, f32[4,32,256]{2,1,0:T(8,128)S(1)}, u32[]{:S(2)}, u32[]{:S(2)}) collective-permute-start(f32[4,32,256]{2,1,0:T(8,128)S(1)} %get-tuple-element.9.payload), channel_id=1, source_target_pairs={{0,8},{8,0},{16,24},{24,16},{1,9},{9,1},{17,25},{25,17},{2,10},{10... | collective-permute-start | bytes 393224 | tf_op jit(solution)/shard_map/ppermute | solution.py:449
  6.6 8.9 %all-to-all-start = ((f32[8,16,128]{2,1,0:T(8,128)}), f32[8,16,128]{2,1,0:T(8,128)S(1)}, u32[]{:S(2)}, u32[]{:S(2)}) async-start(f32[8,16,128]{2,1,0:T(8,128)} %bitcast), calls=%async_computation | async-start | bytes 131072 | tf_op jit(solution)/shard_map/all_to_all | solution.py:452
